TPU v7x, 32 devices: a whole 2x2x4 slice. The times are simulated.
32 devices in a mesh: batch: 4 (over z), blk: 4 (over y, x), tensor: 2 (over core).
Axes of the slice: x: 2, y: 2, z: 4, core: 2. Of those that a mesh axis runs over, the one named last changes fastest.
Arguments:
- layer_in: bfloat16 [16384, 896], P(('batch', 'blk', 'tensor')), may hold values from -6 to 6
- cotangent: bfloat16 [16384, 896], P(('batch', 'blk', 'tensor')), may hold values from -6 to 6
- lengths: int32 [4, 1], P('batch'), may hold values from 2048 to 4096, as said below
- attn_gain: float32 [896], replicated, may hold values from 0.5 to 1.5
- w_query: bfloat16 [896, 896], P(None, 'tensor'), may hold values from -0.1875 to 0.1875
- query_bias: bfloat16 [896], P('tensor'), may hold values from -3 to 3
- w_key: bfloat16 [896, 128], P(None, 'tensor'), may hold values from -0.1875 to 0.1875
- key_bias: bfloat16 [128], P('tensor'), may hold values from -3 to 3
- w_value: bfloat16 [896, 128], P(None, 'tensor'), may hold values from -0.1875 to 0.1875
- value_bias: bfloat16 [128], P('tensor'), may hold values from -0.59765625 to 0.59765625
- w_out: bfloat16 [896, 896], P('tensor'), may hold values from -1.5 to 1.5
- mlp_gain: float32 [896], replicated, may hold values from 0.5 to 1.5
- w_gate: bfloat16 [896, 4864], P(None, 'tensor'), may hold values from -0.1875 to 0.1875
- w_up: bfloat16 [896, 4864], P(None, 'tensor'), may hold values from -0.1875 to 0.1875
- w_down: bfloat16 [4864, 896], P('tensor'), may hold values from -0.078125 to 0.078125
Outputs:
- layer_out: bfloat16 [16384, 896], P(('batch', 'blk', 'tensor'))
- input_grad: bfloat16 [16384, 896], P(('batch', 'blk', 'tensor'))
- grad_attn_gain: float32 [896], replicated
- grad_query: float32 [896, 896], P(None, 'tensor')
- grad_query_bias: float32 [896], P('tensor')
- grad_key: float32 [896, 128], P(None, 'tensor')
- grad_key_bias: float32 [128], P('tensor')
- grad_value: float32 [896, 128], P(None, 'tensor')
- grad_value_bias: float32 [128], P('tensor')
- grad_out: float32 [896, 896], P('tensor')
- grad_mlp_gain: float32 [896], replicated
- grad_gate: float32 [896, 4864], P(None, 'tensor')
- grad_up: float32 [896, 4864], P(None, 'tensor')
- grad_down: float32 [4864, 896], P('tensor')
Inputs may be any that keep to these rules, and one draw needn't show every extreme that they name: `lengths`: row g gives, for the single bucket of 4096 positions of batch group g, the length of the one sequence that starts at the bucket's first position; the rest of the bucket is padding. In every draw some bucket is full and some holds exactly half of 4096.
All inputs are finite; a program needn't handle non-finite values.
Results may differ from a plain program's by a relative error of at most 0.03.
Values may be sent and summed in bfloat16 or wider, within the bound.
A program may use at most 192 MiB of HBM per device.

v0:
```python
import jax
import jax.numpy as jnp
from jax import lax
from jax.sharding import PartitionSpec as P

HEAD = 64


rope_base = 1000000.0
norm_eps = 1e-06
masked_value = -1e30


def rotary_tables(positions, width):
    freq = rope_base ** (-(jnp.arange(width // 2, dtype=jnp.float32) * 2.0) / width)
    phase = positions.astype(jnp.float32)[:, None] * freq[None, :]
    return (jnp.cos(phase)[:, None, :], jnp.sin(phase)[:, None, :])


def rotate(values, cosine, sine):
    half = values.shape[-1] // 2
    first = values[..., :half]
    second = values[..., half:]
    return jnp.concatenate(
        [first * cosine - second * sine, second * cosine + first * sine], axis=-1
    )


def unrotate(values, cosine, sine):
    half = values.shape[-1] // 2
    first = values[..., :half]
    second = values[..., half:]
    return jnp.concatenate(
        [first * cosine + second * sine, second * cosine - first * sine], axis=-1
    )


def norm_back(grad, normed, scale, gain):
    weighted = grad * gain
    return scale * (weighted - normed * jnp.mean(weighted * normed, axis=1, keepdims=True))


def contract_rows(left, right):
    return lax.dot_general(
        left, right, (((0,), (0,)), ((), ())), preferred_element_type=jnp.float32
    )


def contract_cols(left, right):
    return lax.dot_general(
        left, right, (((1,), (1,)), ((), ())), preferred_element_type=jnp.float32
    )


def bucket_length(positions, lengths_row, bucket):
    buckets = jnp.arange(lengths_row.shape[0], dtype=jnp.int32)
    match = (positions // bucket)[:, None] == buckets[None, :]
    return jnp.sum(jnp.where(match, lengths_row[None, :], 0), axis=1)


def allowed_pairs(query_pos, key_pos, key_len, bucket):
    same = (query_pos // bucket)[:, None] == (key_pos // bucket)[None, :]
    causal = key_pos[None, :] <= query_pos[:, None]
    alive = (key_pos % bucket < key_len)[None, :]
    return same & causal & alive


def shards(
    layer_in,
    cotangent,
    lengths,
    attn_gain,
    w_query,
    query_bias,
    w_key,
    key_bias,
    w_value,
    value_bias,
    w_out,
    mlp_gain,
    w_gate,
    w_up,
    w_down,
):
    rows_own = layer_in.shape[0]
    block_rows = rows_own * lax.axis_size("tensor")
    block_count = lax.axis_size("blk")
    lengths_row = lengths[0]
    bucket = block_rows * block_count // lengths_row.shape[0]
    query_width = w_query.shape[1]
    key_width = w_key.shape[1]
    kv_dev = key_width // HEAD
    group_size = query_width // key_width
    scale = HEAD ** (-0.5)
    block_start = lax.axis_index("blk") * block_rows
    query_pos = block_start + jnp.arange(block_rows, dtype=jnp.int32)
    own_pos = lax.dynamic_slice_in_dim(query_pos, lax.axis_index("tensor") * rows_own, rows_own, 0)
    live_own = own_pos % bucket < bucket_length(own_pos, lengths_row, bucket)
    key_pos_all = jnp.arange(block_rows * block_count, dtype=jnp.int32)
    key_len_all = bucket_length(key_pos_all, lengths_row, bucket)
    cosine, sine = rotary_tables(query_pos % bucket, HEAD)
    own_in = layer_in.astype(jnp.float32)
    scale_first = lax.rsqrt(jnp.mean(own_in * own_in, axis=1, keepdims=True) + norm_eps)
    normed_first = own_in * scale_first
    normed_in = (normed_first * attn_gain).astype(jnp.bfloat16)
    block_in = lax.all_gather(normed_in, "tensor", axis=0, tiled=True)
    weights_qkv = jnp.concatenate([w_query, w_key, w_value], axis=1)
    bias_qkv = jnp.concatenate([query_bias, key_bias, value_bias]).astype(jnp.float32)
    projected = jnp.dot(block_in, weights_qkv, preferred_element_type=jnp.float32) + bias_qkv
    query = projected[:, :query_width].reshape(block_rows, query_width // HEAD, HEAD)
    keys = projected[:, query_width : query_width + key_width].reshape(block_rows, kv_dev, HEAD)
    values_low = projected[:, query_width + key_width :].astype(jnp.bfloat16)
    query_four = (
        rotate(query, cosine, sine)
        .astype(jnp.bfloat16)
        .reshape(block_rows, kv_dev, group_size, HEAD)
    )
    key_low = rotate(keys, cosine, sine).reshape(block_rows, key_width).astype(jnp.bfloat16)
    packed = jnp.concatenate([key_low, values_low], axis=1)
    all_kv = lax.all_gather(packed, "blk", axis=0, tiled=True)

    def block_inputs(index):
        start = index * block_rows
        piece = lax.dynamic_slice_in_dim(all_kv, start, block_rows, 0)
        key_pos = start + jnp.arange(block_rows, dtype=jnp.int32)
        key_len = lax.dynamic_slice_in_dim(key_len_all, start, block_rows, 0)
        allowed = allowed_pairs(query_pos, key_pos, key_len, bucket)
        key_part = piece[:, :key_width].reshape(block_rows, kv_dev, HEAD)
        value_part = piece[:, key_width:].reshape(block_rows, kv_dev, HEAD)
        return (allowed, key_part, value_part)

    def forward_block(carry, index):
        allowed, key_part, value_part = block_inputs(index)

        def forward_compute():
            run_max, run_sum, accum = carry
            scores = (
                jnp.einsum(
                    "qgsd,kgd->gsqk", query_four, key_part, preferred_element_type=jnp.float32
                )
                * scale
            )
            scores = jnp.where(allowed, scores, masked_value)
            new_max = jnp.maximum(run_max, jnp.max(scores, axis=-1))
            weights = jnp.where(allowed, jnp.exp(scores - new_max[..., None]), 0.0)
            decay = jnp.exp(run_max - new_max)
            new_sum = run_sum * decay + jnp.sum(weights, axis=-1)
            new_accum = accum * decay[..., None] + jnp.einsum(
                "gsqk,kgd->gsqd",
                weights.astype(jnp.bfloat16),
                value_part,
                preferred_element_type=jnp.float32,
            )
            return (new_max, new_sum, new_accum)

        return (lax.cond(jnp.any(allowed), forward_compute, lambda: carry), None)

    stats_shape = (kv_dev, group_size, block_rows)
    initial = (
        jnp.full(stats_shape, masked_value, jnp.float32),
        jnp.zeros(stats_shape, jnp.float32),
        jnp.zeros(stats_shape + (HEAD,), jnp.float32),
    )
    blocks = jnp.arange(block_count, dtype=jnp.int32)
    (row_max, row_sum, accum), unused = lax.scan(forward_block, initial, blocks)
    context_four = accum / row_sum[..., None]
    context_low = (
        context_four.transpose(2, 0, 1, 3).reshape(block_rows, query_width).astype(jnp.bfloat16)
    )
    resid = own_in + lax.psum_scatter(
        jnp.dot(context_low, w_out, preferred_element_type=jnp.float32).astype(jnp.bfloat16),
        "tensor",
        scatter_dimension=0,
        tiled=True,
    ).astype(jnp.float32)
    scale_second = lax.rsqrt(jnp.mean(resid * resid, axis=1, keepdims=True) + norm_eps)
    normed_second = resid * scale_second
    mlp_in = (normed_second * mlp_gain).astype(jnp.bfloat16)
    block_mid = lax.all_gather(mlp_in, "tensor", axis=0, tiled=True)
    gate = jnp.dot(block_mid, w_gate, preferred_element_type=jnp.float32)
    upper = jnp.dot(block_mid, w_up, preferred_element_type=jnp.float32)
    activ = gate / (1.0 + jnp.exp(-gate))
    hidden = (activ * upper).astype(jnp.bfloat16)
    layer_out = (
        resid
        + lax.psum_scatter(
            jnp.dot(hidden, w_down, preferred_element_type=jnp.float32).astype(jnp.bfloat16),
            "tensor",
            scatter_dimension=0,
            tiled=True,
        ).astype(jnp.float32)
    ).astype(jnp.bfloat16)
    masked_cot = cotangent * live_own[:, None].astype(jnp.bfloat16)
    cot_block = lax.all_gather(masked_cot, "tensor", axis=0, tiled=True)
    d_hidden = contract_cols(cot_block, w_down)
    sigma = 1.0 / (1.0 + jnp.exp(-gate))
    d_gate = (d_hidden * upper * sigma * (1.0 + gate * (1.0 - sigma))).astype(jnp.bfloat16)
    d_up = (d_hidden * activ).astype(jnp.bfloat16)
    grad_down = contract_rows(hidden, cot_block)
    grad_gate = contract_rows(block_mid, d_gate)
    grad_up = contract_rows(block_mid, d_up)
    d_mid = lax.psum_scatter(
        (contract_cols(d_gate, w_gate) + contract_cols(d_up, w_up)).astype(jnp.bfloat16),
        "tensor",
        scatter_dimension=0,
        tiled=True,
    ).astype(jnp.float32)
    mlp_gain_part = jnp.sum(d_mid * normed_second, axis=0)
    d_resid = masked_cot.astype(jnp.float32) + norm_back(
        d_mid, normed_second, scale_second, mlp_gain
    )
    d_resid_low = d_resid.astype(jnp.bfloat16)
    resid_block = lax.all_gather(d_resid_low, "tensor", axis=0, tiled=True)
    grad_out = contract_rows(context_low, resid_block)
    d_context = contract_cols(resid_block, w_out).astype(jnp.bfloat16)
    d_context_four = d_context.reshape(block_rows, kv_dev, group_size, HEAD).transpose(1, 2, 0, 3)
    delta = jnp.sum(d_context_four.astype(jnp.float32) * context_four, axis=-1)

    def backward_block(d_query, index):
        allowed, key_part, value_part = block_inputs(index)

        def backward_compute():
            scores = (
                jnp.einsum(
                    "qgsd,kgd->gsqk", query_four, key_part, preferred_element_type=jnp.float32
                )
                * scale
            )
            probs = jnp.where(
                allowed, jnp.exp(scores - row_max[..., None]) / row_sum[..., None], 0.0
            )
            probs_low = probs.astype(jnp.bfloat16)
            d_probs = jnp.einsum(
                "gsqd,kgd->gsqk", d_context_four, value_part, preferred_element_type=jnp.float32
            )
            d_scores = (probs * (d_probs - delta[..., None])).astype(jnp.bfloat16)
            new_query = (
                d_query
                + jnp.einsum(
                    "gsqk,kgd->gsqd", d_scores, key_part, preferred_element_type=jnp.float32
                )
                * scale
            )
            d_keys = (
                jnp.einsum(
                    "gsqk,qgsd->kgd", d_scores, query_four, preferred_element_type=jnp.float32
                )
                * scale
            )
            d_values = jnp.einsum(
                "gsqk,gsqd->kgd", probs_low, d_context_four, preferred_element_type=jnp.float32
            )
            joined = jnp.concatenate(
                [d_keys.reshape(block_rows, key_width), d_values.reshape(block_rows, key_width)],
                axis=1,
            )
            return (new_query, joined)

        def skipped():
            return (d_query, jnp.zeros((block_rows, 2 * key_width), jnp.float32))

        return lax.cond(jnp.any(allowed), backward_compute, skipped)

    d_query, kv_terms = lax.scan(
        backward_block, jnp.zeros(stats_shape + (HEAD,), jnp.float32), blocks
    )
    kv_terms = kv_terms.reshape(block_count * block_rows, 2 * key_width)
    d_kv = lax.psum_scatter(
        kv_terms.astype(jnp.bfloat16), "blk", scatter_dimension=0, tiled=True
    ).astype(jnp.float32)
    d_query = d_query.transpose(2, 0, 1, 3).reshape(block_rows, query_width // HEAD, HEAD)
    dq_low = unrotate(d_query, cosine, sine).reshape(block_rows, query_width).astype(jnp.bfloat16)
    dk_low = (
        unrotate(d_kv[:, :key_width].reshape(block_rows, kv_dev, HEAD), cosine, sine)
        .reshape(block_rows, key_width)
        .astype(jnp.bfloat16)
    )
    dv_low = d_kv[:, key_width:].astype(jnp.bfloat16)
    d_proj = jnp.concatenate([dq_low, dk_low, dv_low], axis=1)
    grad_qkv = contract_rows(block_in, d_proj)
    bias_grad = jnp.sum(d_proj.astype(jnp.float32), axis=0)
    d_in = lax.psum_scatter(
        contract_cols(d_proj, weights_qkv).astype(jnp.bfloat16),
        "tensor",
        scatter_dimension=0,
        tiled=True,
    ).astype(jnp.float32)
    attn_gain_part = jnp.sum(d_in * normed_first, axis=0)
    input_grad = (d_resid + norm_back(d_in, normed_first, scale_first, attn_gain)).astype(
        jnp.bfloat16
    )
    gains = lax.psum((attn_gain_part, mlp_gain_part), ("batch", "blk", "tensor"))
    split_two = query_width + key_width
    summed = lax.psum(
        (
            grad_qkv[:, :query_width],
            grad_qkv[:, query_width:split_two],
            grad_qkv[:, split_two:],
            bias_grad[:query_width],
            bias_grad[query_width:split_two],
            bias_grad[split_two:],
            grad_out,
            grad_gate,
            grad_up,
            grad_down,
        ),
        ("batch", "blk"),
    )
    return (
        layer_out,
        input_grad,
        gains[0],
        summed[0],
        summed[3],
        summed[1],
        summed[4],
        summed[2],
        summed[5],
        summed[6],
        gains[1],
        summed[7],
        summed[8],
        summed[9],
    )


def solution(mesh):
    placed = (
        P(("batch", "blk", "tensor"), None),
        P(("batch", "blk", "tensor"), None),
        P("batch", None),
        P(),
        P(None, "tensor"),
        P("tensor"),
        P(None, "tensor"),
        P("tensor"),
        P(None, "tensor"),
        P("tensor"),
        P("tensor", None),
        P(),
        P(None, "tensor"),
        P(None, "tensor"),
        P("tensor", None),
    )
    return jax.shard_map(
        shards,
        mesh=mesh,
        in_specs=placed,
        out_specs=(
            P(("batch", "blk", "tensor"), None),
            P(("batch", "blk", "tensor"), None),
            P(),
            P(None, "tensor"),
            P("tensor"),
            P(None, "tensor"),
            P("tensor"),
            P(None, "tensor"),
            P("tensor"),
            P("tensor", None),
            P(),
            P(None, "tensor"),
            P(None, "tensor"),
            P("tensor", None),
        ),
        check_vma=False,
    )
```

profile of v0, /device:TPU:0, one launch (start us, length us, event | category | flops | bytes accessed | tf_op | source)
XLA Modules:
  0.0 1512.6 jit_solution(730433908866160200)
XLA Ops:
  9.4 2.4 fusion.83
  12.2 12.7 all-gather.6.cloned.1.call-done
  24.9 2.9 convolution_add_fusion
  34.1 24.4 %all-gather.8.cloned.1.call-done = bf16[4096,128]{0,1:T(8,128)(2,1)} async-done(((bf16[1024,128]{0,1:T(8,128)(2,1)}), bf16[4096,128]{0,1:T(8,128)(2,1)}) %all-gather.8.cloned.1.call-update) | async-done | bytes 1048592 | tf_op jit(solution)/shard_map/all_gather | solution.py:120
  60.0 60.9 %while.39 = (s32[]{:T(128)}, f32[1,7,1024]{2,1,0:T(8,128)S(1)}, f32[1,7,1024]{2,1,0:T(8,128)S(1)}, f32[1,7,1024,64]{2,3,1,0:T(8,128)}, s32[4]{0:T(128)S(1)}, /*i...) while((s32[]{:T(128)}, f32[1,7,1024]{2,1,0:T(8,128)S(1)}, ...), condition=%wide.region_7.8_spmd.clone.clone, body=%wide.region_1.7_spmd.clone.clone.sunk | while | flops 1980698624 | bytes 97633616 | solution.py:165
  64.8 41.8 %conditional.8 = ((f32[1,7,1024]{2,1,0:T(8,128)S(1)}, f32[1,7,1024]{2,1,0:T(8,128)S(1)}, f32[1,7,1024,64]{2,3,1,0:T(8,128)})) conditional(s32[]{:T(128)} %convert_element_type.316, (f32[1,7,1024]{2,1,0:T(8,128)S(1)}, f32[1,7,1024]{2,1,0:T(8,128)S(1)}, f32[1,7,1024,64]{2,3,1,0:T(8,128)}) %tuple.132, (pred[1024,1024]{0,1:T(8,128)(4,1)S(1)}, ...), branch_computations={%region_3.3_spmd, %region_4.6_spmd} | conditional | flops 1975407616 | bytes 96535600 | solution.py:156
  64.8 13.0 fusion.12
  77.8 14.9 bitcast_add_fusion
  92.7 13.8 fusion.14
  123.7 2.5 convolution_convert_fusion.2
  126.3 134.8 %reduce-scatter.6.cloned.1.call-done = bf16[512,896]{1,0:T(8,128)(2,1)} async-done(((bf16[1024,896]{1,0:T(8,128)(2,1)}), bf16[512,896]{1,0:T(8,128)(2,1)}) %reduce-scatter.6.cloned.1.call-update) | async-done | bytes 917520 | tf_op jit(solution)/shard_map/reduce_scatter | solution.py:170
  268.8 8.0 all-gather.10.cloned.1.call-done
  276.8 10.6 fusion.125
  287.4 10.4 fusion.126
  297.8 17.7 %multiply_convert_fusion = (bf16[1024,2432]{1,0:T(8,128)(2,1)}, bf16[1024,2432]{1,0:T(8,128)(2,1)}, bf16[1024,2432]{1,0:T(8,128)(2,1)}) fusion(f32[1024,2432]{1,0:T(8,128)} %fusion.125, f32[1024,2432]{1,0:T(8,128)} %fusion.126, bf16[1024,896]{1,0:T(8,128)(2,1)} %all-gather.12.cloned.1.call-done, bf16[2432,896]{1,0:T(8,128)(2,1)} %param.37), kind=kOutput, calls=%fused_computation.102 | convolution fusion | flops 4500094976 | bytes 41058304 | tf_op jit(solution)/shard_map/dot_general | solution.py:50
  315.5 8.8 fusion.127
  324.3 8.9 add_convert_fusion
  333.3 10.7 reduce-scatter.10.cloned.1.call-done
  344.0 2.8 fusion.82
  349.2 11.4 all-gather.14.cloned.1.call-done
  360.6 2.6 convolution_convert_fusion.3
  364.2 82.6 %while.40 = (s32[]{:T(128)}, f32[1,7,1024,64]{2,3,1,0:T(8,128)S(1)}, bf16[4,1024,128]{1,2,0:T(8,128)(2,1)}, s32[4]{0:T(128)S(1)}, s32[4096]{0:T(1024)}, /*index=...) while((s32[]{:T(128)}, ...), condition=%wide.region_18.19_spmd.clone.clone, body=%wide.region_14.18_spmd.clone.clone.sunk | while | flops 4792564736 | bytes 211089840 | solution.py:264
  366.4 2.8 fusion.173
  369.8 57.4 %conditional.9 = (f32[1,7,1024,64]{2,3,1,0:T(8,128)S(1)}, bf16[1,1024,128]{1,2,0:T(8,128)(2,1)S(1)}) conditional(s32[]{:T(128)} %convert_element_type.317, f32[1,7,1024,64]{2,3,1,0:T(8,128)S(1)} %get-tuple-element.963, (pred[1024,1024]{0,1:T(8,128)(4,1)}, bf16[4096,128]{0,1:T(8,128)(2,1)}, s32[]{:T(128)}, bf16[1024,1,7,64]{0,3,2,1:T(8,128)(2,1)S(1)}, ...), branch_computations={%region_16.16_spmd, %region_17.17_spmd} | conditional | flops 4787273728 | bytes 209466992 | solution.py:262
  369.8 12.7 fusion.44
  382.5 14.5 fusion.32
  397.0 5.1 copy-done.2
  402.2 4.6 fusion.40
  406.8 12.1 fusion.37
  418.9 8.3 bitcast_add_fusion.2
  430.0 2.8 fusion.173
  436.2 2.8 fusion.173
  442.4 2.8 fusion.173
  446.8 2.3 copy.43
  449.6 200.6 %reduce-scatter.12.cloned.1.call-done = bf16[1024,128]{0,1:T(8,128)(2,1)} async-done(((bf16[4096,128]{0,1:T(8,128)(2,1)}), bf16[1024,128]{0,1:T(8,128)(2,1)}) %reduce-scatter.12.cloned.1.call-update) | async-done | bytes 262160 | tf_op jit(solution)/shard_map/reduce_scatter | solution.py:268
  651.9 3.0 convolution_convert_fusion
  655.0 9.7 convolution_convert_fusion.1
  664.8 11.2 fusion.129
  676.0 11.1 fusion.130
  687.2 7.7 fusion.131
  702.4 43.3 %all-reduce.1 = (f32[448]{0:T(512)}, f32[64]{0:T(128)}, f32[64]{0:T(128)}) all-reduce(f32[448]{0:T(512)S(1)} %slice.98, f32[64]{0:T(128)S(1)} %get-tuple-element.734, f32[64]{0:T(128)S(1)} %get-tuple-element.733), channel_id=1, replica_groups=mesh['batch'=4,'blk'=4,'tensor'=2] {'batch','blk'}, use_global_device_ids=true, to_apply=%region_26.27 | all-reduce | flops 576 | bytes 4608 | tf_op jit(solution)/shard_map/psum | solution.py:294
  747.8 41.6 %all-reduce = (f32[896]{0:T(1024)}, f32[896]{0:T(1024)}) all-reduce(f32[896]{0:T(1024)S(1)} %get-tuple-element.642, f32[896]{0:T(1024)S(1)} %copy-done.48), channel_id=1, replica_groups=mesh['batch'=4,'blk'=4,'tensor'=2] {'batch','blk','tensor'}, use_global_device_ids=true, to_apply=%region_23.24 | all-reduce | flops 1792 | bytes 14336 | tf_op jit(solution)/shard_map/psum | solution.py:292
  789.5 3.8 fusion.78
  793.2 688.8 %all-reduce.5.cloned.1.call-done = (f32[896,448]{0,1:T(8,128)}, f32[896,64]{0,1:T(8,128)}, f32[896,64]{0,1:T(8,128)}, f32[448,896]{1,0:T(8,128)}, f32[896,2432]{...) async-done(((f32[896,448]{0,1:T(8,128)}, f32[896,64]{0,1:T(8,128)}, f32[896,64]{0,1:T(8,128)}, f32[448,896]{1,0:T(8,128)}, f32[896,2432]{1,0:T(8,128)}, ...) | async-done | bytes 29818896 | tf_op jit(solution)/shard_map/psum | solution.py:294
  1482.0 2.8 copy.86
  1487.4 8.6 copy.90
  1496.0 4.4 copy.91
  1502.1 3.5 copy.92
  (284 shorter events, 61.4 us)
Async XLA Ops:
  7.2 116.5 %copy-start = (bf16[448,896]{1,0:T(8,128)(2,1)S(1)}, bf16[448,896]{1,0:T(8,128)(2,1)}, u32[]{:S(2)}) copy-start(bf16[448,896]{1,0:T(8,128)(2,1)} %param.33) | copy-start | bytes 2408452
  7.2 4.7 copy-start.54
  7.2 4.8 copy-start.29
  7.2 17.6 %all-gather.6.cloned.1.call-start = ((), (), s32[]{:S(2)}) async-start(), calls=%async_computation.5 | async-start | bytes 2752512 | tf_op jit(solution)/shard_map/all_gather | solution.py:106
  11.8 46.7 %all-gather.8.cloned.1.call-start = ((), (), s32[]{:S(2)}) async-start(), calls=%async_computation.6 | async-start | bytes 1310720 | tf_op jit(solution)/shard_map/all_gather | solution.py:120
  11.9 17.3 %copy-start.52 = (f32[32]{0:T(128)}, f32[32]{0:T(128)S(1)}, u32[]{:S(2)}) copy-start(f32[32]{0:T(128)S(1)} %multiply_power_fusion) | copy-start | bytes 388
  12.0 17.3 %copy-start.38 = (f32[1024]{0:T(1024)}, f32[1024]{0:T(1024)S(1)}, u32[]{:S(2)}) copy-start(f32[1024]{0:T(1024)S(1)} %fusion.114) | copy-start | bytes 12292
  12.2 15.6 %copy-start.30 = (bf16[896,576]{0,1:T(8,128)(2,1)}, bf16[896,576]{0,1:T(8,128)(2,1)S(1)}, u32[]{:S(2)}) copy-start(bf16[896,576]{0,1:T(8,128)(2,1)S(1)} %constant_dynamic-update-slice_fusion.1) | copy-start | bytes 3096580
  30.6 230.4 %reduce-scatter.6.cloned.1.call-start = ((), (), s32[]{:S(2)}) async-start(), calls=%async_computation.7 | async-start | bytes 2752512 | tf_op jit(solution)/shard_map/reduce_scatter | solution.py:170
  121.0 5.2 copy-start.14
  121.0 5.2 copy-start.17
  126.2 134.8 %copy-start.3 = (bf16[512,896]{1,0:T(8,128)(2,1)S(1)}, bf16[512,896]{1,0:T(8,128)(2,1)}, u32[]{:S(2)}) copy-start(bf16[512,896]{1,0:T(8,128)(2,1)} %param.23) | copy-start | bytes 2752516
  126.2 150.5 %all-gather.10.cloned.1.call-start = ((), (), s32[]{:S(2)}) async-start(), calls=%async_computation.8 | async-start | bytes 2752512 | tf_op jit(solution)/shard_map/all_gather | solution.py:179
  265.2 32.6 %all-gather.12.cloned.1.call-start = ((), (), s32[]{:S(2)}) async-start(), calls=%async_computation.10 | async-start | bytes 2752512 | tf_op jit(solution)/shard_map/all_gather | solution.py:194
  268.3 75.7 %reduce-scatter.10.cloned.1.call-start = ((), (), s32[]{:S(2)}) async-start(), calls=%async_computation.11 | async-start | bytes 2752512 | tf_op jit(solution)/shard_map/reduce_scatter | solution.py:202
  276.7 10.6 copy-start.58
  315.5 8.9 copy-start.62
  333.3 27.3 %all-gather.14.cloned.1.call-start = ((), (), s32[]{:S(2)}) async-start(), calls=%async_computation.12 | async-start | bytes 2752512 | tf_op jit(solution)/shard_map/all_gather | solution.py:213
  349.1 301.2 %reduce-scatter.12.cloned.1.call-start = ((), (), s32[]{:S(2)}) async-start(), calls=%async_computation.13 | async-start | bytes 1310720 | tf_op jit(solution)/shard_map/reduce_scatter | solution.py:268
  349.2 14.1 copy-start.8
  397.0 5.1 copy-start.2
  449.2 296.5 %reduce-scatter.14.cloned.1.call-start = ((), (), s32[]{:S(2)}) async-start(), calls=%async_computation.14 | async-start | bytes 2752512 | tf_op jit(solution)/shard_map/reduce_scatter | solution.py:282
  449.2 202.0 %copy-start.39 = (f32[1024]{0:T(1024)S(1)}, f32[1024]{0:T(1024)}, u32[]{:S(2)}) copy-start(f32[1024]{0:T(1024)} %copy-done.38) | copy-start | bytes 12292
  449.3 202.0 %copy-start.53 = (f32[32]{0:T(128)S(1)}, f32[32]{0:T(128)}, u32[]{:S(2)}) copy-start(f32[32]{0:T(128)} %copy-done.52) | copy-start | bytes 388
  449.5 202.3 %copy-start.31 = (bf16[896,576]{0,1:T(8,128)(2,1)S(1)}, bf16[896,576]{0,1:T(8,128)(2,1)}, u32[]{:S(2)}) copy-start(bf16[896,576]{0,1:T(8,128)(2,1)} %copy-done.30) | copy-start | bytes 3096580
  449.6 247.5 %copy-start.16 = (bf16[1024,7,64]{0,2,1:T(8,128)(2,1)}, bf16[1024,7,64]{0,2,1:T(8,128)(2,1)S(1)}, u32[]{:S(2)}) copy-start(bf16[1024,7,64]{0,2,1:T(8,128)(2,1)S(1)} %pad_maximum_fusion.2) | copy-start | bytes 2752516
  654.9 134.5 %reduce-scatter.8.cloned.1.call-start = ((), (), s32[]{:S(2)}) async-start(), calls=%async_computation.9 | async-start | bytes 2752512 | tf_op jit(solution)/shard_map/reduce_scatter | solution.py:186
  655.0 9.8 copy-start.59
  664.7 817.3 %all-reduce.5.cloned.1.call-start = ((), (), s32[]{:S(2)}) async-start(), calls=%async_computation.15 | async-start | bytes 59637760 | tf_op jit(solution)/shard_map/psum | solution.py:294
  664.8 22.4 %slice-start.4 = ((s8[4980736]{0:T(1024)(128)(4,1)}), s8[4194304]{0:T(1024)(128)(4,1)S(1)}, s32[]{:S(2)}) async-start(s8[4980736]{0:T(1024)(128)(4,1)} %bitcast.209), calls=%async_computation.20 | async-start | bytes 8388608
  676.0 11.2 copy-start.60
  676.0 11.2 slice-start.5
  687.2 7.7 copy-start.28
  687.2 7.7 copy-start.61
  700.6 45.1 %copy-start.4 = (bf16[512,896]{1,0:T(8,128)(2,1)S(1)}, bf16[512,896]{1,0:T(8,128)(2,1)}, u32[]{:S(2)}) copy-start(bf16[512,896]{1,0:T(8,128)(2,1)} %param.23) | copy-start | bytes 2752516
  700.6 45.1 %copy-start.43 = (f32[896]{0:T(1024)S(1)}, f32[896]{0:T(1024)}, u32[]{:S(2)}) copy-start(f32[896]{0:T(1024)} %param.26) | copy-start | bytes 10756
  700.6 45.1 %copy-start.45 = (f32[512]{0:T(512)S(1)}, f32[512]{0:T(512)}, u32[]{:S(2)}) copy-start(f32[512]{0:T(512)} %copy-done.44) | copy-start | bytes 6148
  700.7 47.1 %copy-start.48 = (f32[896]{0:T(1024)S(1)}, f32[896]{0:T(1024)}, u32[]{:S(2)}) copy-start(f32[896]{0:T(1024)} %get-tuple-element.640) | copy-start | bytes 10756
  700.7 88.7 %copy-start.7 = (bf16[512,896]{1,0:T(8,128)(2,1)S(1)}, bf16[512,896]{1,0:T(8,128)(2,1)}, u32[]{:S(2)}) copy-start(bf16[512,896]{1,0:T(8,128)(2,1)} %reduce-scatter.6.cloned.1.call-done) | copy-start | bytes 2752516
  700.7 88.7 %copy-start.11 = (bf16[512,896]{1,0:T(8,128)(2,1)S(1)}, bf16[512,896]{1,0:T(8,128)(2,1)}, u32[]{:S(2)}) copy-start(bf16[512,896]{1,0:T(8,128)(2,1)} %param.24) | copy-start | bytes 2752516
  700.7 88.7 %copy-start.37 = (f32[896]{0:T(1024)S(1)}, f32[896]{0:T(1024)}, u32[]{:S(2)}) copy-start(f32[896]{0:T(1024)} %param.34) | copy-start | bytes 10756
  700.7 88.7 %copy-start.42 = (f32[512]{0:T(512)S(1)}, f32[512]{0:T(512)}, u32[]{:S(2)}) copy-start(f32[512]{0:T(512)} %copy-done.40) | copy-start | bytes 6148
  700.7 88.7 %copy-start.47 = (f32[512]{0:T(512)S(1)}, f32[512]{0:T(512)}, u32[]{:S(2)}) copy-start(f32[512]{0:T(512)} %copy-done.46) | copy-start | bytes 6148
  700.7 88.7 %copy-start.51 = (bf16[512]{0:T(512)(128)(2,1)S(1)}, bf16[512]{0:T(512)(128)(2,1)}, u32[]{:S(2)}) copy-start(bf16[512]{0:T(512)(128)(2,1)} %copy-done.49) | copy-start | bytes 3076
  1487.4 8.6 copy-start.9
  1487.4 13.0 slice-start
  1487.4 14.6 slice-start.1
  1496.0 6.1 slice-start.2
  (32 other events, 80.6 us)
Sparse Core Ops, SparseCore 0:
  12.0 12.8 all-gather.5
  30.7 27.7 all-gather.7
  126.3 134.6 reduce-scatter.5
  265.4 11.3 all-gather.9
  278.8 11.3 all-gather.11
  333.4 10.5 reduce-scatter.9
  349.3 11.3 all-gather.13
  449.3 200.9 reduce-scatter.11
  655.0 9.3 reduce-scatter.13
  666.5 10.5 reduce-scatter.7
  700.8 781.1 all-reduce.4
where the time goes:
time: 1520 us; the launch traced here: 1510 us
  waiting for transfers between devices  1090 us (72%)
  matrix products  191 us (13%)
  blocking collectives  84.9 us (6%)
  other arithmetic  68.8 us (5%)
  local copies, waits for them, and re-layouts  48.1 us (3%)
  between operations  15.8 us (1%)
    psum x1, waiting for transfers between devices, shards(): lax.psum((grad_qkv[:, :query_width], grad_qkv[:, query_width:split_two],...  689 us
    reduce_scatter x1, waiting for transfers between devices, shards(): lax.psum_scatter(kv_terms.astype(jnp.bfloat16), 'blk', scatter_dimension=...  201 us
    reduce_scatter x1, waiting for transfers between devices, shards(): lax.psum_scatter(jnp.dot(context_low, w_out, preferred_element_type=jnp.f...  135 us
    psum x1, blocking collectives, shards(): lax.psum((grad_qkv[:, :query_width], grad_qkv[:, query_width:split_two],...  43.3 us
    psum x1, blocking collectives, shards(): lax.psum((attn_gain_part, mlp_gain_part), ('batch', 'blk', 'tensor'))  41.6 us
    dot_general x5, matrix products, contract_cols(): lax.dot_general(left, right, (((1,), (1,)), ((), ())), preferred_element_...  41.1 us
    dot_general x5, matrix products, contract_rows(): lax.dot_general(left, right, (((0,), (0,)), ((), ())), preferred_element_...  33.7 us
  transfers between devices with their start and end apart: 11, of which 8 were waited for; matrix products, arithmetic and copies ran while one was open for 5% of the time, Pallas kernels for 0%

commit v1 on v0

v1 whole, which is shorter than its diff:
```python
import functools
import math

import jax
import jax.numpy as jnp
from jax import lax
from jax.experimental import pallas as pl
from jax.experimental.pallas import tpu as pltpu
from jax.sharding import PartitionSpec as P

HEAD = 64
SLOT = 128

rope_base = 1000000.0
norm_eps = 1e-06
masked_value = -1e30
bf16 = jnp.bfloat16
f32 = jnp.float32


def dot(left, right, dims, kind=f32):
    return lax.dot_general(left, right, (dims, ((), ())), preferred_element_type=kind)


NN = ((1,), (0,))
NT = ((1,), (1,))
TN = ((0,), (0,))


def contract_rows(left, right, kind=f32):
    return dot(left, right, TN, kind)


def contract_cols(left, right, kind=f32):
    return dot(left, right, NT, kind)


def norm_back(grad, normed, scale, gain):
    weighted = grad * gain
    return scale * (weighted - normed * jnp.mean(weighted * normed, axis=1, keepdims=True))


def partner(value, axis, bit):
    n = lax.axis_size(axis)
    return lax.ppermute(value, axis, [(i, i ^ (1 << bit)) for i in range(n)])


def bits_of(axis):
    return [(axis, bit) for bit in range(int(math.log2(lax.axis_size(axis))))]


def my_bit(axis, bit):
    return (lax.axis_index(axis) >> bit) & 1


def in_order(own, other, axis, bit):
    first = my_bit(axis, bit) == 0
    return jnp.where(
        first, jnp.concatenate([own, other], 0), jnp.concatenate([other, own], 0)
    )


def gather_pair(own, axis, bit):
    return in_order(own, partner(own, axis, bit), axis, bit)


def scatter_pair(value, axis, bit):
    half = value.shape[0] // 2
    mine = my_bit(axis, bit)
    keep = lax.dynamic_slice_in_dim(value, mine * half, half, 0)
    send = lax.dynamic_slice_in_dim(value, (1 - mine) * half, half, 0)
    got = partner(send, axis, bit)
    return (keep.astype(f32) + got.astype(f32)).astype(bf16)


def add_pair(value, axis, bit):
    got = partner(value, axis, bit)
    return (value.astype(f32) + got.astype(f32)).astype(bf16)


def reduce_all(value, steps):
    halved = []
    for axis, bit in steps:
        if value.shape[0] % 16 == 0:
            value = scatter_pair(value, axis, bit)
            halved.append((axis, bit))
        else:
            value = add_pair(value, axis, bit)
    for axis, bit in reversed(halved):
        value = gather_pair(value, axis, bit)
    return value


def reduce_grad(value):
    half = value.shape[0] // 2
    plane, line = bits_of("blk"), bits_of("batch")
    first = reduce_all(value[:half], plane + line)
    second = reduce_all(value[half:], plane[::-1] + line)
    return jnp.concatenate([first, second], 0).astype(f32)


def attn_fwd_kernel(
    heads, rows, info, q_ref, kv_ref, ctx_ref, slots_ref, lse_ref, k1, v1, q1, m_s, acc_s
):
    tq, tk = 256, 512
    blk, length = info[0], info[1]
    total = kv_ref.shape[0]
    lane = lax.broadcasted_iota(jnp.int32, (tk, SLOT), 1)
    row = lax.broadcasted_iota(jnp.int32, (tk, SLOT), 0)

    def prepare(i, _):
        at = pl.ds(i * tk, tk)
        kv = kv_ref[at, :].astype(f32)
        dead = jnp.where(row + i * tk < length, 0.0, masked_value)
        k1[at, :] = jnp.where(lane < HEAD, kv, jnp.where(lane == HEAD, dead, 0.0)).astype(bf16)
        v1[at, :] = jnp.where(lane < HEAD, 1.0, kv).astype(bf16)
        return 0

    lax.fori_loop(0, (blk + 1) * (rows // tk), prepare, 0)
    one = jnp.where(lax.broadcasted_iota(jnp.int32, (tq, SLOT), 1) == HEAD, 1.0, 0.0)

    def tile(at, masked):
        kt = k1[at, :]
        vt = v1[at, :]
        for h in range(heads):
            s = dot(q1[:, h * SLOT : (h + 1) * SLOT], kt, NT)
            if masked is not None:
                s = jnp.where(masked, s, masked_value)
            m_prev = m_s[h]
            m_new = jnp.maximum(m_prev, jnp.max(s, axis=1, keepdims=True))
            alpha = jnp.exp(m_prev - m_new)
            p = jnp.exp(s - jnp.concatenate([m_new] * (tk // SLOT), 1))
            acc_s[h] = acc_s[h] * alpha + dot(p.astype(bf16), vt, NN)
            m_s[h] = m_new

    def query_tile(qt, _):
        at_q = pl.ds(qt * tq, tq)
        for h in range(heads):
            cols = slice(h * SLOT, (h + 1) * SLOT)
            q1[:, cols] = (q_ref[at_q, cols].astype(f32) + one).astype(bf16)
        m_s[...] = jnp.full(m_s.shape, masked_value, f32)
        acc_s[...] = jnp.zeros(acc_s.shape, f32)
        full = blk * (rows // tk) + (qt * tq) // tk

        def full_tile(i, _):
            tile(pl.ds(pl.multiple_of(i * tk, tk), tk), None)
            return 0

        lax.fori_loop(0, full, full_tile, 0)
        shift = (qt * tq) % tk
        ri = lax.broadcasted_iota(jnp.int32, (tq, tk), 0) + shift
        ci = lax.broadcasted_iota(jnp.int32, (tq, tk), 1)
        tile(pl.ds(pl.multiple_of(full * tk, tk), tk), ci <= ri)
        pos = lax.broadcasted_iota(jnp.int32, (1, tq), 1) + blk * rows + qt * tq
        for h in range(heads):
            acc = acc_s[h]
            out = acc / pltpu.roll(acc, HEAD, 1)
            wide = jnp.where(lax.broadcasted_iota(jnp.int32, (tq, SLOT), 1) < HEAD, 0.0, out)
            slots_ref[at_q, h * SLOT : (h + 1) * SLOT] = wide.astype(bf16)
            ctx_ref[at_q, h * HEAD : (h + 1) * HEAD] = wide[:, HEAD:].astype(bf16)
            lse = jnp.transpose(m_s[h] + jnp.log(acc))[0:1, :]
            lse_ref[h : h + 1, pl.ds(pl.multiple_of(qt * tq, tq), tq)] = jnp.where(
                pos < length, lse, -masked_value
            )
        return 0

    lax.fori_loop(0, rows // tq, query_tile, 0)


def attn_fwd(info, q, kv, heads):
    rows = q.shape[0]
    vm = pl.BlockSpec(memory_space=pltpu.VMEM)
    return pl.pallas_call(
        functools.partial(attn_fwd_kernel, heads, rows),
        out_shape=(
            jax.ShapeDtypeStruct((rows, heads * HEAD), bf16),
            jax.ShapeDtypeStruct((rows, heads * SLOT), bf16),
            jax.ShapeDtypeStruct((8, rows), f32),
        ),
        in_specs=[pl.BlockSpec(memory_space=pltpu.SMEM), vm, vm],
        out_specs=(vm, vm, vm),
        scratch_shapes=[
            pltpu.VMEM(kv.shape, bf16),
            pltpu.VMEM(kv.shape, bf16),
            pltpu.VMEM((256, heads * SLOT), bf16),
            pltpu.VMEM((heads, 256, SLOT), f32),
            pltpu.VMEM((heads, 256, SLOT), f32),
        ],
        compiler_params=pltpu.CompilerParams(vmem_limit_bytes=48 * 2**20),
        name="attn_fwd",
    )(info, q, kv)


def turn(x, cosine, sine_low, sine_high):
    return (
        x * cosine + pltpu.roll(x, SLOT - 32, 1) * sine_low + pltpu.roll(x, 32, 1) * sine_high
    )


def attn_bwd_kernel(
    heads, rows, info, q_ref, kv_ref, do_ref, slots_ref, lse_ref, dq_ref, dkv_ref, k0, delta_s, dq_s
):
    tq, tk = 256, 512
    blk = info[0]
    total = kv_ref.shape[0]
    lane = lax.broadcasted_iota(jnp.int32, (tk, SLOT), 1)

    def prepare(i, _):
        at = pl.ds(i * tk, tk)
        k0[at, :] = jnp.where(lane < HEAD, kv_ref[at, :].astype(f32), 0.0).astype(bf16)
        return 0

    lax.fori_loop(0, (blk + 1) * (rows // tk), prepare, 0)

    def deltas(qt, _):
        at = pl.ds(qt * tq, tq)
        for h in range(heads):
            cols = slice(h * SLOT, (h + 1) * SLOT)
            prod = do_ref[at, cols].astype(f32) * slots_ref[at, cols].astype(f32)
            col = jnp.sum(prod, axis=1, keepdims=True)
            wide = jnp.transpose(jnp.broadcast_to(col, (tq, SLOT)))
            delta_s[h : h + 1, pl.ds(pl.multiple_of(qt * tq, tq), tq)] = wide[0:1, :]
        return 0

    lax.fori_loop(0, rows // tq, deltas, 0)
    dq_s[...] = jnp.zeros(dq_s.shape, f32)

    def pair(kt, vt, kvt, qt, masked):
        at = pl.ds(pl.multiple_of(qt * tq, tq), tq)
        grad = None
        for h in range(heads):
            cols = slice(h * SLOT, (h + 1) * SLOT)
            q = q_ref[at, cols]
            do = do_ref[at, cols]
            s = dot(kt, q, NT)
            p = jnp.exp(s - lse_ref[h : h + 1, at])
            if masked is not None:
                p = jnp.where(masked, p, 0.0)
            dp = dot(kvt, do, NT)
            ds = (p * (dp - delta_s[h : h + 1, at])).astype(bf16)
            part = dot(ds, q, NN) + dot(p.astype(bf16), do, NN)
            grad = part if grad is None else grad + part
            dq_s[at, cols] += dot(ds, kt, TN)
        return grad

    def key_tile(i, _):
        at_k = pl.ds(pl.multiple_of(i * tk, tk), tk)
        kt = k0[at_k, :]
        kvt = kv_ref[at_k, :]
        own = blk * (rows // tk)
        first = jnp.maximum(i - own, 0) * (tk // tq)
        ki = lax.broadcasted_iota(jnp.int32, (tk, tq), 0)
        qi = lax.broadcasted_iota(jnp.int32, (tk, tq), 1)

        @pl.when(i < own)
        def _():
            def step(qt, grad):
                return grad + pair(kt, None, kvt, qt, None)

            grad = lax.fori_loop(0, rows // tq, step, jnp.zeros((tk, SLOT), f32))
            dkv_ref[at_k, :] = grad.astype(bf16)

        @pl.when(i >= own)
        def _():
            grad = jnp.zeros((tk, SLOT), f32)
            for j in range(tk // tq):
                grad = grad + pair(kt, None, kvt, first + j, ki <= qi + j * tq)

            def step(qt, grad):
                return grad + pair(kt, None, kvt, qt, None)

            grad = lax.fori_loop(first + tk // tq, rows // tq, step, grad)
            dkv_ref[at_k, :] = grad.astype(bf16)

        return 0

    lax.fori_loop(0, (blk + 1) * (rows // tk), key_tile, 0)

    def clear(i, _):
        dkv_ref[pl.ds(pl.multiple_of(i * tk, tk), tk), :] = jnp.zeros((tk, SLOT), bf16)
        return 0

    lax.fori_loop((blk + 1) * (rows // tk), total // tk, clear, 0)
    dq_ref[...] = dq_s[...]


def attn_bwd(info, q, kv, d_slots, slots, lse, heads):
    rows = q.shape[0]
    vm = pl.BlockSpec(memory_space=pltpu.VMEM)
    return pl.pallas_call(
        functools.partial(attn_bwd_kernel, heads, rows),
        out_shape=(
            jax.ShapeDtypeStruct((rows, heads * SLOT), f32),
            jax.ShapeDtypeStruct(kv.shape, bf16),
        ),
        in_specs=[pl.BlockSpec(memory_space=pltpu.SMEM), vm, vm, vm, vm, vm],
        out_specs=(vm, vm),
        scratch_shapes=[
            pltpu.VMEM(kv.shape, bf16),
            pltpu.VMEM((8, rows), f32),
            pltpu.VMEM((rows, heads * SLOT), f32),
        ],
        compiler_params=pltpu.CompilerParams(vmem_limit_bytes=48 * 2**20),
        name="attn_bwd",
    )(info, q, kv, d_slots, slots, lse)


def spread(weights, heads, first):
    wide = weights.reshape(heads, HEAD, -1)
    zeros = jnp.zeros_like(wide)
    return jnp.concatenate([wide, zeros] if first else [zeros, wide], 1).reshape(heads * SLOT, -1)


def rotary(positions):
    half = HEAD // 2
    freq = rope_base ** (-(jnp.arange(half, dtype=f32) * 2.0) / HEAD)
    phase = positions.astype(f32)[:, None] * freq[None, :]
    cosine, sine = jnp.cos(phase), jnp.sin(phase)
    return cosine, sine


def shards(
    layer_in,
    cotangent,
    lengths,
    attn_gain,
    w_query,
    query_bias,
    w_key,
    key_bias,
    w_value,
    value_bias,
    w_out,
    mlp_gain,
    w_gate,
    w_up,
    w_down,
):
    rows_own, width = layer_in.shape
    rows = rows_own * lax.axis_size("tensor")
    blocks = lax.axis_size("blk")
    heads = w_query.shape[1] // HEAD
    blk = lax.axis_index("blk")
    core = lax.axis_index("tensor")
    bucket = rows * blocks
    length = lengths[0, 0]
    info = jnp.stack([blk.astype(jnp.int32), length])
    start = blk * rows
    own_start = core * rows_own

    x = gather_pair(layer_in, "tensor", 0).astype(f32)
    cot = gather_pair(cotangent, "tensor", 0)
    positions = start + jnp.arange(rows, dtype=jnp.int32)
    live = positions % bucket < length
    cot = jnp.where(live[:, None], cot, 0)

    cosine, sine = rotary(positions)
    zero32 = jnp.zeros_like(sine)
    fill = jnp.ones((rows, HEAD), f32)
    cos_w = jnp.concatenate([cosine, cosine, fill], 1)
    sin_a = jnp.concatenate([sine, zero32, zero32, zero32], 1)
    sin_b = jnp.concatenate([zero32, sine, zero32, zero32], 1)
    slots_n = heads + 1
    w_all = jnp.concatenate(
        [spread(w_query.T, heads, True), w_key.T, w_value.T], 0
    )
    b_all = jnp.concatenate(
        [
            spread(query_bias[:, None], heads, True)[:, 0],
            key_bias,
            value_bias,
        ]
    ).astype(f32)

    def rotate(v, sign):
        v = v.reshape(rows, slots_n, SLOT)
        up = jnp.roll(v, -32, axis=2)
        down = jnp.roll(v, 32, axis=2)
        out = (
            v * cos_w[:, None, :]
            - sign * up * sin_a[:, None, :]
            + sign * down * sin_b[:, None, :]
        )
        return out.reshape(rows, slots_n * SLOT)

    rho1 = lax.rsqrt(jnp.mean(x * x, axis=1, keepdims=True) + norm_eps)
    n1 = x * rho1
    normed_in = (n1 * attn_gain).astype(bf16)
    proj = rotate(contract_cols(normed_in, w_all) + b_all, 1.0)
    q_low = (proj[:, : heads * SLOT].astype(bf16) * HEAD**-0.5).astype(bf16)
    kv = proj[:, heads * SLOT :].astype(bf16)
    for axis, bit in bits_of("blk"):
        kv = gather_pair(kv, axis, bit)
    ctx, ctx_slots, lse = attn_fwd(info, q_low, kv, heads)

    ctx_other = partner(ctx, "tensor", 0)
    w_out_other = partner(w_out, "tensor", 0)
    resid = x + (
        jnp.dot(ctx, w_out, preferred_element_type=f32)
        + jnp.dot(ctx_other, w_out_other, preferred_element_type=f32)
    )
    rho2 = lax.rsqrt(jnp.mean(resid * resid, axis=1, keepdims=True) + norm_eps)
    n2 = resid * rho2
    mlp_in = (n2 * mlp_gain).astype(bf16)
    gate = jnp.dot(mlp_in, w_gate, preferred_element_type=f32)
    upper = jnp.dot(mlp_in, w_up, preferred_element_type=f32)
    sigma = 1.0 / (1.0 + jnp.exp(-gate))
    activ = gate * sigma
    hidden = (activ * upper).astype(bf16)
    grad_down = reduce_grad(contract_rows(hidden, cot, bf16))
    d_hidden = contract_cols(cot, w_down)
    d_gate = (d_hidden * upper * sigma * (1.0 + gate * (1.0 - sigma))).astype(bf16)
    d_up = (d_hidden * activ).astype(bf16)
    grad_gate = reduce_grad(contract_rows(mlp_in, d_gate, bf16))
    grad_up = reduce_grad(contract_rows(mlp_in, d_up, bf16))
    d_mid_part = (contract_cols(d_gate, w_gate) + contract_cols(d_up, w_up)).astype(bf16)
    d_mid = d_mid_part.astype(f32) + partner(d_mid_part, "tensor", 0).astype(f32)
    ffn_out = jnp.dot(hidden, w_down, preferred_element_type=f32).astype(bf16)
    ffn_out = scatter_pair(ffn_out, "tensor", 0).astype(f32)
    own = lambda v: lax.dynamic_slice_in_dim(v, own_start, rows_own, 0)
    layer_out = (own(resid) + ffn_out).astype(bf16)
    mlp_gain_part = jnp.sum(d_mid * n2, axis=0)
    d_resid = cot.astype(f32) + norm_back(d_mid, n2, rho2, mlp_gain)
    d_resid_low = d_resid.astype(bf16)
    grad_out = contract_rows(ctx, d_resid_low, bf16)
    w_out_slots = spread(w_out, heads, False)
    d_slots = contract_cols(d_resid_low, w_out_slots, f32).astype(bf16)
    dq, dkv = attn_bwd(info, q_low, kv, d_slots, ctx_slots, lse, heads)
    for axis, bit in reversed(bits_of("blk")):
        dkv = scatter_pair(dkv, axis, bit)
    keep = (jnp.arange(SLOT) < HEAD).astype(f32)
    dq = jnp.where(keep > 0, dq.reshape(rows, heads, SLOT), 0.0).reshape(rows, heads * SLOT)
    d_proj = rotate(
        jnp.concatenate([dq * HEAD**-0.5, dkv.astype(f32)], 1), -1.0
    ).astype(bf16)
    grad_all = contract_rows(d_proj, normed_in, bf16)
    bias_all = jnp.sum(d_proj.astype(f32), axis=0)
    d_in = contract_cols(d_proj, w_all.T).astype(bf16)
    d_in = scatter_pair(d_in, "tensor", 0).astype(f32)
    n1_own = own(n1)
    attn_gain_part = jnp.sum(d_in * n1_own, axis=0)
    input_grad = (own(d_resid) + norm_back(d_in, n1_own, own(rho1), attn_gain)).astype(bf16)

    qk = heads * SLOT
    grad_q = grad_all[:qk].reshape(heads, SLOT, width)[:, :HEAD].reshape(heads * HEAD, width)
    bias_q = bias_all[:qk].reshape(heads, SLOT)[:, :HEAD].reshape(heads * HEAD)
    nq = heads * HEAD
    small = jnp.concatenate([grad_out, grad_q, grad_all[qk:]], 0)
    small = jnp.pad(small, ((0, (-small.shape[0]) % 256), (0, 0)))
    small = reduce_grad(small)
    vectors = jnp.concatenate([bias_q, bias_all[qk:], attn_gain_part, mlp_gain_part])
    vectors = lax.psum(vectors, ("batch", "blk"))
    nb = bias_all.shape[0] - qk + nq
    attn_gain_sum = lax.psum(vectors[nb : nb + width], "tensor")
    grad_query = small[nq : 2 * nq].T
    grad_key = small[2 * nq : 2 * nq + HEAD].T
    grad_value = small[2 * nq + HEAD : 2 * nq + 2 * HEAD].T
    return (
        layer_out,
        input_grad,
        attn_gain_sum,
        grad_query,
        vectors[:nq],
        grad_key,
        vectors[nq : nq + HEAD],
        grad_value,
        vectors[nq + HEAD : nq + 2 * HEAD],
        small[:nq],
        vectors[nb + width :],
        grad_gate,
        grad_up,
        grad_down,
    )


def solution(mesh):
    rows = P(("batch", "blk", "tensor"), None)
    cols, part, split = P(None, "tensor"), P("tensor"), P("tensor", None)
    return jax.shard_map(
        shards,
        mesh=mesh,
        in_specs=(
            rows, rows, P("batch", None), P(), cols, part, cols, part, cols, part, split, P(),
            cols, cols, split,
        ),
        out_specs=(
            rows, rows, P(), cols, part, cols, part, cols, part, split, P(), cols, cols, split,
        ),
        check_vma=False,
    )
```

time: 1520 us -> 854 us (0.56)
  waiting for transfers between devices: 1090 us -> 223 us
  starting transfers between devices: 1.14 us -> 237 us
  matrix products: 191 us -> 94.9 us
  Pallas kernels: 0 us -> 43.3 us
  other arithmetic: 68.8 us -> 110 us
    psum x1 -> x0, waiting for transfers between devices: 689 us -> none  [shards(): lax.psum((grad_qkv[:, :query_width], grad_qkv[:, query_width:split_two],...]
    reduce_scatter x5 -> x0, waiting for transfers between devices: 346 us -> none  [the longest x1 201 us: shards(): lax.psum_scatter(kv_terms.astype(jnp.bfloat16), 'blk', scatter_dimension=...]
    ppermute x0 -> x69, starting transfers between devices: none -> 237 us  [partner(): return lax.ppermute(value, axis, [(i, i ^ 1 << bit) for i in range(n)])]
    ppermute x0 -> x69, waiting for transfers between devices: none -> 223 us  [partner(): return lax.ppermute(value, axis, [(i, i ^ 1 << bit) for i in range(n)])]
    dot_general x22 -> x16, matrix products: 191 us -> 94.9 us  [the longest x11 64.4 us: dot(): lax.dot_general(left, right, (dims, ((), ())), preferred_element_type=kind)]
    all_gather x5 -> x0, waiting for transfers between devices: 56.5 us -> none  [the longest x1 24.4 us: shards(): all_kv = lax.all_gather(packed, 'blk', axis=0, tiled=True)]
    pallas_call x0 -> x2, Pallas kernels: none -> 43.3 us  [the longest x1 24.6 us: attn_bwd(): pl.pallas_call(functools.partial(attn_bwd_kernel, heads, rows), out_shape...]
    select_n x17 -> x28, other arithmetic: 0.79 us -> 32.5 us  [in_order(): jnp.where(first, jnp.concatenate([own, other], 0), jnp.concatenate([other...]
  transfers between devices with their start and end apart: 11 -> 69, of which waited for: 8 -> 31; matrix products, arithmetic and copies ran while one was open for 5% -> 21% of each run, Pallas kernels for 0% -> 5%
where the time goes in v1:
time: 854 us; the launch traced here: 838 us
  starting transfers between devices  237 us (28%)
  waiting for transfers between devices  223 us (26%)
  other arithmetic  110 us (13%)
  matrix products  94.9 us (11%)
  blocking collectives  78.5 us (9%)
  local copies, waits for them, and re-layouts  49.3 us (6%)
  Pallas kernels  43.3 us (5%)
    ppermute x69, starting transfers between devices, partner(): return lax.ppermute(value, axis, [(i, i ^ 1 << bit) for i in range(n)])  237 us
    ppermute x69, waiting for transfers between devices, partner(): return lax.ppermute(value, axis, [(i, i ^ 1 << bit) for i in range(n)])  223 us
    psum x1, blocking collectives, shards(): vectors = lax.psum(vectors, ('batch', 'blk'))  75.5 us
    dot_general x11, matrix products, dot(): lax.dot_general(left, right, (dims, ((), ())), preferred_element_type=kind)  64.4 us
    select_n x28, other arithmetic, in_order(): jnp.where(first, jnp.concatenate([own, other], 0), jnp.concatenate([other...  32.5 us
    pallas_call x1, Pallas kernels, attn_bwd(): pl.pallas_call(functools.partial(attn_bwd_kernel, heads, rows), out_shape...  24.6 us
    pallas_call x1, Pallas kernels, attn_fwd(): pl.pallas_call(functools.partial(attn_fwd_kernel, heads, rows), out_shape...  18.7 us
    unnamed x142, local copies, waits for them, and re-layouts  17.9 us
  transfers between devices with their start and end apart: 69, of which 31 were waited for; matrix products, arithmetic and copies ran while one was open for 21% of the time, Pallas kernels for 5%

profile of v1, /device:TPU:0, one launch (start us, length us, event | category | flops | bytes accessed | tf_op | source)
XLA Modules:
  0.0 838.4 jit_solution(13651814703203326544)
XLA Ops:
  24.8 7.4 fusion.2
  38.4 4.4 collective-permute-done.1
  46.5 10.1 %collective-permute-done.2 = bf16[2048,128]{1,0:T(8,128)(2,1)S(1)} collective-permute-done((bf16[2048,128]{1,0:T(8,128)(2,1)S(1)}, bf16[2048,128]{1,0:T(8,128)(2,1)S(1)}, u32[]{:S(2)}, u32[]{:S(2)}) %collective-permute-start.2) | collective-permute-done | bytes 524320 | tf_op jit(solution)/shard_map/ppermute | solution.py:45
  57.0 18.7 %attn_fwd.1 = (bf16[1024,448]{1,0:T(8,128)(2,1)S(1)}, bf16[1024,896]{1,0:T(8,128)(2,1)S(1)}, f32[8,1024]{1,0:T(8,128)S(1)}) custom-call(s32[2]{0:T(128)S(1)} %pad_add_fusion.info, bf16[1024,896]{1,0:T(8,128)(2,1)S(1)} %slice_multiply_fusion.q_ref, bf16[4096,128]{1,0:T(8,128)(2,1)S(1)} %maximum_select_fusion.14.kv_ref), custom_call_target="tpu_custom_call" | custom-call | tf_op jit(solution)/shard_map/attn_fwd/pallas_call | solution.py:173
  83.4 4.7 convert_multiply_fusion
  95.8 8.1 fusion.48
  103.9 8.2 fusion.49
  112.1 17.2 %multiply_convert_fusion = (bf16[1024,2432]{1,0:T(8,128)(2,1)}, bf16[1024,2432]{1,0:T(8,128)(2,1)}, bf16[1024,2432]{1,0:T(8,128)(2,1)}) fusion(f32[1024,2432]{1,0:T(8,128)} %fusion.48, f32[1024,2432]{1,0:T(8,128)} %fusion.49, bf16[2432,896]{1,0:T(8,128)(2,1)} %param.29, bf16[512,896]{0,1:T(8,128)(2,1)} %collective-permute-done.6, bf16[512,896]{0,1:T(8,128)(2,1)} %copy.62, ...), kind=kOutput, calls=%fused_computation | convolution fusion | flops 4509270016 | bytes 41059328 | tf_op jit(solution)/shard_map/dot_general | solution.py:22
  129.3 8.3 fusion.50
  137.7 5.4 fusion.51
  143.1 8.7 %convolution_convert_fusion.2 = bf16[1024,896]{0,1:T(8,128)(2,1)S(1)} fusion(bf16[1024,2432]{1,0:T(8,128)(2,1)} %get-tuple-element.77, bf16[2432,896]{1,0:T(8,128)(2,1)} %param.29), kind=kOutput, calls=%fused_computation.70 | convolution fusion | flops 4463656960 | bytes 11173888 | tf_op jit(solution)/shard_map/dot_general | solution.py:418
  152.4 7.8 fusion.52
  160.3 6.1 add_convert_fusion
  168.0 38.9 %collective-permute-start.34 = (bf16[224,2432]{1,0:T(8,128)(2,1)}, bf16[224,2432]{1,0:T(8,128)(2,1)}, u32[]{:S(2)}, u32[]{:S(2)}) collective-permute-start(bf16[224,2432]{1,0:T(8,128)(2,1)} %constant_dynamic-slice_fusion.14), channel_id=1, source_target_pairs={{0,4},{2,6},{4,0},{6,2},{1,5},{3,7},{5,1},{7,3},{8,12},{10,14},{12... | collective-permute-start | bytes 3268616 | tf_op jit(solution)/shard_map/ppermute | solution.py:45
  208.0 20.2 %collective-permute-start.27 = (bf16[224,2432]{1,0:T(8,128)(2,1)}, bf16[224,2432]{1,0:T(8,128)(2,1)}, u32[]{:S(2)}, u32[]{:S(2)}) collective-permute-start(bf16[224,2432]{1,0:T(8,128)(2,1)} %constant_dynamic-slice_fusion.17), channel_id=1, source_target_pairs={{0,2},{2,0},{4,6},{6,4},{1,3},{3,1},{5,7},{7,5},{8,10},{10,8},{12,... | collective-permute-start | bytes 3268616 | tf_op jit(solution)/shard_map/ppermute | solution.py:45
  231.3 8.5 %fusion.33 = bf16[2432,896]{1,0:T(8,128)(2,1)S(1)} fusion(bf16[1024,2432]{1,0:T(8,128)(2,1)S(1)} %bitcast.119, bf16[512,896]{0,1:T(8,128)(2,1)} %collective-permute-done.6, bf16[512,896]{0,1:T(8,128)(2,1)} %copy.62, pred[1024]{0:T(1024)(128)(4,1)S(1)} %fusion.25, pred[]{:T(512)S(6)} %eq.12), kind=kOutput, calls=%fused_computation.200 | convolution fusion | flops 4471914496 | bytes 11174913 | tf_op jit(solution)/shard_map/dot_general | solution.py:22
  258.1 17.5 %collective-permute-start.35 = (bf16[112,2432]{1,0:T(8,128)(2,1)S(1)}, bf16[112,2432]{1,0:T(8,128)(2,1)S(1)}, u32[]{:S(2)}, u32[]{:S(2)}) collective-permute-start(bf16[112,2432]{1,0:T(8,128)(2,1)S(1)} %constant_dynamic-slice_fusion.13), channel_id=1, source_target_pairs={{0,2},{2,0},{4,6},{6,4},{1,3},{3,1},{5,7},{7,5},{8,10},{10,8},{12,... | collective-permute-start | bytes 1634312 | tf_op jit(solution)/shard_map/ppermute | solution.py:45
  281.3 17.6 %collective-permute-start.49 = (bf16[112,2432]{1,0:T(8,128)(2,1)S(1)}, bf16[112,2432]{1,0:T(8,128)(2,1)S(1)}, u32[]{:S(2)}, u32[]{:S(2)}) collective-permute-start(bf16[112,2432]{1,0:T(8,128)(2,1)S(1)} %constant_dynamic-slice_fusion.7), channel_id=1, source_target_pairs={{0,2},{2,0},{4,6},{6,4},{1,3},{3,1},{5,7},{7,5},{8,10},{10,8},{12,... | collective-permute-start | bytes 1634312 | tf_op jit(solution)/shard_map/ppermute | solution.py:45
  301.5 10.0 %collective-permute-done.35 = bf16[112,2432]{1,0:T(8,128)(2,1)S(1)} collective-permute-done((bf16[112,2432]{1,0:T(8,128)(2,1)S(1)}, bf16[112,2432]{1,0:T(8,128)(2,1)S(1)}, u32[]{:S(2)}, u32[]{:S(2)}) %collective-permute-start.35) | collective-permute-done | bytes 544800 | tf_op jit(solution)/shard_map/ppermute | solution.py:45
  313.7 9.4 %collective-permute-done.49 = bf16[112,2432]{1,0:T(8,128)(2,1)S(1)} collective-permute-done((bf16[112,2432]{1,0:T(8,128)(2,1)S(1)}, bf16[112,2432]{1,0:T(8,128)(2,1)S(1)}, u32[]{:S(2)}, u32[]{:S(2)}) %collective-permute-start.49) | collective-permute-done | bytes 544800 | tf_op jit(solution)/shard_map/ppermute | solution.py:45
  326.4 8.1 collective-permute-done.63
  342.5 5.2 multiply_add_fusion
  350.1 24.6 %attn_bwd.1 = (f32[1024,896]{1,0:T(8,128)}, bf16[4096,128]{1,0:T(8,128)(2,1)S(1)}) custom-call(s32[2]{0:T(128)S(1)} %pad_add_fusion.info, bf16[1024,896]{1,0:T(8,128)(2,1)S(1)} %slice_multiply_fusion.q_ref, bf16[4096,128]{1,0:T(8,128)(2,1)S(1)} %maximum_select_fusion.14.kv_ref, bf16[1024,896]{1,0:T(8,128)(2,1)S(1)} %convolution_convert_fusion.1.do_ref, ...), custom_call_target="tpu_custom_call" | custom-call | tf_op jit(solution)/shard_map/attn_bwd/pallas_call | solution.py:290
  380.3 45.1 %collective-permute-start.8 = (bf16[2048,128]{1,0:T(8,128)(2,1)S(1)}, bf16[2048,128]{1,0:T(8,128)(2,1)S(1)}, u32[]{:S(2)}, u32[]{:S(2)}) collective-permute-start(bf16[2048,128]{1,0:T(8,128)(2,1)S(1)} %constant_dynamic-slice_fusion.26), channel_id=1, source_target_pairs={{0,4},{2,6},{4,0},{6,2},{1,5},{3,7},{5,1},{7,3},{8,12},{10,14},{12... | collective-permute-start | bytes 1572872 | tf_op jit(solution)/shard_map/ppermute | solution.py:45
  432.9 23.2 %collective-permute-done.37 = bf16[56,2432]{1,0:T(8,128)(2,1)S(1)} collective-permute-done((bf16[56,2432]{1,0:T(8,128)(2,1)S(1)}, bf16[56,2432]{1,0:T(8,128)(2,1)S(1)}, u32[]{:S(2)}, u32[]{:S(2)}) %collective-permute-start.37) | collective-permute-done | bytes 272416 | tf_op jit(solution)/shard_map/ppermute | solution.py:45
  456.2 11.6 %collective-permute-done.30 = bf16[56,2432]{1,0:T(8,128)(2,1)S(1)} collective-permute-done((bf16[56,2432]{1,0:T(8,128)(2,1)S(1)}, bf16[56,2432]{1,0:T(8,128)(2,1)S(1)}, u32[]{:S(2)}, u32[]{:S(2)}) %collective-permute-start.30) | collective-permute-done | bytes 272416 | tf_op jit(solution)/shard_map/ppermute | solution.py:45
  467.8 11.6 %collective-permute-done.51 = bf16[56,2432]{1,0:T(8,128)(2,1)S(1)} collective-permute-done((bf16[56,2432]{1,0:T(8,128)(2,1)S(1)}, bf16[56,2432]{1,0:T(8,128)(2,1)S(1)}, u32[]{:S(2)}, u32[]{:S(2)}) %collective-permute-start.51) | collective-permute-done | bytes 272416 | tf_op jit(solution)/shard_map/ppermute | solution.py:45
  480.3 5.1 collective-permute-done.44
  486.1 5.1 collective-permute-done.65
  492.0 5.0 collective-permute-done.58
  502.9 5.7 collective-permute-done.31
  508.6 23.1 %collective-permute-start.9 = (bf16[1024,128]{1,0:T(8,128)(2,1)S(1)}, bf16[1024,128]{1,0:T(8,128)(2,1)S(1)}, u32[]{:S(2)}, u32[]{:S(2)}) collective-permute-start(bf16[1024,128]{1,0:T(8,128)(2,1)S(1)} %constant_dynamic-slice_fusion.25), channel_id=1, source_target_pairs={{0,2},{2,0},{4,6},{6,4},{1,3},{3,1},{5,7},{7,5},{8,10},{10,8},{12,... | collective-permute-start | bytes 786440 | tf_op jit(solution)/shard_map/ppermute | solution.py:45
  532.6 4.9 collective-permute-start.39
  539.5 9.7 %collective-permute-start.53 = (bf16[112,2432]{1,0:T(8,128)(2,1)}, bf16[112,2432]{1,0:T(8,128)(2,1)}, u32[]{:S(2)}, u32[]{:S(2)}) collective-permute-start(bf16[112,2432]{1,0:T(8,128)(2,1)} %maximum_select_fusion.20), channel_id=1, source_target_pairs={{0,2},{2,0},{4,6},{6,4},{1,3},{3,1},{5,7},{7,5},{8,10},{10,8},{12,... | collective-permute-start | bytes 1634312 | tf_op jit(solution)/shard_map/ppermute | solution.py:45
  551.3 4.7 collective-permute-start.67
  597.4 6.6 collective-permute-done.19
  609.9 17.9 %collective-permute-done.20 = bf16[128,896]{1,0:T(8,128)(2,1)S(1)} collective-permute-done((bf16[128,896]{1,0:T(8,128)(2,1)S(1)}, bf16[128,896]{1,0:T(8,128)(2,1)S(1)}, u32[]{:S(2)}, u32[]{:S(2)}) %collective-permute-start.20) | collective-permute-done | bytes 229408 | tf_op jit(solution)/shard_map/ppermute | solution.py:45
  627.8 26.6 %collective-permute-done.12 = bf16[128,896]{1,0:T(8,128)(2,1)S(1)} collective-permute-done((bf16[128,896]{1,0:T(8,128)(2,1)S(1)}, bf16[128,896]{1,0:T(8,128)(2,1)S(1)}, u32[]{:S(2)}, u32[]{:S(2)}) %collective-permute-start.12) | collective-permute-done | bytes 229408 | tf_op jit(solution)/shard_map/ppermute | solution.py:45
  654.6 4.7 collective-permute-done.21
  659.3 4.7 collective-permute-done.13
  666.4 4.4 collective-permute-done.22
  671.4 5.8 collective-permute-done.14
  681.9 75.5 %psum.14 = f32[2368]{0:T(1024)S(1)} all-reduce(f32[2368]{0:T(1024)S(1)} %concatenate.276), channel_id=1, replica_groups=mesh['batch'=4,'blk'=4,'tensor'=2] {'batch','blk'}, use_global_device_ids=true, to_apply=%region_7.8 | all-reduce | flops 2368 | bytes 18944 | tf_op jit(solution)/shard_map/psum | solution.py:452
  790.4 4.1 maximum_convert_fusion
  794.5 9.8 %collective-permute-done.68 = bf16[608,896]{1,0:T(8,128)(2,1)S(1)} collective-permute-done((bf16[608,896]{1,0:T(8,128)(2,1)}, bf16[608,896]{1,0:T(8,128)(2,1)S(1)}, u32[]{:S(2)}, u32[]{:S(2)}) %collective-permute-start.68) | collective-permute-done | bytes 1089568 | tf_op jit(solution)/shard_map/ppermute | solution.py:45
  805.8 4.1 maximum_convert_fusion.1
  809.9 15.3 %collective-permute-done.61 = bf16[608,896]{1,0:T(8,128)(2,1)S(1)} collective-permute-done((bf16[608,896]{1,0:T(8,128)(2,1)}, bf16[608,896]{1,0:T(8,128)(2,1)S(1)}, u32[]{:S(2)}, u32[]{:S(2)}) %collective-permute-start.61) | collective-permute-done | bytes 1089568 | tf_op jit(solution)/shard_map/ppermute | solution.py:45
  826.0 4.1 maximum_convert_fusion.2
  (415 shorter events, 221.8 us)
Async XLA Ops:
  35.9 54.7 %collective-permute-start.4 = (bf16[448,896]{1,0:T(8,128)(2,1)}, bf16[448,896]{1,0:T(8,128)(2,1)}, u32[]{:S(2)}, u32[]{:S(2)}) collective-permute-start(bf16[448,896]{1,0:T(8,128)(2,1)} %param.25), channel_id=1, source_target_pairs={{0,1},{1,0},{2,3},{3,2},{4,5},{5,4},{6,7},{7,6},{8,9},{9,8},{10,11... | collective-permute-start | bytes 2408456 | tf_op jit(solution)/shard_map/ppermute | solution.py:45
  37.4 74.7 %collective-permute-start.6 = (bf16[512,896]{0,1:T(8,128)(2,1)}, bf16[512,896]{0,1:T(8,128)(2,1)}, u32[]{:S(2)}, u32[]{:S(2)}) collective-permute-start(bf16[512,896]{0,1:T(8,128)(2,1)} %copy.62), channel_id=1, source_target_pairs={{0,1},{1,0},{2,3},{3,2},{4,5},{5,4},{6,7},{7,6},{8,9},{9,8},{10,11... | collective-permute-start | bytes 2752520 | tf_op jit(solution)/shard_map/ppermute | solution.py:45
  151.9 92.0 %collective-permute-start.5 = (bf16[512,896]{0,1:T(8,128)(2,1)S(1)}, bf16[512,896]{0,1:T(8,128)(2,1)S(1)}, u32[]{:S(2)}, u32[]{:S(2)}) collective-permute-start(bf16[512,896]{0,1:T(8,128)(2,1)S(1)} %constant_dynamic-slice_fusion.27), channel_id=1, source_target_pairs={{0,1},{1,0},{2,3},{3,2},{4,5},{5,4},{6,7},{7,6},{8,9},{9,8},{10,11... | collective-permute-start | bytes 2752520 | tf_op jit(solution)/shard_map/ppermute | solution.py:45
  166.5 172.1 %collective-permute-start.7 = (bf16[1024,896]{0,1:T(8,128)(2,1)}, bf16[1024,896]{0,1:T(8,128)(2,1)}, u32[]{:S(2)}, u32[]{:S(2)}) collective-permute-start(bf16[1024,896]{0,1:T(8,128)(2,1)} %add_convert_fusion), channel_id=1, source_target_pairs={{0,1},{1,0},{2,3},{3,2},{4,5},{5,4},{6,7},{7,6},{8,9},{9,8},{10,11... | collective-permute-start | bytes 5505032 | tf_op jit(solution)/shard_map/ppermute | solution.py:45
  168.0 80.4 %collective-permute-start.34 = (bf16[224,2432]{1,0:T(8,128)(2,1)}, bf16[224,2432]{1,0:T(8,128)(2,1)}, u32[]{:S(2)}, u32[]{:S(2)}) collective-permute-start(bf16[224,2432]{1,0:T(8,128)(2,1)} %constant_dynamic-slice_fusion.14), channel_id=1, source_target_pairs={{0,4},{2,6},{4,0},{6,2},{1,5},{3,7},{5,1},{7,3},{8,12},{10,14},{12... | collective-permute-start | bytes 3268616 | tf_op jit(solution)/shard_map/ppermute | solution.py:45
  208.0 45.3 %collective-permute-start.27 = (bf16[224,2432]{1,0:T(8,128)(2,1)}, bf16[224,2432]{1,0:T(8,128)(2,1)}, u32[]{:S(2)}, u32[]{:S(2)}) collective-permute-start(bf16[224,2432]{1,0:T(8,128)(2,1)} %constant_dynamic-slice_fusion.17), channel_id=1, source_target_pairs={{0,2},{2,0},{4,6},{6,4},{1,3},{3,1},{5,7},{7,5},{8,10},{10,8},{12,... | collective-permute-start | bytes 3268616 | tf_op jit(solution)/shard_map/ppermute | solution.py:45
  230.9 27.2 %collective-permute-start.48 = (bf16[224,2432]{1,0:T(8,128)(2,1)}, bf16[224,2432]{1,0:T(8,128)(2,1)}, u32[]{:S(2)}, u32[]{:S(2)}) collective-permute-start(bf16[224,2432]{1,0:T(8,128)(2,1)} %constant_dynamic-slice_fusion.8), channel_id=1, source_target_pairs={{0,4},{2,6},{4,0},{6,2},{1,5},{3,7},{5,1},{7,3},{8,12},{10,14},{12... | collective-permute-start | bytes 3268616 | tf_op jit(solution)/shard_map/ppermute | solution.py:45
  243.9 33.2 %collective-permute-start.41 = (bf16[224,2432]{1,0:T(8,128)(2,1)}, bf16[224,2432]{1,0:T(8,128)(2,1)}, u32[]{:S(2)}, u32[]{:S(2)}) collective-permute-start(bf16[224,2432]{1,0:T(8,128)(2,1)} %constant_dynamic-slice_fusion.11), channel_id=1, source_target_pairs={{0,2},{2,0},{4,6},{6,4},{1,3},{3,1},{5,7},{7,5},{8,10},{10,8},{12,... | collective-permute-start | bytes 3268616 | tf_op jit(solution)/shard_map/ppermute | solution.py:45
  248.4 32.8 %collective-permute-start.62 = (bf16[608,896]{1,0:T(8,128)(2,1)}, bf16[608,896]{1,0:T(8,128)(2,1)S(1)}, u32[]{:S(2)}, u32[]{:S(2)}) collective-permute-start(bf16[608,896]{1,0:T(8,128)(2,1)} %constant_dynamic-slice_fusion.2), channel_id=1, source_target_pairs={{0,4},{2,6},{4,0},{6,2},{1,5},{3,7},{5,1},{7,3},{8,12},{10,14},{12... | collective-permute-start | bytes 3268616 | tf_op jit(solution)/shard_map/ppermute | solution.py:45
  253.2 46.6 %collective-permute-start.55 = (bf16[608,896]{1,0:T(8,128)(2,1)S(1)}, bf16[608,896]{1,0:T(8,128)(2,1)S(1)}, u32[]{:S(2)}, u32[]{:S(2)}) collective-permute-start(bf16[608,896]{1,0:T(8,128)(2,1)S(1)} %copy-done.41), channel_id=1, source_target_pairs={{0,2},{2,0},{4,6},{6,4},{1,3},{3,1},{5,7},{7,5},{8,10},{10,8},{12,... | collective-permute-start | bytes 3268616 | tf_op jit(solution)/shard_map/ppermute | solution.py:45
  258.1 53.4 %collective-permute-start.35 = (bf16[112,2432]{1,0:T(8,128)(2,1)S(1)}, bf16[112,2432]{1,0:T(8,128)(2,1)S(1)}, u32[]{:S(2)}, u32[]{:S(2)}) collective-permute-start(bf16[112,2432]{1,0:T(8,128)(2,1)S(1)} %constant_dynamic-slice_fusion.13), channel_id=1, source_target_pairs={{0,2},{2,0},{4,6},{6,4},{1,3},{3,1},{5,7},{7,5},{8,10},{10,8},{12,... | collective-permute-start | bytes 1634312 | tf_op jit(solution)/shard_map/ppermute | solution.py:45
  277.2 46.7 %collective-permute-start.28 = (bf16[112,2432]{1,0:T(8,128)(2,1)S(1)}, bf16[112,2432]{1,0:T(8,128)(2,1)S(1)}, u32[]{:S(2)}, u32[]{:S(2)}) collective-permute-start(bf16[112,2432]{1,0:T(8,128)(2,1)S(1)} %constant_dynamic-slice_fusion.16), channel_id=1, source_target_pairs={{0,4},{2,6},{4,0},{6,2},{1,5},{3,7},{5,1},{7,3},{8,12},{10,14},{12... | collective-permute-start | bytes 1634312 | tf_op jit(solution)/shard_map/ppermute | solution.py:45
  281.3 41.9 %collective-permute-start.49 = (bf16[112,2432]{1,0:T(8,128)(2,1)S(1)}, bf16[112,2432]{1,0:T(8,128)(2,1)S(1)}, u32[]{:S(2)}, u32[]{:S(2)}) collective-permute-start(bf16[112,2432]{1,0:T(8,128)(2,1)S(1)} %constant_dynamic-slice_fusion.7), channel_id=1, source_target_pairs={{0,2},{2,0},{4,6},{6,4},{1,3},{3,1},{5,7},{7,5},{8,10},{10,8},{12,... | collective-permute-start | bytes 1634312 | tf_op jit(solution)/shard_map/ppermute | solution.py:45
  323.8 54.8 %collective-permute-start.36 = (bf16[56,2432]{1,0:T(8,128)(2,1)S(1)}, bf16[56,2432]{1,0:T(8,128)(2,1)S(1)}, u32[]{:S(2)}, u32[]{:S(2)}) collective-permute-start(bf16[56,2432]{1,0:T(8,128)(2,1)S(1)} %constant_dynamic-slice_fusion.12), channel_id=1, source_target_pairs={{0,8},{8,0},{16,24},{24,16},{1,9},{9,1},{17,25},{25,17},{2,10},{10... | collective-permute-start | bytes 817160 | tf_op jit(solution)/shard_map/ppermute | solution.py:45
  325.7 54.6 %collective-permute-start.29 = (bf16[56,2432]{1,0:T(8,128)(2,1)S(1)}, bf16[56,2432]{1,0:T(8,128)(2,1)S(1)}, u32[]{:S(2)}, u32[]{:S(2)}) collective-permute-start(bf16[56,2432]{1,0:T(8,128)(2,1)S(1)} %constant_dynamic-slice_fusion.15), channel_id=1, source_target_pairs={{0,8},{8,0},{16,24},{24,16},{1,9},{9,1},{17,25},{25,17},{2,10},{10... | collective-permute-start | bytes 817160 | tf_op jit(solution)/shard_map/ppermute | solution.py:45
  334.5 91.0 %collective-permute-start.50 = (bf16[56,2432]{1,0:T(8,128)(2,1)S(1)}, bf16[56,2432]{1,0:T(8,128)(2,1)S(1)}, u32[]{:S(2)}, u32[]{:S(2)}) collective-permute-start(bf16[56,2432]{1,0:T(8,128)(2,1)S(1)} %constant_dynamic-slice_fusion.6), channel_id=1, source_target_pairs={{0,8},{8,0},{16,24},{24,16},{1,9},{9,1},{17,25},{25,17},{2,10},{10... | collective-permute-start | bytes 817160 | tf_op jit(solution)/shard_map/ppermute | solution.py:45
  336.8 91.4 %collective-permute-start.43 = (bf16[56,2432]{1,0:T(8,128)(2,1)S(1)}, bf16[56,2432]{1,0:T(8,128)(2,1)S(1)}, u32[]{:S(2)}, u32[]{:S(2)}) collective-permute-start(bf16[56,2432]{1,0:T(8,128)(2,1)S(1)} %constant_dynamic-slice_fusion.9), channel_id=1, source_target_pairs={{0,8},{8,0},{16,24},{24,16},{1,9},{9,1},{17,25},{25,17},{2,10},{10... | collective-permute-start | bytes 817160 | tf_op jit(solution)/shard_map/ppermute | solution.py:45
  338.6 90.1 %collective-permute-start.64 = (bf16[152,896]{1,0:T(8,128)(2,1)S(1)}, bf16[152,896]{1,0:T(8,128)(2,1)}, u32[]{:S(2)}, u32[]{:S(2)}) collective-permute-start(bf16[152,896]{1,0:T(8,128)(2,1)S(1)} %constant_dynamic-slice_fusion), channel_id=1, source_target_pairs={{0,8},{8,0},{16,24},{24,16},{1,9},{9,1},{17,25},{25,17},{2,10},{10... | collective-permute-start | bytes 817160 | tf_op jit(solution)/shard_map/ppermute | solution.py:45
  378.6 53.8 %collective-permute-start.57 = (bf16[152,896]{1,0:T(8,128)(2,1)S(1)}, bf16[152,896]{1,0:T(8,128)(2,1)S(1)}, u32[]{:S(2)}, u32[]{:S(2)}) collective-permute-start(bf16[152,896]{1,0:T(8,128)(2,1)S(1)} %constant_dynamic-slice_fusion.3), channel_id=1, source_target_pairs={{0,8},{8,0},{16,24},{24,16},{1,9},{9,1},{17,25},{25,17},{2,10},{10... | collective-permute-start | bytes 817160 | tf_op jit(solution)/shard_map/ppermute | solution.py:45
  380.3 116.7 %collective-permute-start.8 = (bf16[2048,128]{1,0:T(8,128)(2,1)S(1)}, bf16[2048,128]{1,0:T(8,128)(2,1)S(1)}, u32[]{:S(2)}, u32[]{:S(2)}) collective-permute-start(bf16[2048,128]{1,0:T(8,128)(2,1)S(1)} %constant_dynamic-slice_fusion.26), channel_id=1, source_target_pairs={{0,4},{2,6},{4,0},{6,2},{1,5},{3,7},{5,1},{7,3},{8,12},{10,14},{12... | collective-permute-start | bytes 1572872 | tf_op jit(solution)/shard_map/ppermute | solution.py:45
  425.5 30.6 %collective-permute-start.37 = (bf16[56,2432]{1,0:T(8,128)(2,1)S(1)}, bf16[56,2432]{1,0:T(8,128)(2,1)S(1)}, u32[]{:S(2)}, u32[]{:S(2)}) collective-permute-start(bf16[56,2432]{1,0:T(8,128)(2,1)S(1)} %add_convert_fusion.28), channel_id=1, source_target_pairs={{0,16},{8,24},{16,0},{24,8},{1,17},{9,25},{17,1},{25,9},{2,18},{10... | collective-permute-start | bytes 817160 | tf_op jit(solution)/shard_map/ppermute | solution.py:45
  428.2 39.5 %collective-permute-start.30 = (bf16[56,2432]{1,0:T(8,128)(2,1)S(1)}, bf16[56,2432]{1,0:T(8,128)(2,1)S(1)}, u32[]{:S(2)}, u32[]{:S(2)}) collective-permute-start(bf16[56,2432]{1,0:T(8,128)(2,1)S(1)} %add_convert_fusion.30), channel_id=1, source_target_pairs={{0,16},{8,24},{16,0},{24,8},{1,17},{9,25},{17,1},{25,9},{2,18},{10... | collective-permute-start | bytes 817160 | tf_op jit(solution)/shard_map/ppermute | solution.py:45
  428.7 50.7 %collective-permute-start.51 = (bf16[56,2432]{1,0:T(8,128)(2,1)S(1)}, bf16[56,2432]{1,0:T(8,128)(2,1)S(1)}, u32[]{:S(2)}, u32[]{:S(2)}) collective-permute-start(bf16[56,2432]{1,0:T(8,128)(2,1)S(1)} %add_convert_fusion.24), channel_id=1, source_target_pairs={{0,16},{8,24},{16,0},{24,8},{1,17},{9,25},{17,1},{25,9},{2,18},{10... | collective-permute-start | bytes 817160 | tf_op jit(solution)/shard_map/ppermute | solution.py:45
  432.4 53.0 %collective-permute-start.44 = (bf16[56,2432]{1,0:T(8,128)(2,1)S(1)}, bf16[56,2432]{1,0:T(8,128)(2,1)S(1)}, u32[]{:S(2)}, u32[]{:S(2)}) collective-permute-start(bf16[56,2432]{1,0:T(8,128)(2,1)S(1)} %add_convert_fusion.26), channel_id=1, source_target_pairs={{0,16},{8,24},{16,0},{24,8},{1,17},{9,25},{17,1},{25,9},{2,18},{10... | collective-permute-start | bytes 817160 | tf_op jit(solution)/shard_map/ppermute | solution.py:45
  456.1 35.1 %collective-permute-start.65 = (bf16[152,896]{1,0:T(8,128)(2,1)S(1)}, bf16[152,896]{1,0:T(8,128)(2,1)S(1)}, u32[]{:S(2)}, u32[]{:S(2)}) collective-permute-start(bf16[152,896]{1,0:T(8,128)(2,1)S(1)} %add_convert_fusion.20), channel_id=1, source_target_pairs={{0,16},{8,24},{16,0},{24,8},{1,17},{9,25},{17,1},{25,9},{2,18},{10... | collective-permute-start | bytes 817160 | tf_op jit(solution)/shard_map/ppermute | solution.py:45
  467.8 29.2 %collective-permute-start.58 = (bf16[152,896]{1,0:T(8,128)(2,1)S(1)}, bf16[152,896]{1,0:T(8,128)(2,1)S(1)}, u32[]{:S(2)}, u32[]{:S(2)}) collective-permute-start(bf16[152,896]{1,0:T(8,128)(2,1)S(1)} %add_convert_fusion.22), channel_id=1, source_target_pairs={{0,16},{8,24},{16,0},{24,8},{1,17},{9,25},{17,1},{25,9},{2,18},{10... | collective-permute-start | bytes 817160 | tf_op jit(solution)/shard_map/ppermute | solution.py:45
  491.2 41.4 %collective-permute-start.52 = (bf16[56,2432]{1,0:T(8,128)(2,1)S(1)}, bf16[56,2432]{1,0:T(8,128)(2,1)S(1)}, u32[]{:S(2)}, u32[]{:S(2)}) collective-permute-start(bf16[56,2432]{1,0:T(8,128)(2,1)S(1)} %add_convert_fusion.23), channel_id=1, source_target_pairs={{0,8},{8,0},{16,24},{24,16},{1,9},{9,1},{17,25},{25,17},{2,10},{10... | collective-permute-start | bytes 817160 | tf_op jit(solution)/shard_map/ppermute | solution.py:45
  496.9 41.5 %collective-permute-start.45 = (bf16[56,2432]{1,0:T(8,128)(2,1)S(1)}, bf16[56,2432]{1,0:T(8,128)(2,1)S(1)}, u32[]{:S(2)}, u32[]{:S(2)}) collective-permute-start(bf16[56,2432]{1,0:T(8,128)(2,1)S(1)} %add_convert_fusion.25), channel_id=1, source_target_pairs={{0,8},{8,0},{16,24},{24,16},{1,9},{9,1},{17,25},{25,17},{2,10},{10... | collective-permute-start | bytes 817160 | tf_op jit(solution)/shard_map/ppermute | solution.py:45
  497.0 42.5 %collective-permute-start.66 = (bf16[152,896]{1,0:T(8,128)(2,1)S(1)}, bf16[152,896]{1,0:T(8,128)(2,1)S(1)}, u32[]{:S(2)}, u32[]{:S(2)}) collective-permute-start(bf16[152,896]{1,0:T(8,128)(2,1)S(1)} %add_convert_fusion.19), channel_id=1, source_target_pairs={{0,8},{8,0},{16,24},{24,16},{1,9},{9,1},{17,25},{25,17},{2,10},{10... | collective-permute-start | bytes 817160 | tf_op jit(solution)/shard_map/ppermute | solution.py:45
  502.8 47.4 %collective-permute-start.59 = (bf16[152,896]{1,0:T(8,128)(2,1)S(1)}, bf16[152,896]{1,0:T(8,128)(2,1)S(1)}, u32[]{:S(2)}, u32[]{:S(2)}) collective-permute-start(bf16[152,896]{1,0:T(8,128)(2,1)S(1)} %add_convert_fusion.21), channel_id=1, source_target_pairs={{0,8},{8,0},{16,24},{24,16},{1,9},{9,1},{17,25},{25,17},{2,10},{10... | collective-permute-start | bytes 817160 | tf_op jit(solution)/shard_map/ppermute | solution.py:45
  508.6 42.7 %collective-permute-start.9 = (bf16[1024,128]{1,0:T(8,128)(2,1)S(1)}, bf16[1024,128]{1,0:T(8,128)(2,1)S(1)}, u32[]{:S(2)}, u32[]{:S(2)}) collective-permute-start(bf16[1024,128]{1,0:T(8,128)(2,1)S(1)} %constant_dynamic-slice_fusion.25), channel_id=1, source_target_pairs={{0,2},{2,0},{4,6},{6,4},{1,3},{3,1},{5,7},{7,5},{8,10},{10,8},{12,... | collective-permute-start | bytes 786440 | tf_op jit(solution)/shard_map/ppermute | solution.py:45
  532.6 46.0 %collective-permute-start.39 = (bf16[112,2432]{1,0:T(8,128)(2,1)S(1)}, bf16[112,2432]{1,0:T(8,128)(2,1)}, u32[]{:S(2)}, u32[]{:S(2)}) collective-permute-start(bf16[112,2432]{1,0:T(8,128)(2,1)S(1)} %maximum_select_fusion.18), channel_id=1, source_target_pairs={{0,2},{2,0},{4,6},{6,4},{1,3},{3,1},{5,7},{7,5},{8,10},{10,8},{12,... | collective-permute-start | bytes 1634312 | tf_op jit(solution)/shard_map/ppermute | solution.py:45
  538.5 43.7 %collective-permute-start.32 = (bf16[112,2432]{1,0:T(8,128)(2,1)}, bf16[112,2432]{1,0:T(8,128)(2,1)}, u32[]{:S(2)}, u32[]{:S(2)}) collective-permute-start(bf16[112,2432]{1,0:T(8,128)(2,1)} %maximum_select_fusion.17), channel_id=1, source_target_pairs={{0,4},{2,6},{4,0},{6,2},{1,5},{3,7},{5,1},{7,3},{8,12},{10,14},{12... | collective-permute-start | bytes 1634312 | tf_op jit(solution)/shard_map/ppermute | solution.py:45
  539.5 44.6 %collective-permute-start.53 = (bf16[112,2432]{1,0:T(8,128)(2,1)}, bf16[112,2432]{1,0:T(8,128)(2,1)}, u32[]{:S(2)}, u32[]{:S(2)}) collective-permute-start(bf16[112,2432]{1,0:T(8,128)(2,1)} %maximum_select_fusion.20), channel_id=1, source_target_pairs={{0,2},{2,0},{4,6},{6,4},{1,3},{3,1},{5,7},{7,5},{8,10},{10,8},{12,... | collective-permute-start | bytes 1634312 | tf_op jit(solution)/shard_map/ppermute | solution.py:45
  550.2 36.9 %collective-permute-start.46 = (bf16[112,2432]{1,0:T(8,128)(2,1)}, bf16[112,2432]{1,0:T(8,128)(2,1)}, u32[]{:S(2)}, u32[]{:S(2)}) collective-permute-start(bf16[112,2432]{1,0:T(8,128)(2,1)} %maximum_select_fusion.19), channel_id=1, source_target_pairs={{0,4},{2,6},{4,0},{6,2},{1,5},{3,7},{5,1},{7,3},{8,12},{10,14},{12... | collective-permute-start | bytes 1634312 | tf_op jit(solution)/shard_map/ppermute | solution.py:45
  551.3 37.6 %collective-permute-start.67 = (bf16[304,896]{1,0:T(8,128)(2,1)}, bf16[304,896]{1,0:T(8,128)(2,1)}, u32[]{:S(2)}, u32[]{:S(2)}) collective-permute-start(bf16[304,896]{1,0:T(8,128)(2,1)} %maximum_select_fusion.22), channel_id=1, source_target_pairs={{0,2},{2,0},{4,6},{6,4},{1,3},{3,1},{5,7},{7,5},{8,10},{10,8},{12,... | collective-permute-start | bytes 1634312 | tf_op jit(solution)/shard_map/ppermute | solution.py:45
  578.6 28.4 %collective-permute-start.60 = (bf16[304,896]{1,0:T(8,128)(2,1)}, bf16[304,896]{1,0:T(8,128)(2,1)S(1)}, u32[]{:S(2)}, u32[]{:S(2)}) collective-permute-start(bf16[304,896]{1,0:T(8,128)(2,1)} %maximum_select_fusion.21), channel_id=1, source_target_pairs={{0,4},{2,6},{4,0},{6,2},{1,5},{3,7},{5,1},{7,3},{8,12},{10,14},{12... | collective-permute-start | bytes 1634312 | tf_op jit(solution)/shard_map/ppermute | solution.py:45
  582.2 95.0 %collective-permute-start.10 = (bf16[512,896]{0,1:T(8,128)(2,1)S(1)}, bf16[512,896]{0,1:T(8,128)(2,1)S(1)}, u32[]{:S(2)}, u32[]{:S(2)}) collective-permute-start(bf16[512,896]{0,1:T(8,128)(2,1)S(1)} %copy-done.43), channel_id=1, source_target_pairs={{0,1},{1,0},{2,3},{3,2},{4,5},{5,4},{6,7},{7,6},{8,9},{9,8},{10,11... | collective-permute-start | bytes 2752520 | tf_op jit(solution)/shard_map/ppermute | solution.py:45
  588.9 191.7 %collective-permute-start.40 = (bf16[224,2432]{1,0:T(8,128)(2,1)S(1)}, bf16[224,2432]{1,0:T(8,128)(2,1)}, u32[]{:S(2)}, u32[]{:S(2)}) collective-permute-start(bf16[224,2432]{1,0:T(8,128)(2,1)S(1)} %maximum_select_fusion.9), channel_id=1, source_target_pairs={{0,4},{2,6},{4,0},{6,2},{1,5},{3,7},{5,1},{7,3},{8,12},{10,14},{12... | collective-permute-start | bytes 3268616 | tf_op jit(solution)/shard_map/ppermute | solution.py:45
  597.1 186.9 %collective-permute-start.33 = (bf16[224,2432]{1,0:T(8,128)(2,1)S(1)}, bf16[224,2432]{1,0:T(8,128)(2,1)}, u32[]{:S(2)}, u32[]{:S(2)}) collective-permute-start(bf16[224,2432]{1,0:T(8,128)(2,1)S(1)} %maximum_select_fusion.8), channel_id=1, source_target_pairs={{0,2},{2,0},{4,6},{6,4},{1,3},{3,1},{5,7},{7,5},{8,10},{10,8},{12,... | collective-permute-start | bytes 3268616 | tf_op jit(solution)/shard_map/ppermute | solution.py:45
  604.0 182.4 %collective-permute-start.54 = (bf16[224,2432]{1,0:T(8,128)(2,1)}, bf16[224,2432]{1,0:T(8,128)(2,1)}, u32[]{:S(2)}, u32[]{:S(2)}) collective-permute-start(bf16[224,2432]{1,0:T(8,128)(2,1)} %maximum_select_fusion.11), channel_id=1, source_target_pairs={{0,4},{2,6},{4,0},{6,2},{1,5},{3,7},{5,1},{7,3},{8,12},{10,14},{12... | collective-permute-start | bytes 3268616 | tf_op jit(solution)/shard_map/ppermute | solution.py:45
  677.2 84.6 %collective-permute-start.23 = (bf16[32,896]{1,0:T(8,128)(2,1)S(1)}, bf16[32,896]{1,0:T(8,128)(2,1)S(1)}, u32[]{:S(2)}, u32[]{:S(2)}) collective-permute-start(bf16[32,896]{1,0:T(8,128)(2,1)S(1)} %add_convert_fusion.36), channel_id=1, source_target_pairs={{0,16},{8,24},{16,0},{24,8},{1,17},{9,25},{17,1},{25,9},{2,18},{10... | collective-permute-start | bytes 172040 | tf_op jit(solution)/shard_map/ppermute | solution.py:45
  677.2 84.6 %collective-permute-start.15 = (bf16[32,896]{1,0:T(8,128)(2,1)S(1)}, bf16[32,896]{1,0:T(8,128)(2,1)S(1)}, u32[]{:S(2)}, u32[]{:S(2)}) collective-permute-start(bf16[32,896]{1,0:T(8,128)(2,1)S(1)} %add_convert_fusion.37), channel_id=1, source_target_pairs={{0,16},{8,24},{16,0},{24,8},{1,17},{9,25},{17,1},{25,9},{2,18},{10... | collective-permute-start | bytes 172040 | tf_op jit(solution)/shard_map/ppermute | solution.py:45
  775.0 30.0 %collective-permute-start.47 = (bf16[224,2432]{1,0:T(8,128)(2,1)S(1)}, bf16[224,2432]{1,0:T(8,128)(2,1)S(1)}, u32[]{:S(2)}, u32[]{:S(2)}) collective-permute-start(bf16[224,2432]{1,0:T(8,128)(2,1)S(1)} %maximum_select_fusion.10), channel_id=1, source_target_pairs={{0,2},{2,0},{4,6},{6,4},{1,3},{3,1},{5,7},{7,5},{8,10},{10,8},{12,... | collective-permute-start | bytes 3268616 | tf_op jit(solution)/shard_map/ppermute | solution.py:45
  777.1 27.2 %collective-permute-start.68 = (bf16[608,896]{1,0:T(8,128)(2,1)}, bf16[608,896]{1,0:T(8,128)(2,1)S(1)}, u32[]{:S(2)}, u32[]{:S(2)}) collective-permute-start(bf16[608,896]{1,0:T(8,128)(2,1)} %maximum_select_fusion.13), channel_id=1, source_target_pairs={{0,4},{2,6},{4,0},{6,2},{1,5},{3,7},{5,1},{7,3},{8,12},{10,14},{12... | collective-permute-start | bytes 3268616 | tf_op jit(solution)/shard_map/ppermute | solution.py:45
  780.6 44.6 %collective-permute-start.61 = (bf16[608,896]{1,0:T(8,128)(2,1)}, bf16[608,896]{1,0:T(8,128)(2,1)S(1)}, u32[]{:S(2)}, u32[]{:S(2)}) collective-permute-start(bf16[608,896]{1,0:T(8,128)(2,1)} %maximum_select_fusion.12), channel_id=1, source_target_pairs={{0,2},{2,0},{4,6},{6,4},{1,3},{3,1},{5,7},{7,5},{8,10},{10,8},{12,... | collective-permute-start | bytes 3268616 | tf_op jit(solution)/shard_map/ppermute | solution.py:45
  784.1 46.0 %collective-permute-start.26 = (bf16[256,896]{1,0:T(8,128)(2,1)S(1)}, bf16[256,896]{1,0:T(8,128)(2,1)S(1)}, u32[]{:S(2)}, u32[]{:S(2)}) collective-permute-start(bf16[256,896]{1,0:T(8,128)(2,1)S(1)} %maximum_select_fusion.25), channel_id=1, source_target_pairs={{0,4},{2,6},{4,0},{6,2},{1,5},{3,7},{5,1},{7,3},{8,12},{10,14},{12... | collective-permute-start | bytes 1376264 | tf_op jit(solution)/shard_map/ppermute | solution.py:45
  786.4 47.9 %collective-permute-start.18 = (bf16[256,896]{1,0:T(8,128)(2,1)S(1)}, bf16[256,896]{1,0:T(8,128)(2,1)S(1)}, u32[]{:S(2)}, u32[]{:S(2)}) collective-permute-start(bf16[256,896]{1,0:T(8,128)(2,1)S(1)} %maximum_select_fusion.24), channel_id=1, source_target_pairs={{0,2},{2,0},{4,6},{6,4},{1,3},{3,1},{5,7},{7,5},{8,10},{10,8},{12,... | collective-permute-start | bytes 1376264 | tf_op jit(solution)/shard_map/ppermute | solution.py:45
  (89 other events, 1342.2 us)

commit v2 on v1

--- a/solution.py
+++ b/solution.py
@@ -197,112 +197,640 @@
     )
 
 
-def attn_bwd_kernel(
-    heads, rows, info, q_ref, kv_ref, do_ref, slots_ref, lse_ref, dq_ref, dkv_ref, k0, delta_s, dq_s
+PART = 128
+
+
+def ffn_kernel(
+    x_ref, ctx_ref, ctx_o_ref, wo_ref, wo_o_ref, gain_ref, cot_ref, wg_ref, wu_ref, wd_ref,
+    resid_ref, g_ref, dmid_ref, out_ref, mlp, mlp_t, cot_t, trio, dmid_s, out_s,
 ):
+    step = pl.program_id(0)
+    rows = x_ref.shape[0]
+    tile = 256
+
+    @pl.when(step == 0)
+    def _():
+        def first(r, _):
+            at = pl.ds(pl.multiple_of(r * tile, tile), tile)
+            resid = (
+                x_ref[at, :].astype(f32)
+                + dot(ctx_ref[at, :], wo_ref[...], NN)
+                + dot(ctx_o_ref[at, :], wo_o_ref[...], NN)
+            )
+            resid_ref[at, :] = resid
+            rho = lax.rsqrt(jnp.mean(resid * resid, axis=1, keepdims=True) + norm_eps)
+            normed = resid * rho * gain_ref[...]
+            mlp[at, :] = normed.astype(bf16)
+            mlp_t[:, at] = jnp.transpose(normed).astype(bf16)
+            cot_t[:, at] = jnp.transpose(cot_ref[at, :].astype(f32)).astype(bf16)
+            return 0
+
+        lax.fori_loop(0, rows // tile, first, 0)
+        dmid_s[...] = jnp.zeros(dmid_s.shape, f32)
+        out_s[...] = jnp.zeros(out_s.shape, f32)
+
+    pair = jnp.concatenate([wg_ref[...], wu_ref[...]], 1)
+    down = wd_ref[...]
+    for r in range(rows // tile):
+        at = slice(r * tile, (r + 1) * tile)
+        both = dot(mlp[at, :], pair, NN)
+        gate, upper = both[:, :PART], both[:, PART:]
+        d_hidden = dot(cot_ref[at, :], down, NT)
+        sigma = 1.0 / (1.0 + jnp.exp(-gate))
+        activ = gate * sigma
+        hidden = (activ * upper).astype(bf16)
+        d_gate = (d_hidden * upper * sigma * (1.0 + gate * (1.0 - sigma))).astype(bf16)
+        d_up = (d_hidden * activ).astype(bf16)
+        d_pair = jnp.concatenate([d_gate, d_up], 1)
+        trio[at, :PART] = hidden
+        trio[at, PART:] = d_pair
+        out_s[at, :] += dot(hidden, down, NN)
+        dmid_s[at, :] += dot(d_pair, pair, NT)
+    g_ref[0, :, :PART] = dot(cot_t[...], trio[:, :PART], NN).astype(bf16)
+    g_ref[0, :, PART:] = dot(mlp_t[...], trio[:, PART:], NN).astype(bf16)
+
+    @pl.when(step == pl.num_programs(0) - 1)
+    def _():
+        dmid_ref[...] = dmid_s[...].astype(bf16)
+        out_ref[...] = out_s[...].astype(bf16)
+
+
+def feed_forward(x, ctx, ctx_o, w_out, w_out_o, gain, cot, w_gate, w_up, w_down):
+    rows, width = x.shape
+    hidden = w_gate.shape[1]
+    steps = hidden // PART
+    whole = lambda a: pl.BlockSpec(a.shape, lambda j: (0,) * a.ndim)
+    row_block = pl.BlockSpec((rows, width), lambda j: (0, 0))
+    return pl.pallas_call(
+        ffn_kernel,
+        grid=(steps,),
+        out_shape=(
+            jax.ShapeDtypeStruct((rows, width), f32),
+            jax.ShapeDtypeStruct((steps, width, 3 * PART), bf16),
+            jax.ShapeDtypeStruct((rows, width), bf16),
+            jax.ShapeDtypeStruct((rows, width), bf16),
+        ),
+        in_specs=[
+            whole(x), whole(ctx), whole(ctx_o), whole(w_out), whole(w_out_o), whole(gain),
+            whole(cot),
+            pl.BlockSpec((width, PART), lambda j: (0, j)),
+            pl.BlockSpec((width, PART), lambda j: (0, j)),
+            pl.BlockSpec((PART, width), lambda j: (j, 0)),
+        ],
+        out_specs=(
+            row_block,
+            pl.BlockSpec((1, width, 3 * PART), lambda j: (j, 0, 0)),
+            row_block,
+            row_block,
+        ),
+        scratch_shapes=[
+            pltpu.VMEM((rows, width), bf16),
+            pltpu.VMEM((width, rows), bf16),
+            pltpu.VMEM((width, rows), bf16),
+            pltpu.VMEM((rows, 3 * PART), bf16),
+            pltpu.VMEM((rows, width), f32),
+            pltpu.VMEM((rows, width), f32),
+        ],
+        compiler_params=pltpu.CompilerParams(
+            vmem_limit_bytes=56 * 2**20, dimension_semantics=("arbitrary",)
+        ),
+        name="ffn",
+    )(x, ctx, ctx_o, w_out, w_out_o, gain, cot, w_gate, w_up, w_down)
+
+
+RING = 4
+CHUNK = 3 * PART
+
+
+class Stream:
+    def __init__(self, first, count, axes):
+        self.first, self.count = first, count
+        self.reduce, self.sizes = [], []
+        size = count
+        for axis, bit in axes:
+            half = size % 32 == 0
+            size = size // 2 if half else size
+            self.reduce.append((half, axis, bit))
+            self.sizes.append(size)
+        self.gather = [(axis, bit) for half, axis, bit in reversed(self.reduce) if half]
+        self.stages = len(self.reduce) + len(self.gather) + 1
+
+    def scratch(self):
+        copies = len(self.reduce) + len(self.gather)
+        return [pltpu.VMEM((RING, self.sizes[0], CHUNK), bf16)] + [
+            pltpu.VMEM((RING, size, CHUNK), bf16) for size in self.sizes
+        ] + [
+            pltpu.SemaphoreType.DMA((copies, RING)),
+            pltpu.SemaphoreType.DMA((copies, RING)),
+            pltpu.SemaphoreType.DMA((2, RING)),
+        ]
+
+    def bind(self, refs, sources, out):
+        n = len(self.reduce)
+        self.keep, self.got = refs[0], refs[1 : n + 1]
+        self.send, self.recv, self.local = refs[n + 1 :]
+        self.sources, self.out = sources, out
+        self.peer, self.mine, offset = [], [], self.first
+        self.offsets = []
+        for (half, axis, bit), size in zip(self.reduce, self.sizes):
+            at = lax.axis_index(axis)
+            one = lax.rem(at // (1 << bit), 2)
+            self.peer.append({axis: at + (1 - 2 * one) * (1 << bit)})
+            self.mine.append(one)
+            offset = offset + one * size if half else offset
+            self.offsets.append(offset)
+        self.whole = []
+        offset, size = self.offsets[-1], self.sizes[-1]
+        self.gather_peer = []
+        for k in reversed(range(n)):
+            half = self.reduce[k][0]
+            if half:
+                self.whole.append((offset, size))
+                self.gather_peer.append(self.peer[k])
+                offset, size = offset - self.mine[k] * size, 2 * size
+
+    def copy(self, k, ring, src, dst, peer):
+        return pltpu.make_async_remote_copy(
+            src_ref=src,
+            dst_ref=dst,
+            send_sem=self.send.at[k, ring],
+            recv_sem=self.recv.at[k, ring],
+            device_id=peer,
+            device_id_type=pl.DeviceIdType.MESH,
+        )
+
+    def start_first(self, ring, source):
+        size, one = self.sizes[0], self.mine[0]
+        theirs = pl.multiple_of(self.first + (1 - one) * size, 16)
+        own = pl.multiple_of(self.first + one * size, 16)
+        self.copy(
+            0, ring, source.at[pl.ds(theirs, size), :], self.got[0].at[ring], self.peer[0]
+        ).start()
+        pltpu.make_async_copy(
+            source.at[pl.ds(own, size), :], self.keep.at[ring], self.local.at[0, ring]
+        ).start()
+
+    def reduce_copy(self, k, ring):
+        if k == 0:
+            src = self.keep.at[ring]
+        elif self.reduce[k][0]:
+            size = self.sizes[k]
+            theirs = pl.multiple_of((1 - self.mine[k]) * size, 16)
+            src = self.got[k - 1].at[ring, pl.ds(theirs, size), :]
+        else:
+            src = self.got[k - 1].at[ring]
+        return self.copy(k, ring, src, self.got[k].at[ring], self.peer[k])
+
+    def gather_copy(self, t, ring, chunk):
+        offset, size = self.whole[t]
+        rows = pl.ds(pl.multiple_of(offset, 16), size)
+        place = self.out.at[chunk, rows, :]
+        src = self.got[-1].at[ring] if t == 0 else place
+        return self.copy(len(self.reduce) + t, ring, src, place, self.gather_peer[t])
+
+    def own_copy(self, ring, chunk):
+        offset, size = self.whole[0]
+        rows = pl.ds(pl.multiple_of(offset, 16), size)
+        return pltpu.make_async_copy(
+            self.got[-1].at[ring], self.out.at[chunk, rows, :], self.local.at[1, ring]
+        )
+
+    def stage(self, s, chunk):
+        ring = lax.rem(chunk, RING)
+        n = len(self.reduce)
+        if s == 0:
+            base = 0
+            for count, place in self.sources:
+                @pl.when((chunk >= base) & (chunk < base + count))
+                def _(base=base, place=place):
+                    self.start_first(ring, place(chunk - base))
+
+                base += count
+            return
+        if s <= n:
+            k = s - 1
+            if k == 0:
+                pltpu.make_async_copy(
+                    self.got[0].at[ring], self.keep.at[ring], self.local.at[0, ring]
+                ).wait()
+            self.reduce_copy(k, ring).wait()
+            size = self.sizes[k]
+            if k == 0:
+                own = self.keep[ring]
+            elif self.reduce[k][0]:
+                own = self.got[k - 1][ring, pl.ds(pl.multiple_of(self.mine[k] * size, 16), size), :]
+            else:
+                own = self.got[k - 1][ring]
+            total = own.astype(f32) + self.got[k][ring].astype(f32)
+            self.got[k][ring] = total.astype(bf16)
+            if s < n:
+                self.reduce_copy(s, ring).start()
+            else:
+                self.own_copy(ring, chunk).start()
+                self.gather_copy(0, ring, chunk).start()
+            return
+        t = s - n - 1
+        self.gather_copy(t, ring, chunk).wait()
+        if t == 0:
+            self.own_copy(ring, chunk).wait()
+        if t + 1 < len(self.gather):
+            self.gather_copy(t + 1, ring, chunk).start()
+
+
+def make_streams(width, plane, line):
+    unit = width // 7
+    return [
+        Stream(0, 3 * unit, plane + line),
+        Stream(3 * unit, 3 * unit, plane[::-1] + line),
+        Stream(6 * unit, unit, line + plane),
+    ]
+
+
+def turn(v, cosine, sine_a, sine_b):
+    return v * cosine + pltpu.roll(v, SLOT - 32, 1) * sine_a - pltpu.roll(v, 32, 1) * sine_b
+
+
+LOADS = (
+    "dmid", "resid", "cot", "w_slots", "ctx", "slots", "q", "kv", "lse",
+    "cosine", "sine_a", "sine_b", "normed", "w_all", "own_in", "gain1", "gain2", "part",
+)
+
+
+def backward_kernel(heads, streams, n_ffn, n_small, *refs):
+    nl = len(LOADS)
+    hbm = dict(zip(LOADS, refs[:nl]))
+    grads_ref = refs[nl]
+    sums_ref, layer_out_ref, input_grad_ref = refs[nl + 1 : nl + 4]
+    refs = list(refs[nl + 4 :])
+    m = dict(zip(LOADS, refs[:nl]))
+    refs = refs[nl:]
+    (
+        load_sem, dmid_o, part_o, do, dlow, delta, dq, dkv, dkv_o, k0, dproj, small,
+        din_send, din_own, din_o, rowsum, vec, pair_send, pair_recv, kv_send, kv_recv, out_sem,
+    ) = refs[:22]
+    refs = refs[22:]
+    rows, width = m["cot"].shape
+    half = rows // 2
+    blk, nb = lax.axis_index("blk"), lax.axis_size("blk")
+    core = lax.axis_index("tensor")
+    nz = lax.axis_size("batch")
+    other = {"tensor": 1 - core}
+    tile = 256
+
+    pos = 0
+    for st in streams:
+        cnt = len(st.scratch())
+        st.bind(
+            refs[pos : pos + cnt],
+            [(n_ffn, lambda c: grads_ref.at[c]), (n_small, lambda c: small.at[c])],
+            sums_ref,
+        )
+        pos += cnt
+
+    loads = {
+        name: pltpu.make_async_copy(hbm[name], m[name], load_sem.at[i])
+        for i, name in enumerate(LOADS)
+    }
+    for copy in loads.values():
+        copy.start()
+
+    barrier = pltpu.get_barrier_semaphore()
+    peers = [other]
+    peers += [{"blk": lax.rem(blk + d, nb)} for d in range(1, nb)]
+    batch = lax.axis_index("batch")
+    peers += [
+        {"batch": batch + (1 - 2 * lax.rem(batch // (1 << b), 2)) * (1 << b)}
+        for b in range(int(math.log2(nz)))
+    ]
+    for peer in peers:
+        pl.semaphore_signal(barrier, 1, device_id=peer, device_id_type=pl.DeviceIdType.MESH)
+    pl.semaphore_wait(barrier, len(peers))
+
+    def swap(k, src, dst):
+        return pltpu.make_async_remote_copy(
+            src_ref=src, dst_ref=dst, send_sem=pair_send.at[k], recv_sem=pair_recv.at[k],
+            device_id=other, device_id_type=pl.DeviceIdType.MESH,
+        )
+
+    def dmid_swap():
+        return swap(0, hbm["dmid"], dmid_o)
+
+    theirs = pl.multiple_of((1 - core) * half, 16)
+    ours = pl.multiple_of(core * half, 16)
+
+    def part_swap():
+        return swap(1, hbm["part"].at[pl.ds(theirs, half), :], part_o)
+
+    def din_swap():
+        return swap(2, din_send, din_o)
+
+    dmid_swap().start()
+    part_swap().start()
+
+    def put(first, at, value):
+        done, n = 0, value.shape[1]
+        while done < n:
+            c, lane = divmod(first + done, CHUNK)
+            take = min(n - done, CHUNK - lane)
+            small[c, at, lane : lane + take] = value[:, done : done + take].astype(bf16)
+            done += take
+
+    nq = heads * HEAD
     tq, tk = 256, 512
-    blk = info[0]
-    total = kv_ref.shape[0]
-    lane = lax.broadcasted_iota(jnp.int32, (tk, SLOT), 1)
-
-    def prepare(i, _):
-        at = pl.ds(i * tk, tk)
-        k0[at, :] = jnp.where(lane < HEAD, kv_ref[at, :].astype(f32), 0.0).astype(bf16)
-        return 0
-
-    lax.fori_loop(0, (blk + 1) * (rows // tk), prepare, 0)
-
-    def deltas(qt, _):
-        at = pl.ds(qt * tq, tq)
-        for h in range(heads):
-            cols = slice(h * SLOT, (h + 1) * SLOT)
-            prod = do_ref[at, cols].astype(f32) * slots_ref[at, cols].astype(f32)
-            col = jnp.sum(prod, axis=1, keepdims=True)
-            wide = jnp.transpose(jnp.broadcast_to(col, (tq, SLOT)))
-            delta_s[h : h + 1, pl.ds(pl.multiple_of(qt * tq, tq), tq)] = wide[0:1, :]
-        return 0
-
-    lax.fori_loop(0, rows // tq, deltas, 0)
-    dq_s[...] = jnp.zeros(dq_s.shape, f32)
-
-    def pair(kt, vt, kvt, qt, masked):
+
+    def before():
+        for name in LOADS:
+            if name != "part":
+                loads[name].wait()
+        loads["part"].wait()
+        dmid_swap().wait()
+        part_swap().wait()
+        vec[...] = jnp.zeros(vec.shape, f32)
+
+        def out_rows(r, _):
+            at = pl.ds(pl.multiple_of(r * tile, tile), tile)
+            mine = pl.ds(pl.multiple_of(ours + r * tile, tile), tile)
+            part_o[at, :] = (
+                m["resid"][mine, :] + m["part"][mine, :].astype(f32) + part_o[at, :].astype(f32)
+            ).astype(bf16)
+            return 0
+
+        lax.fori_loop(0, half // tile, out_rows, 0)
+        pltpu.make_async_copy(part_o, layer_out_ref, out_sem.at[0]).start()
+
+        def norm(r, _):
+            at = pl.ds(pl.multiple_of(r * tile, tile), tile)
+            dmid = m["dmid"][at, :].astype(f32) + dmid_o[at, :].astype(f32)
+            resid = m["resid"][at, :]
+            rho = lax.rsqrt(jnp.mean(resid * resid, axis=1, keepdims=True) + norm_eps)
+            n2 = resid * rho
+            vec[1:2, :] += jnp.sum(dmid * n2, axis=0, keepdims=True)
+            weighted = dmid * m["gain2"][...]
+            d_resid = m["cot"][at, :].astype(f32) + rho * (
+                weighted - n2 * jnp.mean(weighted * n2, axis=1, keepdims=True)
+            )
+            m["resid"][at, :] = d_resid
+            low = d_resid.astype(bf16)
+            dlow[at, :] = low
+            d_ctx = dot(low, m["w_slots"][...], NT)
+            do[at, :] = d_ctx.astype(bf16)
+            for h in range(heads):
+                cols = slice(h * SLOT, (h + 1) * SLOT)
+                prod = do[at, cols].astype(f32) * m["slots"][at, cols].astype(f32)
+                col = jnp.sum(prod, axis=1, keepdims=True)
+                wide = jnp.transpose(jnp.broadcast_to(col, (tile, SLOT)))
+                delta[h : h + 1, at] = wide[0:1, :]
+            return 0
+
+        lax.fori_loop(0, rows // tile, norm, 0)
+
+        def grad_out(k, _):
+            at = pl.ds(pl.multiple_of(k * 128, 128), 128)
+            put(0, at, dot(dlow[:, at], m["ctx"][...], TN))
+            return 0
+
+        lax.fori_loop(0, width // 128, grad_out, 0)
+        lane = lax.broadcasted_iota(jnp.int32, (tk, SLOT), 1)
+
+        def keys(i, _):
+            at = pl.ds(pl.multiple_of(i * tk, tk), tk)
+            k0[at, :] = jnp.where(lane < HEAD, m["kv"][at, :].astype(f32), 0.0).astype(bf16)
+            return 0
+
+        lax.fori_loop(0, (blk + 1) * (rows // tk), keys, 0)
+        dq[...] = jnp.zeros(dq.shape, f32)
+
+    def pair(kt, kvt, qt, masked):
         at = pl.ds(pl.multiple_of(qt * tq, tq), tq)
         grad = None
         for h in range(heads):
             cols = slice(h * SLOT, (h + 1) * SLOT)
-            q = q_ref[at, cols]
-            do = do_ref[at, cols]
+            q = m["q"][at, cols]
+            d_ctx = do[at, cols]
             s = dot(kt, q, NT)
-            p = jnp.exp(s - lse_ref[h : h + 1, at])
+            p = jnp.exp(s - m["lse"][h : h + 1, at])
             if masked is not None:
                 p = jnp.where(masked, p, 0.0)
-            dp = dot(kvt, do, NT)
-            ds = (p * (dp - delta_s[h : h + 1, at])).astype(bf16)
-            part = dot(ds, q, NN) + dot(p.astype(bf16), do, NN)
+            dp = dot(kvt, d_ctx, NT)
+            ds = (p * (dp - delta[h : h + 1, at])).astype(bf16)
+            part = dot(ds, q, NN) + dot(p.astype(bf16), d_ctx, NN)
             grad = part if grad is None else grad + part
-            dq_s[at, cols] += dot(ds, kt, TN)
+            dq[at, cols] += dot(ds, kt, TN)
         return grad
 
-    def key_tile(i, _):
-        at_k = pl.ds(pl.multiple_of(i * tk, tk), tk)
-        kt = k0[at_k, :]
-        kvt = kv_ref[at_k, :]
-        own = blk * (rows // tk)
-        first = jnp.maximum(i - own, 0) * (tk // tq)
+    def own_block():
         ki = lax.broadcasted_iota(jnp.int32, (tk, tq), 0)
         qi = lax.broadcasted_iota(jnp.int32, (tk, tq), 1)
 
-        @pl.when(i < own)
+        def key_tile(i, _):
+            at_k = pl.ds(pl.multiple_of(blk * rows + i * tk, tk), tk)
+            kt, kvt = k0[at_k, :], m["kv"][at_k, :]
+            first = i * (tk // tq)
+
+            def near(j, grad):
+                return grad + pair(kt, kvt, first + j, ki <= qi + j * tq)
+
+            def far(qt, grad):
+                return grad + pair(kt, kvt, qt, None)
+
+            grad = lax.fori_loop(0, tk // tq, near, jnp.zeros((tk, SLOT), f32))
+            grad = lax.fori_loop(first + tk // tq, rows // tq, far, grad)
+            dkv[at_k, :] = grad.astype(bf16)
+            return 0
+
+        lax.fori_loop(0, rows // tk, key_tile, 0)
+
+    def earlier(i):
+        at_k = pl.ds(pl.multiple_of(i * tk, tk), tk)
+        kt, kvt = k0[at_k, :], m["kv"][at_k, :]
+
+        def step(qt, grad):
+            return grad + pair(kt, kvt, qt, None)
+
+        grad = lax.fori_loop(0, rows // tq, step, jnp.zeros((tk, SLOT), f32))
+        dkv[at_k, :] = grad.astype(bf16)
+
+    def kv_copy(d):
+        to = lax.rem(blk + d, nb)
+        at = pl.ds(pl.multiple_of(to * rows, rows), rows)
+        return pltpu.make_async_remote_copy(
+            src_ref=dkv.at[at, :], dst_ref=dkv_o.at[d - 1],
+            send_sem=kv_send.at[d - 1], recv_sem=kv_recv.at[d - 1],
+            device_id={"blk": to}, device_id_type=pl.DeviceIdType.MESH,
+        )
+
+    def kv_start():
+        for d in range(1, nb):
+            @pl.when(lax.rem(blk + d, nb) < blk)
+            def _(d=d):
+                kv_copy(d).start()
+
+    def project():
+        for d in range(1, nb):
+            @pl.when(lax.rem(blk + d, nb) < blk)
+            def _(d=d):
+                kv_copy(d).wait_send()
+
+            @pl.when(lax.rem(blk + nb - d, nb) > blk)
+            def _(d=d):
+                kv_copy(d).wait_recv()
+                for r in range(rows // tile):
+                    at = pl.ds(pl.multiple_of(blk * rows + r * tile, tile), tile)
+                    total = dkv[at, :].astype(f32) + dkv_o[d - 1, r * tile : (r + 1) * tile].astype(f32)
+                    dkv[at, :] = total.astype(bf16)
+
+        rowsum[...] = jnp.zeros(rowsum.shape, f32)
+        lane = lax.broadcasted_iota(jnp.int32, (tile, SLOT), 1)
+
+        def unrotate(r, _):
+            at = pl.ds(pl.multiple_of(r * tile, tile), tile)
+            at_b = pl.ds(pl.multiple_of(blk * rows + r * tile, tile), tile)
+            table = m["cosine"][at, :], m["sine_a"][at, :], m["sine_b"][at, :]
+            for h in range(heads + 1):
+                cols = slice(h * SLOT, (h + 1) * SLOT)
+                if h < heads:
+                    v = jnp.where(lane < HEAD, turn(dq[at, cols] * HEAD**-0.5, *table), 0.0)
+                else:
+                    v = turn(dkv[at_b, :].astype(f32), *table)
+                low = v.astype(bf16)
+                dproj[at, cols] = low
+                rowsum[0:1, cols] += jnp.sum(low.astype(f32), axis=0, keepdims=True)
+            return 0
+
+        lax.fori_loop(0, rows // tile, unrotate, 0)
+
+        def d_in(to, first):
+            def step(r, _):
+                src = pl.ds(pl.multiple_of(first + r * tile, tile), tile)
+                at = pl.ds(pl.multiple_of(r * tile, tile), tile)
+                to[at, :] = dot(dproj[src, :], m["w_all"][...], NN).astype(bf16)
+                return 0
+
+            lax.fori_loop(0, half // tile, step, 0)
+
+        d_in(din_send, theirs)
+        din_swap().start()
+        d_in(din_own, ours)
+
+        def grads(k, _):
+            at = pl.ds(pl.multiple_of(k * 128, 128), 128)
+            g = dot(m["normed"][:, at], dproj[...], TN)
+            for h in range(heads):
+                put(nq + h * HEAD, at, g[:, h * SLOT : h * SLOT + HEAD])
+            put(2 * nq, at, g[:, heads * SLOT :])
+            return 0
+
+        lax.fori_loop(0, width // 128, grads, 0)
+
+    def finish():
+        din_swap().wait()
+
+        def step(r, _):
+            at = pl.ds(pl.multiple_of(r * tile, tile), tile)
+            mine = pl.ds(pl.multiple_of(ours + r * tile, tile), tile)
+            d_in = din_own[at, :].astype(f32) + din_o[at, :].astype(f32)
+            x = m["own_in"][at, :].astype(f32)
+            rho = lax.rsqrt(jnp.mean(x * x, axis=1, keepdims=True) + norm_eps)
+            n1 = x * rho
+            vec[0:1, :] += jnp.sum(d_in * n1, axis=0, keepdims=True)
+            weighted = d_in * m["gain1"][...]
+            grad = m["resid"][mine, :] + rho * (
+                weighted - n1 * jnp.mean(weighted * n1, axis=1, keepdims=True)
+            )
+            din_own[at, :] = grad.astype(bf16)
+            return 0
+
+        lax.fori_loop(0, half // tile, step, 0)
+        pltpu.make_async_copy(din_own, input_grad_ref, out_sem.at[1]).start()
+        for h in range(heads):
+            vec[2:3, h * HEAD : (h + 1) * HEAD] = rowsum[0:1, h * SLOT : h * SLOT + HEAD]
+        vec[2:3, nq : nq + SLOT] = rowsum[0:1, heads * SLOT :]
+        put(2 * nq + SLOT, slice(None), jnp.transpose(vec[...]))
+
+    n_attn = 2 + (nb - 1) * (rows // tk)
+
+    def compute(i):
+        pl.when(i == 0)(before)
+        pl.when(i == 1)(own_block)
+
+        @pl.when((i >= 2) & (i - 2 < blk * (rows // tk)))
         def _():
-            def step(qt, grad):
-                return grad + pair(kt, None, kvt, qt, None)
-
-            grad = lax.fori_loop(0, rows // tq, step, jnp.zeros((tk, SLOT), f32))
-            dkv_ref[at_k, :] = grad.astype(bf16)
-
-        @pl.when(i >= own)
-        def _():
-            grad = jnp.zeros((tk, SLOT), f32)
-            for j in range(tk // tq):
-                grad = grad + pair(kt, None, kvt, first + j, ki <= qi + j * tq)
-
-            def step(qt, grad):
-                return grad + pair(kt, None, kvt, qt, None)
-
-            grad = lax.fori_loop(first + tk // tq, rows // tq, step, grad)
-            dkv_ref[at_k, :] = grad.astype(bf16)
-
+            earlier(i - 2)
+
+        pl.when(i == n_attn)(kv_start)
+        pl.when(i == n_attn + 1)(project)
+        pl.when(i == n_attn + 2)(finish)
+
+    n = n_ffn + n_small
+    depth = max(st.stages for st in streams)
+
+    def slot(i, _):
+        for st in streams:
+            for s in reversed(range(st.stages)):
+                @pl.when((i - s >= 0) & (i - s < n))
+                def _(st=st, s=s):
+                    st.stage(s, i - s)
+
+        compute(i)
         return 0
 
-    lax.fori_loop(0, (blk + 1) * (rows // tk), key_tile, 0)
-
-    def clear(i, _):
-        dkv_ref[pl.ds(pl.multiple_of(i * tk, tk), tk), :] = jnp.zeros((tk, SLOT), bf16)
-        return 0
-
-    lax.fori_loop((blk + 1) * (rows // tk), total // tk, clear, 0)
-    dq_ref[...] = dq_s[...]
-
-
-def attn_bwd(info, q, kv, d_slots, slots, lse, heads):
-    rows = q.shape[0]
-    vm = pl.BlockSpec(memory_space=pltpu.VMEM)
+    lax.fori_loop(0, n + depth - 1, slot, 0)
+    pltpu.make_async_copy(part_o, layer_out_ref, out_sem.at[0]).wait()
+    pltpu.make_async_copy(din_own, input_grad_ref, out_sem.at[1]).wait()
+
+
+def backward(values, grads, heads, plane, line, nb):
+    rows, width = values["cot"].shape
+    half = rows // 2
+    keys = values["kv"].shape[0]
+    n_ffn = grads.shape[0]
+    n_small = -(-(2 * heads * HEAD + 2 * SLOT) // CHUNK)
+    assert n_ffn >= 5 + (nb - 1) * 2
+    streams = make_streams(width, plane, line)
+    hbm = pl.BlockSpec(memory_space=pl.ANY)
+    dma = pltpu.SemaphoreType.DMA
+    scratch = [pltpu.VMEM(values[name].shape, values[name].dtype) for name in LOADS]
+    scratch += [
+        dma((len(LOADS),)),
+        pltpu.VMEM((rows, width), bf16),
+        pltpu.VMEM((half, width), bf16),
+        pltpu.VMEM((rows, heads * SLOT), bf16),
+        pltpu.VMEM((rows, width), bf16),
+        pltpu.VMEM((8, rows), f32),
+        pltpu.VMEM((rows, heads * SLOT), f32),
+        pltpu.VMEM((keys, SLOT), bf16),
+        pltpu.VMEM((nb - 1, rows, SLOT), bf16),
+        pltpu.VMEM((keys, SLOT), bf16),
+        pltpu.VMEM((rows, (heads + 1) * SLOT), bf16),
+        pltpu.VMEM((n_small, width, CHUNK), bf16),
+        pltpu.VMEM((half, width), bf16),
+        pltpu.VMEM((half, width), bf16),
+        pltpu.VMEM((half, width), bf16),
+        pltpu.VMEM((8, (heads + 1) * SLOT), f32),
+        pltpu.VMEM((SLOT, width), f32),
+        dma((3,)),
+        dma((3,)),
+        dma((nb - 1,)),
+        dma((nb - 1,)),
+        dma((2,)),
+    ]
+    for st in streams:
+        scratch += st.scratch()
     return pl.pallas_call(
-        functools.partial(attn_bwd_kernel, heads, rows),
+        functools.partial(backward_kernel, heads, streams, n_ffn, n_small),
         out_shape=(
-            jax.ShapeDtypeStruct((rows, heads * SLOT), f32),
-            jax.ShapeDtypeStruct(kv.shape, bf16),
+            jax.ShapeDtypeStruct((n_ffn + n_small, width, CHUNK), bf16),
+            jax.ShapeDtypeStruct((half, width), bf16),
+            jax.ShapeDtypeStruct((half, width), bf16),
         ),
-        in_specs=[pl.BlockSpec(memory_space=pltpu.SMEM), vm, vm, vm, vm, vm],
-        out_specs=(vm, vm),
-        scratch_shapes=[
-            pltpu.VMEM(kv.shape, bf16),
-            pltpu.VMEM((8, rows), f32),
-            pltpu.VMEM((rows, heads * SLOT), f32),
-        ],
-        compiler_params=pltpu.CompilerParams(vmem_limit_bytes=48 * 2**20),
-        name="attn_bwd",
-    )(info, q, kv, d_slots, slots, lse)
+        in_specs=[hbm] * (len(LOADS) + 1),
+        out_specs=(hbm, hbm, hbm),
+        scratch_shapes=scratch,
+        compiler_params=pltpu.CompilerParams(
+            collective_id=0, has_side_effects=True, vmem_limit_bytes=60 * 2**20
+        ),
+        name="backward",
+    )(*[values[name] for name in LOADS], grads)
 
 
 def spread(weights, heads, first):
@@ -348,7 +876,8 @@
     start = blk * rows
     own_start = core * rows_own
 
-    x = gather_pair(layer_in, "tensor", 0).astype(f32)
+    x_low = gather_pair(layer_in, "tensor", 0)
+    x = x_low.astype(f32)
     cot = gather_pair(cotangent, "tensor", 0)
     positions = start + jnp.arange(rows, dtype=jnp.int32)
     live = positions % bucket < length
@@ -395,78 +924,53 @@
 
     ctx_other = partner(ctx, "tensor", 0)
     w_out_other = partner(w_out, "tensor", 0)
-    resid = x + (
-        jnp.dot(ctx, w_out, preferred_element_type=f32)
-        + jnp.dot(ctx_other, w_out_other, preferred_element_type=f32)
+    resid, grads, dmid, part = feed_forward(
+        x_low, ctx, ctx_other, w_out, w_out_other, mlp_gain[None, :], cot, w_gate, w_up, w_down
     )
-    rho2 = lax.rsqrt(jnp.mean(resid * resid, axis=1, keepdims=True) + norm_eps)
-    n2 = resid * rho2
-    mlp_in = (n2 * mlp_gain).astype(bf16)
-    gate = jnp.dot(mlp_in, w_gate, preferred_element_type=f32)
-    upper = jnp.dot(mlp_in, w_up, preferred_element_type=f32)
-    sigma = 1.0 / (1.0 + jnp.exp(-gate))
-    activ = gate * sigma
-    hidden = (activ * upper).astype(bf16)
-    grad_down = reduce_grad(contract_rows(hidden, cot, bf16))
-    d_hidden = contract_cols(cot, w_down)
-    d_gate = (d_hidden * upper * sigma * (1.0 + gate * (1.0 - sigma))).astype(bf16)
-    d_up = (d_hidden * activ).astype(bf16)
-    grad_gate = reduce_grad(contract_rows(mlp_in, d_gate, bf16))
-    grad_up = reduce_grad(contract_rows(mlp_in, d_up, bf16))
-    d_mid_part = (contract_cols(d_gate, w_gate) + contract_cols(d_up, w_up)).astype(bf16)
-    d_mid = d_mid_part.astype(f32) + partner(d_mid_part, "tensor", 0).astype(f32)
-    ffn_out = jnp.dot(hidden, w_down, preferred_element_type=f32).astype(bf16)
-    ffn_out = scatter_pair(ffn_out, "tensor", 0).astype(f32)
-    own = lambda v: lax.dynamic_slice_in_dim(v, own_start, rows_own, 0)
-    layer_out = (own(resid) + ffn_out).astype(bf16)
-    mlp_gain_part = jnp.sum(d_mid * n2, axis=0)
-    d_resid = cot.astype(f32) + norm_back(d_mid, n2, rho2, mlp_gain)
-    d_resid_low = d_resid.astype(bf16)
-    grad_out = contract_rows(ctx, d_resid_low, bf16)
-    w_out_slots = spread(w_out, heads, False)
-    d_slots = contract_cols(d_resid_low, w_out_slots, f32).astype(bf16)
-    dq, dkv = attn_bwd(info, q_low, kv, d_slots, ctx_slots, lse, heads)
-    for axis, bit in reversed(bits_of("blk")):
-        dkv = scatter_pair(dkv, axis, bit)
-    keep = (jnp.arange(SLOT) < HEAD).astype(f32)
-    dq = jnp.where(keep > 0, dq.reshape(rows, heads, SLOT), 0.0).reshape(rows, heads * SLOT)
-    d_proj = rotate(
-        jnp.concatenate([dq * HEAD**-0.5, dkv.astype(f32)], 1), -1.0
-    ).astype(bf16)
-    grad_all = contract_rows(d_proj, normed_in, bf16)
-    bias_all = jnp.sum(d_proj.astype(f32), axis=0)
-    d_in = contract_cols(d_proj, w_all.T).astype(bf16)
-    d_in = scatter_pair(d_in, "tensor", 0).astype(f32)
-    n1_own = own(n1)
-    attn_gain_part = jnp.sum(d_in * n1_own, axis=0)
-    input_grad = (own(d_resid) + norm_back(d_in, n1_own, own(rho1), attn_gain)).astype(bf16)
-
-    qk = heads * SLOT
-    grad_q = grad_all[:qk].reshape(heads, SLOT, width)[:, :HEAD].reshape(heads * HEAD, width)
-    bias_q = bias_all[:qk].reshape(heads, SLOT)[:, :HEAD].reshape(heads * HEAD)
+    values = dict(
+        dmid=dmid,
+        resid=resid,
+        cot=cot,
+        w_slots=spread(w_out, heads, False),
+        ctx=ctx,
+        slots=ctx_slots,
+        q=q_low,
+        kv=kv,
+        lse=lse,
+        cosine=cos_w,
+        sine_a=sin_a,
+        sine_b=sin_b,
+        normed=normed_in,
+        w_all=w_all,
+        own_in=layer_in,
+        gain1=attn_gain[None, :],
+        gain2=mlp_gain[None, :],
+        part=part,
+    )
+    sums, layer_out, input_grad = backward(
+        values, grads, heads, bits_of("blk"), bits_of("batch"), blocks
+    )
+    n_ffn = grads.shape[0]
+    ffn = sums[:n_ffn].astype(f32)
+    grad_down = ffn[:, :, :PART].transpose(0, 2, 1).reshape(n_ffn * PART, width)
+    grad_gate = ffn[:, :, PART : 2 * PART].transpose(1, 0, 2).reshape(width, n_ffn * PART)
+    grad_up = ffn[:, :, 2 * PART :].transpose(1, 0, 2).reshape(width, n_ffn * PART)
+    small = sums[n_ffn:].transpose(1, 0, 2).reshape(width, -1).astype(f32)
     nq = heads * HEAD
-    small = jnp.concatenate([grad_out, grad_q, grad_all[qk:]], 0)
-    small = jnp.pad(small, ((0, (-small.shape[0]) % 256), (0, 0)))
-    small = reduce_grad(small)
-    vectors = jnp.concatenate([bias_q, bias_all[qk:], attn_gain_part, mlp_gain_part])
-    vectors = lax.psum(vectors, ("batch", "blk"))
-    nb = bias_all.shape[0] - qk + nq
-    attn_gain_sum = lax.psum(vectors[nb : nb + width], "tensor")
-    grad_query = small[nq : 2 * nq].T
-    grad_key = small[2 * nq : 2 * nq + HEAD].T
-    grad_value = small[2 * nq + HEAD : 2 * nq + 2 * HEAD].T
+    vec = small[:, 2 * nq + SLOT : 2 * nq + SLOT + 3].T
+    gain = vec[0] + partner(vec[0], "tensor", 0)
     return (
         layer_out,
         input_grad,
-        attn_gain_sum,
-        grad_query,
-        vectors[:nq],
-        grad_key,
-        vectors[nq : nq + HEAD],
-        grad_value,
-        vectors[nq + HEAD : nq + 2 * HEAD],
-        small[:nq],
-        vectors[nb + width :],
+        gain,
+        small[:, nq : 2 * nq],
+        vec[2, :nq],
+        small[:, 2 * nq : 2 * nq + HEAD],
+        vec[2, nq : nq + HEAD],
+        small[:, 2 * nq + HEAD : 2 * nq + 2 * HEAD],
+        vec[2, nq + HEAD : nq + 2 * HEAD],
+        small[:, :nq].T,
+        vec[1],
         grad_gate,
         grad_up,
         grad_down,

time: 854 us -> 652 us (0.76); the launches traced: 838 us -> 646 us
  Pallas kernels: 43.3 us -> 459 us
  starting transfers between devices: 237 us -> 5.46 us
  waiting for transfers between devices: 223 us -> 16.5 us
  matrix products: 94.9 us -> 2.36 us
  blocking collectives: 78.5 us -> 0 us
  local copies, waits for them, and re-layouts: 49.3 us -> 113 us
  other arithmetic: 110 us -> 48.5 us
    pallas_call x1 -> x2, Pallas kernels: 24.6 us -> 440 us  [the longest x1 357 us: backward(): pl.pallas_call(functools.partial(backward_kernel, heads, streams, n_ffn,...]
    ppermute x69 -> x7, starting transfers between devices: 237 us -> 5.46 us  [partner(): return lax.ppermute(value, axis, [(i, i ^ 1 << bit) for i in range(n)])]
    ppermute x69 -> x7, waiting for transfers between devices: 223 us -> 16.5 us  [partner(): return lax.ppermute(value, axis, [(i, i ^ 1 << bit) for i in range(n)])]
    psum x2 -> x0, blocking collectives: 78.5 us -> none  [the longest x1 75.5 us: shards(): vectors = lax.psum(vectors, ('batch', 'blk'))]
    dot_general x11 -> x1, matrix products: 64.4 us -> 2.36 us  [dot(): lax.dot_general(left, right, (dims, ((), ())), preferred_element_type=kind)]
    transpose x1 -> x6, local copies, waits for them, and re-layouts: 1.26 us -> 54.2 us  [the longest x2 28.5 us: shards(): grad_down = ffn[:, :, :PART].transpose(0, 2, 1).reshape(n_ffn * PART, width)]
    select_n x28 -> x2, other arithmetic: 32.5 us -> 1.61 us  [in_order(): jnp.where(first, jnp.concatenate([own, other], 0), jnp.concatenate([other...]
    dot_general x5 -> x0, matrix products: 30.5 us -> none  [the longest x1 8.72 us: shards(): ffn_out = jnp.dot(hidden, w_down, preferred_element_type=f32).astype(bf16)]
  transfers between devices with their start and end apart: 69 -> 7, of which waited for: 31 -> 2; matrix products, arithmetic and copies ran while one was open for 21% -> 15% of each run, Pallas kernels for 5% -> 3%
where the time goes in v2:
time: 652 us; the launch traced here: 646 us
  Pallas kernels  459 us (70%)
  local copies, waits for them, and re-layouts  113 us (17%)
  other arithmetic  48.5 us (7%)
  waiting for transfers between devices  16.5 us (3%)
    pallas_call x1, Pallas kernels, backward(): pl.pallas_call(functools.partial(backward_kernel, heads, streams, n_ffn,...  357 us
    pallas_call x1, Pallas kernels, feed_forward(): pl.pallas_call(ffn_kernel, grid=(steps,), out_shape=(jax.ShapeDtypeStruct...  83.1 us
    unnamed x45, local copies, waits for them, and re-layouts  29.6 us
    transpose x2, local copies, waits for them, and re-layouts, shards(): grad_down = ffn[:, :, :PART].transpose(0, 2, 1).reshape(n_ffn * PART, width)  28.5 us
    pallas_call x1, Pallas kernels, attn_fwd(): pl.pallas_call(functools.partial(attn_fwd_kernel, heads, rows), out_shape...  18.7 us
    ppermute x7, waiting for transfers between devices, partner(): return lax.ppermute(value, axis, [(i, i ^ 1 << bit) for i in range(n)])  16.5 us
    convert_element_type x1, other arithmetic, shards(): ffn = sums[:n_ffn].astype(f32)  14.9 us
  transfers between devices with their start and end apart: 7, of which 2 were waited for; matrix products, arithmetic and copies ran while one was open for 15% of the time, Pallas kernels for 3%

profile of v2, /device:TPU:0, one launch (start us, length us, event | category | flops | bytes accessed | tf_op | source)
XLA Modules:
  0.0 646.2 jit_solution(17019145022287393101)
XLA Ops:
  1.3 0.8 reshape_broadcast_in_dim.3
  2.1 1.3 concatenate.68
  3.5 0.8 maximum_convert_fusion
  4.3 1.9 multiply_cosine_fusion
  6.7 2.6 fusion.1
  9.9 0.7 copy-done.6
  11.1 2.4 fusion.11
  13.5 0.8 add_bitcast_fusion
  14.4 1.3 copy-done.5
  15.7 1.0 copy.48
  16.7 3.3 fusion.13
  20.0 4.7 fusion.12
  24.7 6.1 maximum_multiply_fusion
  31.1 5.9 fusion
  37.0 1.0 slice.96
  38.0 2.6 collective-permute-start.1
  40.6 6.9 %collective-permute-done.1 = bf16[1024,128]{1,0:T(8,128)(2,1)S(1)} collective-permute-done((bf16[1024,128]{1,0:T(8,128)(2,1)S(1)}, bf16[1024,128]{1,0:T(8,128)(2,1)S(1)}, u32[]{:S(2)}, u32[]{:S(2)}) %collective-permute-start.1) | collective-permute-done | bytes 262176 | tf_op jit(solution)/shard_map/ppermute | solution.py:45
  47.7 1.8 collective-permute-start.2
  50.2 1.7 slice_multiply_fusion.q_ref.refs_6_
  52.0 9.6 %collective-permute-done.2 = bf16[2048,128]{1,0:T(8,128)(2,1)} collective-permute-done((bf16[2048,128]{1,0:T(8,128)(2,1)S(1)}, bf16[2048,128]{1,0:T(8,128)(2,1)}, u32[]{:S(2)}, u32[]{:S(2)}) %collective-permute-start.2) | collective-permute-done | bytes 524320 | tf_op jit(solution)/shard_map/ppermute | solution.py:45
  61.6 1.5 maximum_select_fusion.2.kv_ref.refs_7_
  63.1 18.7 %attn_fwd.1 = (bf16[1024,448]{1,0:T(8,128)(2,1)S(1)}, bf16[1024,896]{1,0:T(8,128)(2,1)S(1)}, f32[8,1024]{1,0:T(8,128)S(1)}) custom-call(s32[2]{0:T(128)S(1)} %pad_add_fusion.info, bf16[1024,896]{1,0:T(8,128)(2,1)S(1)} %slice_multiply_fusion.q_ref.refs_6_, bf16[4096,128]{1,0:T(8,128)(2,1)S(1)} %maximum_select_fusion.2.kv_ref.refs_7_), custom_call_target="tpu_custom_call" | custom-call | tf_op jit(solution)/shard_map/attn_fwd/pallas_call | solution.py:173
  81.8 1.1 copy-done.2
  82.9 1.3 copy-done.3
  84.1 0.6 copy-done.4
  84.7 2.2 copy.38
  88.6 2.5 concatenate.85
  91.2 2.8 pad_maximum_fusion.refs_13_
  94.0 3.8 fusion.4.cot_ref.refs_2_
  97.8 2.2 copy.39.ctx_o_ref
  100.1 83.1 %ffn.1 = (f32[1024,896]{1,0:T(8,128)}, bf16[19,896,384]{2,1,0:T(8,128)(2,1)}, bf16[1024,896]{1,0:T(8,128)(2,1)}, bf16[1024,896]{1,0:T(8,128)(2,1)}) custom-call(bf16[1024,896]{1,0:T(8,128)(2,1)} %copy-done.6, bf16[1024,448]{1,0:T(8,128)(2,1)} %copy-done.2, bf16[1024,448]{1,0:T(8,128)(2,1)} %copy.39.ctx_o_ref, bf16[448,896]{1,0:T(8,128)(2,1)} %wo_ref.1, ...), custom_call_target="tpu_custom_call" | custom-call | tf_op jit(solution)/shard_map/ffn/pallas_call | solution.py:264
  183.2 356.9 %backward.1 = (bf16[22,896,384]{2,1,0:T(8,128)(2,1)}, bf16[512,896]{1,0:T(8,128)(2,1)}, bf16[512,896]{1,0:T(8,128)(2,1)}) custom-call(bf16[1024,896]{1,0:T(8,128)(2,1)} %get-tuple-element.25.refs_0_, f32[1024,896]{1,0:T(8,128)} %get-tuple-element.26.refs_1_, bf16[1024,896]{1,0:T(8,128)(2,1)} %fusion.4.cot_ref.refs_2_, bf16[896,896]{1,0:T(8,128)(2,1)} %bitcast.66, ...), custom_call_target="tpu_custom_call" | custom-call | tf_op jit(solution)/shard_map/backward/pallas_call | solution.py:819
  540.1 3.8 convert_bitcast_fusion
  544.0 5.6 copy.40
  549.6 0.8 slice_bitcast_fusion.4
  550.4 1.8 fusion.14
  552.2 3.8 slice_bitcast_fusion.3
  556.0 14.9 %slice_convert_fusion = f32[19,896,384]{2,1,0:T(8,128)} fusion(bf16[22,896,384]{2,1,0:T(8,128)(2,1)} %get-tuple-element.33), kind=kLoop, calls=%fused_computation | loop fusion | flops 6537216 | bytes 39223296 | tf_op jit(solution)/shard_map/convert_element_type | solution.py:954
  570.9 0.6 slice_reduce_fusion
  571.5 17.9 %slice_bitcast_fusion = (f32[19,128,896]{1,2,0:T(8,128)}, f32[896,19,128]{2,0,1:T(8,128)}, f32[896,19,128]{2,0,1:T(8,128)}) fusion(f32[19,896,384]{2,1,0:T(8,128)} %slice_convert_fusion), kind=kLoop, calls=%fused_computation.1 | loop fusion | bytes 52297728 | tf_op jit(solution)/shard_map/transpose | solution.py:955
  590.6 10.5 %copy.43 = f32[19,128,896]{2,1,0:T(8,128)} copy(f32[19,128,896]{1,2,0:T(8,128)} %get-tuple-element.66) | data formatting | bytes 17432576 | tf_op jit(solution)/shard_map/transpose | solution.py:955
  601.1 10.6 %copy.42 = f32[896,19,128]{0,2,1:T(8,128)} copy(f32[896,19,128]{2,0,1:T(8,128)} %get-tuple-element.67) | data formatting | bytes 17432576 | tf_op jit(solution)/shard_map/transpose | solution.py:957
  611.7 10.5 %copy.45 = f32[896,2432]{1,0:T(8,128)} copy(f32[896,2432]{0,1:T(8,128)} %bitcast.57) | data formatting | bytes 17432576
  622.3 10.6 %copy.41 = f32[896,19,128]{0,2,1:T(8,128)} copy(f32[896,19,128]{2,0,1:T(8,128)} %get-tuple-element.68) | data formatting | bytes 17432576 | tf_op jit(solution)/shard_map/transpose | solution.py:956
  632.8 10.7 %copy.44 = f32[896,2432]{1,0:T(8,128)} copy(f32[896,2432]{0,1:T(8,128)} %bitcast.58) | data formatting | bytes 17432576
  643.5 0.6 add.65
  644.1 0.9 copy.57
  645.0 0.9 copy.58
  (66 shorter events, 5.6 us)
Async XLA Ops:
  0.6 6.1 copy-start.12
  0.7 6.0 collective-permute-start
  3.5 7.1 %copy-start.8 = (bf16[7,128,896]{2,1,0:T(8,128)(2,1)}, bf16[7,128,896]{2,1,0:T(8,128)(2,1)S(1)}, u32[]{:S(2)}) copy-start(bf16[7,128,896]{2,1,0:T(8,128)(2,1)S(1)} %concatenate.68) | copy-start | bytes 4816900
  4.3 5.0 copy-start.18
  6.4 24.4 %copy-start.9 = (f32[1024,128]{1,0:T(8,128)}, f32[1024,128]{1,0:T(8,128)S(1)}, u32[]{:S(2)}) copy-start(f32[1024,128]{1,0:T(8,128)S(1)} %maximum_maximum_fusion.refs_9_) | copy-start | bytes 1572868
  6.7 18.1 %copy-start.10 = (f32[1024,128]{1,0:T(8,128)}, f32[1024,128]{1,0:T(8,128)S(1)}, u32[]{:S(2)}) copy-start(f32[1024,128]{1,0:T(8,128)S(1)} %get-tuple-element.77.refs_10_) | copy-start | bytes 1572868
  6.7 18.1 %copy-start.11 = (f32[1024,128]{1,0:T(8,128)}, f32[1024,128]{1,0:T(8,128)S(1)}, u32[]{:S(2)}) copy-start(f32[1024,128]{1,0:T(8,128)S(1)} %get-tuple-element.78.refs_11_) | copy-start | bytes 1572868
  6.7 4.4 copy-start.15
  6.7 4.4 copy-start.16
  9.3 1.2 copy-start.6
  9.9 1.2 copy-start.7
  13.5 2.2 copy-start.5
  38.0 9.5 %collective-permute-start.1 = (bf16[1024,128]{1,0:T(8,128)(2,1)S(1)}, bf16[1024,128]{1,0:T(8,128)(2,1)S(1)}, u32[]{:S(2)}, u32[]{:S(2)}) collective-permute-start(bf16[1024,128]{1,0:T(8,128)(2,1)S(1)} %slice.96), channel_id=1, source_target_pairs={{0,2},{2,0},{4,6},{6,4},{1,3},{3,1},{5,7},{7,5},{8,10},{10,8},{12,... | collective-permute-start | bytes 786440 | tf_op jit(solution)/shard_map/ppermute | solution.py:45
  47.7 13.9 %collective-permute-start.2 = (bf16[2048,128]{1,0:T(8,128)(2,1)S(1)}, bf16[2048,128]{1,0:T(8,128)(2,1)}, u32[]{:S(2)}, u32[]{:S(2)}) collective-permute-start(bf16[2048,128]{1,0:T(8,128)(2,1)S(1)} %maximum_select_fusion.3), channel_id=1, source_target_pairs={{0,4},{2,6},{4,0},{6,2},{1,5},{3,7},{5,1},{7,3},{8,12},{10,14},{12... | collective-permute-start | bytes 1572872 | tf_op jit(solution)/shard_map/ppermute | solution.py:45
  49.5 44.5 %collective-permute-start.5 = (bf16[512,896]{1,0:T(8,128)(2,1)}, bf16[512,896]{1,0:T(8,128)(2,1)}, u32[]{:S(2)}, u32[]{:S(2)}) collective-permute-start(bf16[512,896]{1,0:T(8,128)(2,1)} %param.16), channel_id=1, source_target_pairs={{0,1},{1,0},{2,3},{3,2},{4,5},{5,4},{6,7},{7,6},{8,9},{9,8},{10,11... | collective-permute-start | bytes 2752520 | tf_op jit(solution)/shard_map/ppermute | solution.py:45
  51.9 39.2 %copy-start = (bf16[1024,896]{1,0:T(8,128)(2,1)}, bf16[1024,896]{1,0:T(8,128)(2,1)S(1)}, u32[]{:S(2)}) copy-start(bf16[1024,896]{1,0:T(8,128)(2,1)S(1)} %slice_multiply_fusion.q_ref.refs_6_) | copy-start | bytes 5505028
  51.9 36.1 %copy-start.19 = (f32[896]{0:T(1024)S(1)}, f32[896]{0:T(1024)}, u32[]{:S(2)}) copy-start(f32[896]{0:T(1024)} %param.26) | copy-start | bytes 10756
  63.0 31.0 %copy-start.1 = (bf16[4096,128]{1,0:T(8,128)(2,1)}, bf16[4096,128]{1,0:T(8,128)(2,1)S(1)}, u32[]{:S(2)}) copy-start(bf16[4096,128]{1,0:T(8,128)(2,1)S(1)} %maximum_select_fusion.2.kv_ref.refs_7_) | copy-start | bytes 3145732
  63.0 28.1 %copy-start.17 = (bf16[896,64]{0,1:T(8,128)(2,1)S(1)}, bf16[896,64]{0,1:T(8,128)(2,1)}, u32[]{:S(2)}) copy-start(bf16[896,64]{0,1:T(8,128)(2,1)} %param.21) | copy-start | bytes 344068
  81.8 1.1 copy-start.2
  82.9 1.3 copy-start.3
  84.1 0.6 copy-start.4
  87.0 10.9 %collective-permute-start.3 = (bf16[1024,448]{0,1:T(8,128)(2,1)}, bf16[1024,448]{0,1:T(8,128)(2,1)}, u32[]{:S(2)}, u32[]{:S(2)}) collective-permute-start(bf16[1024,448]{0,1:T(8,128)(2,1)} %copy.38), channel_id=1, source_target_pairs={{0,1},{1,0},{2,3},{3,2},{4,5},{5,4},{6,7},{7,6},{8,9},{9,8},{10,11... | collective-permute-start | bytes 2752520 | tf_op jit(solution)/shard_map/ppermute | solution.py:45
  87.0 13.1 %collective-permute-start.4 = (bf16[448,896]{1,0:T(8,128)(2,1)}, bf16[448,896]{1,0:T(8,128)(2,1)}, u32[]{:S(2)}, u32[]{:S(2)}) collective-permute-start(bf16[448,896]{1,0:T(8,128)(2,1)} %wo_ref.1), channel_id=1, source_target_pairs={{0,1},{1,0},{2,3},{3,2},{4,5},{5,4},{6,7},{7,6},{8,9},{9,8},{10,11... | collective-permute-start | bytes 2408456 | tf_op jit(solution)/shard_map/ppermute | solution.py:45
  571.5 72.0 %collective-permute-start.6 = (f32[896]{0:T(1024)S(1)}, f32[896]{0:T(1024)S(1)}, u32[]{:S(2)}, u32[]{:S(2)}) collective-permute-start(f32[896]{0:T(1024)S(1)} %get-tuple-element.63), channel_id=1, source_target_pairs={{0,1},{1,0},{2,3},{3,2},{4,5},{5,4},{6,7},{7,6},{8,9},{9,8},{10,11... | collective-permute-start | bytes 10760 | tf_op jit(solution)/shard_map/ppermute | solution.py:45
  632.8 11.3 %copy-start.14 = (bf16[512,896]{1,0:T(8,128)(2,1)S(1)}, bf16[512,896]{1,0:T(8,128)(2,1)}, u32[]{:S(2)}) copy-start(bf16[512,896]{1,0:T(8,128)(2,1)} %get-tuple-element.99) | copy-start | bytes 2752516
  632.8 12.2 %copy-start.13 = (bf16[512,896]{1,0:T(8,128)(2,1)S(1)}, bf16[512,896]{1,0:T(8,128)(2,1)}, u32[]{:S(2)}) copy-start(bf16[512,896]{1,0:T(8,128)(2,1)} %get-tuple-element.100) | copy-start | bytes 2752516

commit v3 on v2

--- a/solution.py
+++ b/solution.py
@@ -3,6 +3,7 @@
 
 import jax
 import jax.numpy as jnp
+import numpy as np
 from jax import lax
 from jax.experimental import pallas as pl
 from jax.experimental.pallas import tpu as pltpu
@@ -27,174 +28,321 @@
 TN = ((0,), (0,))
 
 
-def contract_rows(left, right, kind=f32):
-    return dot(left, right, TN, kind)
-
-
-def contract_cols(left, right, kind=f32):
-    return dot(left, right, NT, kind)
-
-
-def norm_back(grad, normed, scale, gain):
-    weighted = grad * gain
-    return scale * (weighted - normed * jnp.mean(weighted * normed, axis=1, keepdims=True))
-
-
-def partner(value, axis, bit):
-    n = lax.axis_size(axis)
-    return lax.ppermute(value, axis, [(i, i ^ (1 << bit)) for i in range(n)])
-
-
-def bits_of(axis):
-    return [(axis, bit) for bit in range(int(math.log2(lax.axis_size(axis))))]
-
-
-def my_bit(axis, bit):
-    return (lax.axis_index(axis) >> bit) & 1
-
-
-def in_order(own, other, axis, bit):
-    first = my_bit(axis, bit) == 0
-    return jnp.where(
-        first, jnp.concatenate([own, other], 0), jnp.concatenate([other, own], 0)
+def bits_of(mesh_axis):
+    return [(mesh_axis, bit) for bit in range(int(math.log2(lax.axis_size(mesh_axis))))]
+
+
+def rotary_table(count):
+    half = HEAD // 2
+    freq = np.float32(rope_base) ** (-(np.arange(half, dtype=np.float32) * np.float32(2.0)) / np.float32(HEAD))
+    phase = np.arange(count, dtype=np.float32)[:, None] * freq[None, :].astype(np.float32)
+    phase = phase.astype(np.float64)
+    return np.concatenate([np.cos(phase), np.sin(phase)], 1).astype(np.float32)
+
+
+def spread_table(table):
+    n = table.shape[0]
+    wide = jnp.concatenate([table, jnp.zeros_like(table)], 1)
+    lane = lax.broadcasted_iota(jnp.int32, (n, SLOT), 1)
+    cosine = jnp.where(lane < 32, wide, jnp.where(lane < HEAD, pltpu.roll(wide, 32, 1), 1.0))
+    sine_a = jnp.where(lane < 32, pltpu.roll(wide, SLOT - 32, 1), 0.0)
+    sine_b = jnp.where((lane >= 32) & (lane < HEAD), wide, 0.0)
+    return cosine, sine_a, sine_b
+
+
+def turn(v, table, sign):
+    cosine, sine_a, sine_b = table
+    return v * cosine + sign * (
+        pltpu.roll(v, 32, 1) * sine_b - pltpu.roll(v, SLOT - 32, 1) * sine_a
     )
 
 
-def gather_pair(own, axis, bit):
-    return in_order(own, partner(own, axis, bit), axis, bit)
-
-
-def scatter_pair(value, axis, bit):
-    half = value.shape[0] // 2
-    mine = my_bit(axis, bit)
-    keep = lax.dynamic_slice_in_dim(value, mine * half, half, 0)
-    send = lax.dynamic_slice_in_dim(value, (1 - mine) * half, half, 0)
-    got = partner(send, axis, bit)
-    return (keep.astype(f32) + got.astype(f32)).astype(bf16)
-
-
-def add_pair(value, axis, bit):
-    got = partner(value, axis, bit)
-    return (value.astype(f32) + got.astype(f32)).astype(bf16)
-
-
-def reduce_all(value, steps):
-    halved = []
-    for axis, bit in steps:
-        if value.shape[0] % 16 == 0:
-            value = scatter_pair(value, axis, bit)
-            halved.append((axis, bit))
-        else:
-            value = add_pair(value, axis, bit)
-    for axis, bit in reversed(halved):
-        value = gather_pair(value, axis, bit)
-    return value
-
-
-def reduce_grad(value):
-    half = value.shape[0] // 2
-    plane, line = bits_of("blk"), bits_of("batch")
-    first = reduce_all(value[:half], plane + line)
-    second = reduce_all(value[half:], plane[::-1] + line)
-    return jnp.concatenate([first, second], 0).astype(f32)
-
-
-def attn_fwd_kernel(
-    heads, rows, info, q_ref, kv_ref, ctx_ref, slots_ref, lse_ref, k1, v1, q1, m_s, acc_s
-):
-    tq, tk = 256, 512
-    blk, length = info[0], info[1]
-    total = kv_ref.shape[0]
-    lane = lax.broadcasted_iota(jnp.int32, (tk, SLOT), 1)
-    row = lax.broadcasted_iota(jnp.int32, (tk, SLOT), 0)
-
-    def prepare(i, _):
-        at = pl.ds(i * tk, tk)
-        kv = kv_ref[at, :].astype(f32)
-        dead = jnp.where(row + i * tk < length, 0.0, masked_value)
-        k1[at, :] = jnp.where(lane < HEAD, kv, jnp.where(lane == HEAD, dead, 0.0)).astype(bf16)
-        v1[at, :] = jnp.where(lane < HEAD, 1.0, kv).astype(bf16)
+def meet(peers):
+    barrier = pltpu.get_barrier_semaphore()
+    for peer in peers:
+        pl.semaphore_signal(barrier, 1, device_id=peer, device_id_type=pl.DeviceIdType.MESH)
+    pl.semaphore_wait(barrier, len(peers))
+
+
+def remote(src, dst, send, recv, peer):
+    return pltpu.make_async_remote_copy(
+        src_ref=src, dst_ref=dst, send_sem=send, recv_sem=recv,
+        device_id=peer, device_id_type=pl.DeviceIdType.MESH,
+    )
+
+
+ONES = 72
+FRONT_IN = ("own_in", "own_cot", "wq", "wk", "wv", "bq", "bk", "bv", "gain", "table")
+FRONT_OUT = ("x", "cot", "normed", "q", "kv", "ctx", "ctx_o", "slots", "lse")
+
+
+def front_kernel(heads, length_ref, *refs):
+    ni, no = len(FRONT_IN), len(FRONT_OUT)
+    hbm = dict(zip(FRONT_IN, refs[:ni]))
+    out = dict(zip(FRONT_OUT, refs[ni : ni + no]))
+    m = dict(zip(FRONT_OUT, refs[ni + no : ni + 2 * no]))
+    (
+        wq, wk, wv, bq, bk, bv, gain, table, q1, k1, vt1, m_s, acc_s,
+        load_sem, out_sem, pair_send, pair_recv, kv_send, kv_recv,
+    ) = refs[ni + 2 * no :]
+    w = dict(zip(FRONT_IN[2:], (wq, wk, wv, bq, bk, bv, gain, table)))
+    rows, width = m["x"].shape
+    half = rows // 2
+    blk, nb = lax.axis_index("blk"), lax.axis_size("blk")
+    core = lax.axis_index("tensor")
+    other = {"tensor": 1 - core}
+    ours = pl.multiple_of(core * half, 16)
+    theirs = pl.multiple_of((1 - core) * half, 16)
+    start = blk * rows
+    length = length_ref[0, 0]
+    tile, tk = 256, 512
+
+    loads = [
+        pltpu.make_async_copy(hbm["own_in"], m["x"].at[pl.ds(ours, half), :], load_sem.at[0]),
+        pltpu.make_async_copy(hbm["own_cot"], m["cot"].at[pl.ds(ours, half), :], load_sem.at[1]),
+    ] + [
+        pltpu.make_async_copy(hbm[name], w[name], load_sem.at[2 + i])
+        for i, name in enumerate(FRONT_IN[2:])
+    ]
+    for copy in loads:
+        copy.start()
+    meet([other] + [{"blk": lax.rem(blk + d, nb)} for d in range(1, nb)])
+
+    def swap(k, src, dst):
+        return remote(src, dst, pair_send.at[k], pair_recv.at[k], other)
+
+    def x_swap():
+        return swap(0, hbm["own_in"], m["x"].at[pl.ds(ours, half), :])
+
+    def cot_swap():
+        return swap(1, hbm["own_cot"], m["cot"].at[pl.ds(ours, half), :])
+
+    def ctx_swap():
+        return swap(2, m["ctx"], m["ctx_o"])
+
+    def save(name):
+        i = FRONT_OUT.index(name)
+        return pltpu.make_async_copy(m[name], out[name], out_sem.at[i])
+
+    x_swap().start()
+    cot_swap().start()
+    loads[0].wait()
+    for copy in loads[2:]:
+        copy.wait()
+    lane = lax.broadcasted_iota(jnp.int32, (tile, SLOT), 1)
+
+    def rows_in(first):
+        def step(r, _):
+            at = pl.ds(pl.multiple_of(first + r * tile, tile), tile)
+            x = m["x"][at, :].astype(f32)
+            rho = lax.rsqrt(jnp.mean(x * x, axis=1, keepdims=True) + norm_eps)
+            normed = (x * rho * gain[...]).astype(bf16)
+            m["normed"][at, :] = normed
+            factors = spread_table(table[at, :])
+            proj = dot(normed, wq[...], NN) + bq[...].astype(f32)
+            zero = jnp.zeros((tile, HEAD), f32)
+            for h in range(heads):
+                cols = slice(h * SLOT, (h + 1) * SLOT)
+                v = jnp.concatenate([proj[:, h * HEAD : (h + 1) * HEAD], zero], 1)
+                v = turn(v, factors, 1.0).astype(bf16).astype(f32) * HEAD**-0.5
+                m["q"][at, cols] = v.astype(bf16)
+                q1[at, cols] = jnp.where(lane == HEAD, 1.0, v).astype(bf16)
+            kv = jnp.concatenate(
+                [
+                    dot(normed, wk[...], NN) + bk[...].astype(f32),
+                    dot(normed, wv[...], NN) + bv[...].astype(f32),
+                ],
+                1,
+            )
+            at_b = pl.ds(pl.multiple_of(start + first + r * tile, tile), tile)
+            m["kv"][at_b, :] = turn(kv, factors, 1.0).astype(bf16)
+            return 0
+
+        lax.fori_loop(0, half // tile, step, 0)
+
+    rows_in(ours)
+    x_swap().wait()
+    rows_in(theirs)
+
+    def kv_copy(d):
+        at = pl.ds(pl.multiple_of(blk * rows, rows), rows)
+        return remote(
+            m["kv"].at[at, :], m["kv"].at[at, :], kv_send.at[d - 1], kv_recv.at[d - 1],
+            {"blk": lax.rem(blk + d, nb)},
+        )
+
+    for d in range(1, nb):
+        @pl.when(blk + d < nb)
+        def _(d=d):
+            kv_copy(d).start()
+
+    save("x").start()
+    save("normed").start()
+    save("q").start()
+    wide_lane = lax.broadcasted_iota(jnp.int32, (tk, SLOT), 1)
+    wide_row = lax.broadcasted_iota(jnp.int32, (tk, SLOT), 0)
+
+    def prepare(first):
+        at = pl.ds(pl.multiple_of(first, tk), tk)
+        kv = m["kv"][at, :].astype(f32)
+        dead = jnp.where(wide_row + first < length, 0.0, masked_value)
+        k1[at, :] = jnp.where(
+            wide_lane < HEAD, kv, jnp.where(wide_lane == HEAD, dead, 0.0)
+        ).astype(bf16)
+        vt1[0:HEAD, at] = jnp.transpose(kv)[HEAD:, :].astype(bf16)
+        vt1[HEAD:, at] = jnp.ones((ONES - HEAD, tk), bf16)
+        return at
+
+    def attend(first, q0, diagonal):
+        at = prepare(first)
+        kt, vt = k1[at, :], vt1[:, at]
+        n = rows - q0
+        qs = slice(q0, rows)
+
+        def score(h):
+            s = dot(kt, q1[qs, h * SLOT : (h + 1) * SLOT], NT)
+            if diagonal:
+                ki = lax.broadcasted_iota(jnp.int32, (tk, n), 0)
+                qi = lax.broadcasted_iota(jnp.int32, (tk, n), 1)
+                s = jnp.where(ki <= qi, s, masked_value)
+            return s
+
+        def add(h, p, alpha):
+            acc_s[h, :, qs] = acc_s[h, :, qs] * alpha + dot(vt, p, NN)
+
+        ahead, behind = score(0), None
+        for h in range(heads):
+            s = ahead
+            if h + 1 < heads:
+                ahead = score(h + 1)
+            m_prev = m_s[h : h + 1, qs]
+            m_new = jnp.maximum(m_prev, jnp.max(s, axis=0, keepdims=True))
+            alpha = jnp.exp(m_prev - m_new)
+            p = jnp.exp(s - m_new).astype(bf16)
+            m_s[h : h + 1, qs] = m_new
+            if behind is not None:
+                add(*behind)
+            behind = (h, p, alpha)
+        add(*behind)
+
+    m_s[...] = jnp.full(m_s.shape, masked_value, f32)
+    acc_s[...] = jnp.zeros(acc_s.shape, f32)
+    for e in range(rows // tk):
+        attend(start + e * tk, e * tk, True)
+
+    def block(d, _):
+        src = blk - d
+        at = pl.ds(pl.multiple_of(src * rows, rows), rows)
+        remote(
+            m["kv"].at[at, :], m["kv"].at[at, :], kv_send.at[d - 1], kv_recv.at[d - 1],
+            {"blk": src},
+        ).wait_recv()
+
+        def key_tile(i, _):
+            attend(src * rows + i * tk, 0, False)
+            return 0
+
+        lax.fori_loop(0, rows // tk, key_tile, 0)
         return 0
 
-    lax.fori_loop(0, (blk + 1) * (rows // tk), prepare, 0)
-    one = jnp.where(lax.broadcasted_iota(jnp.int32, (tq, SLOT), 1) == HEAD, 1.0, 0.0)
-
-    def tile(at, masked):
-        kt = k1[at, :]
-        vt = v1[at, :]
-        for h in range(heads):
-            s = dot(q1[:, h * SLOT : (h + 1) * SLOT], kt, NT)
-            if masked is not None:
-                s = jnp.where(masked, s, masked_value)
-            m_prev = m_s[h]
-            m_new = jnp.maximum(m_prev, jnp.max(s, axis=1, keepdims=True))
-            alpha = jnp.exp(m_prev - m_new)
-            p = jnp.exp(s - jnp.concatenate([m_new] * (tk // SLOT), 1))
-            acc_s[h] = acc_s[h] * alpha + dot(p.astype(bf16), vt, NN)
-            m_s[h] = m_new
-
-    def query_tile(qt, _):
-        at_q = pl.ds(qt * tq, tq)
-        for h in range(heads):
-            cols = slice(h * SLOT, (h + 1) * SLOT)
-            q1[:, cols] = (q_ref[at_q, cols].astype(f32) + one).astype(bf16)
-        m_s[...] = jnp.full(m_s.shape, masked_value, f32)
-        acc_s[...] = jnp.zeros(acc_s.shape, f32)
-        full = blk * (rows // tk) + (qt * tq) // tk
-
-        def full_tile(i, _):
-            tile(pl.ds(pl.multiple_of(i * tk, tk), tk), None)
-            return 0
-
-        lax.fori_loop(0, full, full_tile, 0)
-        shift = (qt * tq) % tk
-        ri = lax.broadcasted_iota(jnp.int32, (tq, tk), 0) + shift
-        ci = lax.broadcasted_iota(jnp.int32, (tq, tk), 1)
-        tile(pl.ds(pl.multiple_of(full * tk, tk), tk), ci <= ri)
-        pos = lax.broadcasted_iota(jnp.int32, (1, tq), 1) + blk * rows + qt * tq
-        for h in range(heads):
-            acc = acc_s[h]
-            out = acc / pltpu.roll(acc, HEAD, 1)
-            wide = jnp.where(lax.broadcasted_iota(jnp.int32, (tq, SLOT), 1) < HEAD, 0.0, out)
-            slots_ref[at_q, h * SLOT : (h + 1) * SLOT] = wide.astype(bf16)
-            ctx_ref[at_q, h * HEAD : (h + 1) * HEAD] = wide[:, HEAD:].astype(bf16)
-            lse = jnp.transpose(m_s[h] + jnp.log(acc))[0:1, :]
-            lse_ref[h : h + 1, pl.ds(pl.multiple_of(qt * tq, tq), tq)] = jnp.where(
-                pos < length, lse, -masked_value
-            )
+    lax.fori_loop(1, blk + 1, block, 0)
+    pos = lax.broadcasted_iota(jnp.int32, (1, rows), 1) + start
+    zero = jnp.zeros((HEAD, rows), f32)
+    for h in range(heads):
+        acc = acc_s[h]
+        total = acc[HEAD : HEAD + 1, :]
+        ctx = jnp.transpose(jnp.concatenate([zero, acc[:HEAD] / total], 0))
+        m["slots"][:, h * SLOT : (h + 1) * SLOT] = ctx.astype(bf16)
+        m["ctx"][:, h * HEAD : (h + 1) * HEAD] = ctx[:, HEAD:].astype(bf16)
+        m["lse"][h : h + 1, :] = jnp.where(
+            pos < length, m_s[h : h + 1, :] + jnp.log(total), -masked_value
+        )
+    m["lse"][heads:, :] = jnp.zeros((8 - heads, rows), f32)
+    ctx_swap().start()
+    save("ctx").start()
+    save("slots").start()
+    save("lse").start()
+
+    def kv_save(b):
+        at = pl.ds(pl.multiple_of(b * rows, rows), rows)
+        return pltpu.make_async_copy(
+            m["kv"].at[at, :], out["kv"].at[at, :], out_sem.at[FRONT_OUT.index("kv")]
+        )
+
+    def keep_kv(b, _):
+        kv_save(b).start()
+        kv_save(b).wait()
         return 0
 
-    lax.fori_loop(0, rows // tq, query_tile, 0)
-
-
-def attn_fwd(info, q, kv, heads):
-    rows = q.shape[0]
-    vm = pl.BlockSpec(memory_space=pltpu.VMEM)
-    return pl.pallas_call(
-        functools.partial(attn_fwd_kernel, heads, rows),
-        out_shape=(
-            jax.ShapeDtypeStruct((rows, heads * HEAD), bf16),
-            jax.ShapeDtypeStruct((rows, heads * SLOT), bf16),
-            jax.ShapeDtypeStruct((8, rows), f32),
+    loads[1].wait()
+    cot_swap().wait()
+
+    def mask(r, _):
+        at = pl.ds(pl.multiple_of(r * tile, tile), tile)
+        row = lax.broadcasted_iota(jnp.int32, (tile, width), 0) + start + r * tile
+        m["cot"][at, :] = jnp.where(row < length, m["cot"][at, :].astype(f32), 0.0).astype(bf16)
+        return 0
+
+    lax.fori_loop(0, rows // tile, mask, 0)
+    save("cot").start()
+    lax.fori_loop(0, blk + 1, keep_kv, 0)
+    for d in range(1, nb):
+        @pl.when(blk + d < nb)
+        def _(d=d):
+            kv_copy(d).wait_send()
+
+    ctx_swap().wait()
+    save("ctx_o").start()
+    for name in FRONT_OUT:
+        if name != "kv":
+            save(name).wait()
+
+
+def front(length, values, heads, nb):
+    half, width = values["own_in"].shape
+    rows = 2 * half
+    keys = rows * nb
+    shape = jax.ShapeDtypeStruct
+    outs = dict(
+        x=shape((rows, width), bf16),
+        cot=shape((rows, width), bf16),
+        normed=shape((rows, width), bf16),
+        q=shape((rows, heads * SLOT), bf16),
+        kv=shape((keys, SLOT), bf16),
+        ctx=shape((rows, heads * HEAD), bf16),
+        ctx_o=shape((rows, heads * HEAD), bf16),
+        slots=shape((rows, heads * SLOT), bf16),
+        lse=shape((8, rows), f32),
+    )
+    hbm = pl.BlockSpec(memory_space=pl.ANY)
+    dma = pltpu.SemaphoreType.DMA
+    vm = lambda a: pltpu.VMEM(a.shape, a.dtype)
+    results = pl.pallas_call(
+        functools.partial(front_kernel, heads),
+        out_shape=[outs[name] for name in FRONT_OUT],
+        in_specs=[pl.BlockSpec(memory_space=pltpu.SMEM)] + [hbm] * len(FRONT_IN),
+        out_specs=[hbm] * len(FRONT_OUT),
+        scratch_shapes=[vm(outs[name]) for name in FRONT_OUT]
+        + [vm(values[name]) for name in FRONT_IN[2:]]
+        + [
+            pltpu.VMEM((rows, heads * SLOT), bf16),
+            pltpu.VMEM((keys, SLOT), bf16),
+            pltpu.VMEM((ONES, keys), bf16),
+            pltpu.VMEM((8, rows), f32),
+            pltpu.VMEM((heads, ONES, rows), f32),
+            dma((len(FRONT_IN),)),
+            dma((len(FRONT_OUT),)),
+            dma((3,)),
+            dma((3,)),
+            dma((nb - 1,)),
+            dma((nb - 1,)),
+        ],
+        compiler_params=pltpu.CompilerParams(
+            collective_id=1, has_side_effects=True, vmem_limit_bytes=58 * 2**20
         ),
-        in_specs=[pl.BlockSpec(memory_space=pltpu.SMEM), vm, vm],
-        out_specs=(vm, vm, vm),
-        scratch_shapes=[
-            pltpu.VMEM(kv.shape, bf16),
-            pltpu.VMEM(kv.shape, bf16),
-            pltpu.VMEM((256, heads * SLOT), bf16),
-            pltpu.VMEM((heads, 256, SLOT), f32),
-            pltpu.VMEM((heads, 256, SLOT), f32),
-        ],
-        compiler_params=pltpu.CompilerParams(vmem_limit_bytes=48 * 2**20),
-        name="attn_fwd",
-    )(info, q, kv)
-
-
-def turn(x, cosine, sine_low, sine_high):
-    return (
-        x * cosine + pltpu.roll(x, SLOT - 32, 1) * sine_low + pltpu.roll(x, 32, 1) * sine_high
-    )
+        name="front",
+    )(length, *[values[name] for name in FRONT_IN])
+    return dict(zip(FRONT_OUT, results))
 
 
 PART = 128
@@ -446,13 +594,9 @@
     ]
 
 
-def turn(v, cosine, sine_a, sine_b):
-    return v * cosine + pltpu.roll(v, SLOT - 32, 1) * sine_a - pltpu.roll(v, 32, 1) * sine_b
-
-
 LOADS = (
-    "dmid", "resid", "cot", "w_slots", "ctx", "slots", "q", "kv", "lse",
-    "cosine", "sine_a", "sine_b", "normed", "w_all", "own_in", "gain1", "gain2", "part",
+    "dmid", "resid", "cot", "w_out", "ctx", "slots", "q", "kv", "lse",
+    "table", "normed", "wq", "wk", "wv", "own_in", "gain1", "gain2", "part",
 )
 
 
@@ -467,8 +611,9 @@
     (
         load_sem, dmid_o, part_o, do, dlow, delta, dq, dkv, dkv_o, k0, dproj, small,
         din_send, din_own, din_o, rowsum, vec, pair_send, pair_recv, kv_send, kv_recv, out_sem,
-    ) = refs[:22]
-    refs = refs[22:]
+        w_slots, gain_own, gain_o,
+    ) = refs[:25]
+    refs = refs[25:]
     rows, width = m["cot"].shape
     half = rows // 2
     blk, nb = lax.axis_index("blk"), lax.axis_size("blk")
@@ -494,23 +639,18 @@
     for copy in loads.values():
         copy.start()
 
-    barrier = pltpu.get_barrier_semaphore()
-    peers = [other]
-    peers += [{"blk": lax.rem(blk + d, nb)} for d in range(1, nb)]
     batch = lax.axis_index("batch")
-    peers += [
-        {"batch": batch + (1 - 2 * lax.rem(batch // (1 << b), 2)) * (1 << b)}
-        for b in range(int(math.log2(nz)))
-    ]
-    for peer in peers:
-        pl.semaphore_signal(barrier, 1, device_id=peer, device_id_type=pl.DeviceIdType.MESH)
-    pl.semaphore_wait(barrier, len(peers))
+    meet(
+        [other]
+        + [{"blk": lax.rem(blk + d, nb)} for d in range(1, nb)]
+        + [
+            {"batch": batch + (1 - 2 * lax.rem(batch // (1 << b), 2)) * (1 << b)}
+            for b in range(int(math.log2(nz)))
+        ]
+    )
 
     def swap(k, src, dst):
-        return pltpu.make_async_remote_copy(
-            src_ref=src, dst_ref=dst, send_sem=pair_send.at[k], recv_sem=pair_recv.at[k],
-            device_id=other, device_id_type=pl.DeviceIdType.MESH,
-        )
+        return remote(src, dst, pair_send.at[k], pair_recv.at[k], other)
 
     def dmid_swap():
         return swap(0, hbm["dmid"], dmid_o)
@@ -523,6 +663,9 @@
 
     def din_swap():
         return swap(2, din_send, din_o)
+
+    def gain_swap():
+        return swap(3, gain_own, gain_o)
 
     dmid_swap().start()
     part_swap().start()
@@ -546,6 +689,9 @@
         dmid_swap().wait()
         part_swap().wait()
         vec[...] = jnp.zeros(vec.shape, f32)
+        w_slots[...] = jnp.zeros(w_slots.shape, bf16)
+        for h in range(heads):
+            w_slots[h * SLOT + HEAD : (h + 1) * SLOT, :] = m["w_out"][h * HEAD : (h + 1) * HEAD, :]
 
         def out_rows(r, _):
             at = pl.ds(pl.multiple_of(r * tile, tile), tile)
@@ -572,7 +718,7 @@
             m["resid"][at, :] = d_resid
             low = d_resid.astype(bf16)
             dlow[at, :] = low
-            d_ctx = dot(low, m["w_slots"][...], NT)
+            d_ctx = dot(low, w_slots[...], NT)
             do[at, :] = d_ctx.astype(bf16)
             for h in range(heads):
                 cols = slice(h * SLOT, (h + 1) * SLOT)
@@ -602,21 +748,30 @@
 
     def pair(kt, kvt, qt, masked):
         at = pl.ds(pl.multiple_of(qt * tq, tq), tq)
-        grad = None
+
+        def score(h):
+            cols = slice(h * SLOT, (h + 1) * SLOT)
+            return dot(kt, m["q"][at, cols], NT), dot(kvt, do[at, cols], NT)
+
+        def add(h, p, ds):
+            cols = slice(h * SLOT, (h + 1) * SLOT)
+            dq[at, cols] += dot(ds, kt, TN)
+            return dot(ds, m["q"][at, cols], NN) + dot(p, do[at, cols], NN)
+
+        grad, ahead, behind = None, score(0), None
         for h in range(heads):
-            cols = slice(h * SLOT, (h + 1) * SLOT)
-            q = m["q"][at, cols]
-            d_ctx = do[at, cols]
-            s = dot(kt, q, NT)
+            s, dp = ahead
+            if h + 1 < heads:
+                ahead = score(h + 1)
             p = jnp.exp(s - m["lse"][h : h + 1, at])
             if masked is not None:
                 p = jnp.where(masked, p, 0.0)
-            dp = dot(kvt, d_ctx, NT)
             ds = (p * (dp - delta[h : h + 1, at])).astype(bf16)
-            part = dot(ds, q, NN) + dot(p.astype(bf16), d_ctx, NN)
-            grad = part if grad is None else grad + part
-            dq[at, cols] += dot(ds, kt, TN)
-        return grad
+            if behind is not None:
+                part = add(*behind)
+                grad = part if grad is None else grad + part
+            behind = (h, p.astype(bf16), ds)
+        return grad + add(*behind)
 
     def own_block():
         ki = lax.broadcasted_iota(jnp.int32, (tk, tq), 0)
@@ -653,10 +808,8 @@
     def kv_copy(d):
         to = lax.rem(blk + d, nb)
         at = pl.ds(pl.multiple_of(to * rows, rows), rows)
-        return pltpu.make_async_remote_copy(
-            src_ref=dkv.at[at, :], dst_ref=dkv_o.at[d - 1],
-            send_sem=kv_send.at[d - 1], recv_sem=kv_recv.at[d - 1],
-            device_id={"blk": to}, device_id_type=pl.DeviceIdType.MESH,
+        return remote(
+            dkv.at[at, :], dkv_o.at[d - 1], kv_send.at[d - 1], kv_recv.at[d - 1], {"blk": to}
         )
 
     def kv_start():
@@ -680,21 +833,16 @@
                     dkv[at, :] = total.astype(bf16)
 
         rowsum[...] = jnp.zeros(rowsum.shape, f32)
-        lane = lax.broadcasted_iota(jnp.int32, (tile, SLOT), 1)
 
         def unrotate(r, _):
             at = pl.ds(pl.multiple_of(r * tile, tile), tile)
             at_b = pl.ds(pl.multiple_of(blk * rows + r * tile, tile), tile)
-            table = m["cosine"][at, :], m["sine_a"][at, :], m["sine_b"][at, :]
-            for h in range(heads + 1):
-                cols = slice(h * SLOT, (h + 1) * SLOT)
-                if h < heads:
-                    v = jnp.where(lane < HEAD, turn(dq[at, cols] * HEAD**-0.5, *table), 0.0)
-                else:
-                    v = turn(dkv[at_b, :].astype(f32), *table)
-                low = v.astype(bf16)
-                dproj[at, cols] = low
-                rowsum[0:1, cols] += jnp.sum(low.astype(f32), axis=0, keepdims=True)
+            table = spread_table(m["table"][at, :])
+            for h in range(heads):
+                v = turn(dq[at, h * SLOT : (h + 1) * SLOT] * HEAD**-0.5, table, -1.0)
+                dproj[at, h * HEAD : (h + 1) * HEAD] = v[:, :HEAD].astype(bf16)
+            dproj[at, nq:] = turn(dkv[at_b, :].astype(f32), table, -1.0).astype(bf16)
+            rowsum[0:1, :] += jnp.sum(dproj[at, :].astype(f32), axis=0, keepdims=True)
             return 0
 
         lax.fori_loop(0, rows // tile, unrotate, 0)
@@ -703,7 +851,11 @@
             def step(r, _):
                 src = pl.ds(pl.multiple_of(first + r * tile, tile), tile)
                 at = pl.ds(pl.multiple_of(r * tile, tile), tile)
-                to[at, :] = dot(dproj[src, :], m["w_all"][...], NN).astype(bf16)
+                to[at, :] = (
+                    dot(dproj[src, :nq], m["wq"][...], NT)
+                    + dot(dproj[src, nq : nq + HEAD], m["wk"][...], NT)
+                    + dot(dproj[src, nq + HEAD :], m["wv"][...], NT)
+                ).astype(bf16)
                 return 0
 
             lax.fori_loop(0, half // tile, step, 0)
@@ -714,10 +866,7 @@
 
         def grads(k, _):
             at = pl.ds(pl.multiple_of(k * 128, 128), 128)
-            g = dot(m["normed"][:, at], dproj[...], TN)
-            for h in range(heads):
-                put(nq + h * HEAD, at, g[:, h * SLOT : h * SLOT + HEAD])
-            put(2 * nq, at, g[:, heads * SLOT :])
+            put(nq, at, dot(m["normed"][:, at], dproj[...], TN))
             return 0
 
         lax.fori_loop(0, width // 128, grads, 0)
@@ -742,9 +891,11 @@
 
         lax.fori_loop(0, half // tile, step, 0)
         pltpu.make_async_copy(din_own, input_grad_ref, out_sem.at[1]).start()
-        for h in range(heads):
-            vec[2:3, h * HEAD : (h + 1) * HEAD] = rowsum[0:1, h * SLOT : h * SLOT + HEAD]
-        vec[2:3, nq : nq + SLOT] = rowsum[0:1, heads * SLOT :]
+        gain_own[...] = vec[0:8, :]
+        gain_swap().start()
+        vec[2:3, : nq + SLOT] = rowsum[0:1, :]
+        gain_swap().wait()
+        vec[0:1, :] = gain_own[0:1, :] + gain_o[0:1, :]
         put(2 * nq + SLOT, slice(None), jnp.transpose(vec[...]))
 
     n_attn = 2 + (nb - 1) * (rows // tk)
@@ -801,18 +952,21 @@
         pltpu.VMEM((keys, SLOT), bf16),
         pltpu.VMEM((nb - 1, rows, SLOT), bf16),
         pltpu.VMEM((keys, SLOT), bf16),
-        pltpu.VMEM((rows, (heads + 1) * SLOT), bf16),
+        pltpu.VMEM((rows, heads * HEAD + SLOT), bf16),
         pltpu.VMEM((n_small, width, CHUNK), bf16),
         pltpu.VMEM((half, width), bf16),
         pltpu.VMEM((half, width), bf16),
         pltpu.VMEM((half, width), bf16),
-        pltpu.VMEM((8, (heads + 1) * SLOT), f32),
+        pltpu.VMEM((8, heads * HEAD + SLOT), f32),
         pltpu.VMEM((SLOT, width), f32),
-        dma((3,)),
-        dma((3,)),
+        dma((4,)),
+        dma((4,)),
         dma((nb - 1,)),
         dma((nb - 1,)),
         dma((2,)),
+        pltpu.VMEM((heads * SLOT, width), bf16),
+        pltpu.VMEM((8, width), f32),
+        pltpu.VMEM((8, width), f32),
     ]
     for st in streams:
         scratch += st.scratch()
@@ -833,147 +987,103 @@
     )(*[values[name] for name in LOADS], grads)
 
 
-def spread(weights, heads, first):
-    wide = weights.reshape(heads, HEAD, -1)
-    zeros = jnp.zeros_like(wide)
-    return jnp.concatenate([wide, zeros] if first else [zeros, wide], 1).reshape(heads * SLOT, -1)
-
-
-def rotary(positions):
-    half = HEAD // 2
-    freq = rope_base ** (-(jnp.arange(half, dtype=f32) * 2.0) / HEAD)
-    phase = positions.astype(f32)[:, None] * freq[None, :]
-    cosine, sine = jnp.cos(phase), jnp.sin(phase)
-    return cosine, sine
+def unpack_kernel(heads, n_small, chunk_ref, *refs):
+    small, (down, gate, up, g_out, g_q, g_k, g_v, vec) = refs[:n_small], refs[n_small:]
+    step = pl.program_id(0)
+    value = chunk_ref[0]
+    down[...] = jnp.transpose(value[:, :PART].astype(f32))
+    gate[...] = value[:, PART : 2 * PART].astype(f32)
+    up[...] = value[:, 2 * PART :].astype(f32)
+
+    def take(first, count):
+        done = 0
+        while done < count:
+            c, lane = divmod(first + done, CHUNK)
+            n = min(count - done, SLOT - lane % SLOT)
+            yield done, n, small[c][0, :, lane : lane + n].astype(f32)
+            done += n
+
+    @pl.when(step == 0)
+    def _():
+        nq = heads * HEAD
+        for done, n, piece in take(0, nq):
+            g_out[done : done + n, :] = jnp.transpose(piece)
+        for done, n, piece in take(nq, nq):
+            g_q[:, done : done + n] = piece
+        for done, n, piece in take(2 * nq, HEAD):
+            g_k[...] = piece
+        for done, n, piece in take(2 * nq + HEAD, HEAD):
+            g_v[...] = piece
+        for done, n, piece in take(2 * nq + 2 * HEAD, SLOT):
+            vec[...] = jnp.transpose(piece)[0:8, :]
+
+
+def unpack(sums, n_ffn, heads):
+    n, width, _ = sums.shape
+    n_small = n - n_ffn
+    shape = lambda *dims: jax.ShapeDtypeStruct(dims, f32)
+    nq = heads * HEAD
+    whole = [(nq, width), (width, nq), (width, HEAD), (width, HEAD), (8, width)]
+    return pl.pallas_call(
+        functools.partial(unpack_kernel, heads, n_small),
+        grid=(n_ffn,),
+        out_shape=[
+            shape(n_ffn * PART, width), shape(width, n_ffn * PART), shape(width, n_ffn * PART)
+        ] + [shape(*dims) for dims in whole],
+        in_specs=[pl.BlockSpec((1, width, CHUNK), lambda j: (j, 0, 0))]
+        + [
+            pl.BlockSpec((1, width, CHUNK), lambda j, c=c: (n_ffn + c, 0, 0))
+            for c in range(n_small)
+        ],
+        out_specs=[
+            pl.BlockSpec((PART, width), lambda j: (j, 0)),
+            pl.BlockSpec((width, PART), lambda j: (0, j)),
+            pl.BlockSpec((width, PART), lambda j: (0, j)),
+        ] + [pl.BlockSpec(dims, lambda j: (0, 0)) for dims in whole],
+        compiler_params=pltpu.CompilerParams(
+            vmem_limit_bytes=48 * 2**20, dimension_semantics=("arbitrary",)
+        ),
+        name="unpack",
+    )(*[sums] * (1 + n_small))
 
 
 def shards(
-    layer_in,
-    cotangent,
-    lengths,
-    attn_gain,
-    w_query,
-    query_bias,
-    w_key,
-    key_bias,
-    w_value,
-    value_bias,
-    w_out,
-    mlp_gain,
-    w_gate,
-    w_up,
-    w_down,
+    layer_in, cotangent, lengths, attn_gain, w_query, query_bias, w_key, key_bias, w_value,
+    value_bias, w_out, mlp_gain, w_gate, w_up, w_down,
 ):
-    rows_own, width = layer_in.shape
-    rows = rows_own * lax.axis_size("tensor")
-    blocks = lax.axis_size("blk")
+    half, width = layer_in.shape
+    rows = half * lax.axis_size("tensor")
+    nb = lax.axis_size("blk")
     heads = w_query.shape[1] // HEAD
-    blk = lax.axis_index("blk")
-    core = lax.axis_index("tensor")
-    bucket = rows * blocks
-    length = lengths[0, 0]
-    info = jnp.stack([blk.astype(jnp.int32), length])
-    start = blk * rows
-    own_start = core * rows_own
-
-    x_low = gather_pair(layer_in, "tensor", 0)
-    x = x_low.astype(f32)
-    cot = gather_pair(cotangent, "tensor", 0)
-    positions = start + jnp.arange(rows, dtype=jnp.int32)
-    live = positions % bucket < length
-    cot = jnp.where(live[:, None], cot, 0)
-
-    cosine, sine = rotary(positions)
-    zero32 = jnp.zeros_like(sine)
-    fill = jnp.ones((rows, HEAD), f32)
-    cos_w = jnp.concatenate([cosine, cosine, fill], 1)
-    sin_a = jnp.concatenate([sine, zero32, zero32, zero32], 1)
-    sin_b = jnp.concatenate([zero32, sine, zero32, zero32], 1)
-    slots_n = heads + 1
-    w_all = jnp.concatenate(
-        [spread(w_query.T, heads, True), w_key.T, w_value.T], 0
+    tables = jnp.asarray(rotary_table(rows * nb)).reshape(nb, rows, HEAD)
+    table = lax.dynamic_index_in_dim(tables, lax.axis_index("blk"), 0, keepdims=False)
+    inputs = dict(
+        own_in=layer_in, own_cot=cotangent, wq=w_query, wk=w_key, wv=w_value,
+        bq=query_bias[None, :], bk=key_bias[None, :], bv=value_bias[None, :],
+        gain=attn_gain[None, :], table=table,
     )
-    b_all = jnp.concatenate(
-        [
-            spread(query_bias[:, None], heads, True)[:, 0],
-            key_bias,
-            value_bias,
-        ]
-    ).astype(f32)
-
-    def rotate(v, sign):
-        v = v.reshape(rows, slots_n, SLOT)
-        up = jnp.roll(v, -32, axis=2)
-        down = jnp.roll(v, 32, axis=2)
-        out = (
-            v * cos_w[:, None, :]
-            - sign * up * sin_a[:, None, :]
-            + sign * down * sin_b[:, None, :]
-        )
-        return out.reshape(rows, slots_n * SLOT)
-
-    rho1 = lax.rsqrt(jnp.mean(x * x, axis=1, keepdims=True) + norm_eps)
-    n1 = x * rho1
-    normed_in = (n1 * attn_gain).astype(bf16)
-    proj = rotate(contract_cols(normed_in, w_all) + b_all, 1.0)
-    q_low = (proj[:, : heads * SLOT].astype(bf16) * HEAD**-0.5).astype(bf16)
-    kv = proj[:, heads * SLOT :].astype(bf16)
-    for axis, bit in bits_of("blk"):
-        kv = gather_pair(kv, axis, bit)
-    ctx, ctx_slots, lse = attn_fwd(info, q_low, kv, heads)
-
-    ctx_other = partner(ctx, "tensor", 0)
-    w_out_other = partner(w_out, "tensor", 0)
+    w_out_o = lax.ppermute(w_out, "tensor", [(0, 1), (1, 0)])
+    mid = front(lengths, inputs, heads, nb)
     resid, grads, dmid, part = feed_forward(
-        x_low, ctx, ctx_other, w_out, w_out_other, mlp_gain[None, :], cot, w_gate, w_up, w_down
+        mid["x"], mid["ctx"], mid["ctx_o"], w_out, w_out_o, mlp_gain[None, :], mid["cot"],
+        w_gate, w_up, w_down,
     )
     values = dict(
-        dmid=dmid,
-        resid=resid,
-        cot=cot,
-        w_slots=spread(w_out, heads, False),
-        ctx=ctx,
-        slots=ctx_slots,
-        q=q_low,
-        kv=kv,
-        lse=lse,
-        cosine=cos_w,
-        sine_a=sin_a,
-        sine_b=sin_b,
-        normed=normed_in,
-        w_all=w_all,
-        own_in=layer_in,
-        gain1=attn_gain[None, :],
-        gain2=mlp_gain[None, :],
-        part=part,
+        dmid=dmid, resid=resid, w_out=w_out, table=table, wq=w_query, wk=w_key, wv=w_value,
+        own_in=layer_in, gain1=attn_gain[None, :], gain2=mlp_gain[None, :], part=part,
     )
+    for name in ("cot", "ctx", "slots", "q", "kv", "lse", "normed"):
+        values[name] = mid[name]
     sums, layer_out, input_grad = backward(
-        values, grads, heads, bits_of("blk"), bits_of("batch"), blocks
+        values, grads, heads, bits_of("blk"), bits_of("batch"), nb
     )
-    n_ffn = grads.shape[0]
-    ffn = sums[:n_ffn].astype(f32)
-    grad_down = ffn[:, :, :PART].transpose(0, 2, 1).reshape(n_ffn * PART, width)
-    grad_gate = ffn[:, :, PART : 2 * PART].transpose(1, 0, 2).reshape(width, n_ffn * PART)
-    grad_up = ffn[:, :, 2 * PART :].transpose(1, 0, 2).reshape(width, n_ffn * PART)
-    small = sums[n_ffn:].transpose(1, 0, 2).reshape(width, -1).astype(f32)
+    g_down, g_gate, g_up, g_out, g_query, g_key, g_value, vec = unpack(
+        sums, grads.shape[0], heads
+    )
     nq = heads * HEAD
-    vec = small[:, 2 * nq + SLOT : 2 * nq + SLOT + 3].T
-    gain = vec[0] + partner(vec[0], "tensor", 0)
     return (
-        layer_out,
-        input_grad,
-        gain,
-        small[:, nq : 2 * nq],
-        vec[2, :nq],
-        small[:, 2 * nq : 2 * nq + HEAD],
-        vec[2, nq : nq + HEAD],
-        small[:, 2 * nq + HEAD : 2 * nq + 2 * HEAD],
-        vec[2, nq + HEAD : nq + 2 * HEAD],
-        small[:, :nq].T,
-        vec[1],
-        grad_gate,
-        grad_up,
-        grad_down,
+        layer_out, input_grad, vec[0], g_query, vec[2, :nq], g_key, vec[2, nq : nq + HEAD],
+        g_value, vec[2, nq + HEAD : nq + 2 * HEAD], g_out, vec[1], g_gate, g_up, g_down,
     )
 
 

time: 652 us -> 469 us (0.72)
  local copies, waits for them, and re-layouts: 113 us -> 20.4 us
  other arithmetic: 48.5 us -> 0 us
  waiting for transfers between devices: 16.5 us -> 0.01 us
  Pallas kernels: 459 us -> 446 us
    transpose x6 -> x0, local copies, waits for them, and re-layouts: 54.2 us -> none  [the longest x2 28.5 us: shards(): grad_down = ffn[:, :, :PART].transpose(0, 2, 1).reshape(n_ffn * PART, width)]
    pallas_call x1, Pallas kernels: 357 us -> 321 us  [backward(): pl.pallas_call(functools.partial(backward_kernel, heads, streams, n_ffn,...]
    pallas_call x1 -> x2, Pallas kernels: 18.7 us -> 42.4 us  [the longest x1 21.7 us: front(): pl.pallas_call(functools.partial(front_kernel, heads), out_shape=[outs[na...]
    convert_element_type x5 -> x0, other arithmetic: 20.1 us -> none  [the longest x1 14.9 us: shards(): ffn = sums[:n_ffn].astype(f32)]
    unnamed x45 -> x12, local copies, waits for them, and re-layouts: 29.6 us -> 13 us
    ppermute x7 -> x1, waiting for transfers between devices: 16.5 us -> 0.01 us  [shards(): w_out_o = lax.ppermute(w_out, 'tensor', [(0, 1), (1, 0)])]
    slice x4 -> x0, local copies, waits for them, and re-layouts: 10.9 us -> none  [the longest x2 8.06 us: rotate(): up = jnp.roll(v, -32, axis=2)]
    mul x2 -> x0, other arithmetic: 7.77 us -> none  [the longest x1 6.09 us: rotate(): sign * up * sin_a[:, None, :]]
  transfers between devices with their start and end apart: 7 -> 1, of which waited for: 2 -> 0; matrix products, arithmetic and copies ran while one was open for 15% -> 2% of each run, Pallas kernels for 3% -> 5%
where the time goes in v3:
time: 469 us; the launch traced here: 468 us
  Pallas kernels  446 us (95%)
  local copies, waits for them, and re-layouts  20.4 us (4%)
    pallas_call x1, Pallas kernels, backward(): pl.pallas_call(functools.partial(backward_kernel, heads, streams, n_ffn,...  321 us
    pallas_call x1, Pallas kernels, feed_forward(): pl.pallas_call(ffn_kernel, grid=(steps,), out_shape=(jax.ShapeDtypeStruct...  83.1 us
    pallas_call x1, Pallas kernels, front(): pl.pallas_call(functools.partial(front_kernel, heads), out_shape=[outs[na...  21.7 us
    pallas_call x1, Pallas kernels, unpack(): pl.pallas_call(functools.partial(unpack_kernel, heads, n_small), grid=(n_...  20.7 us
    unnamed x12, local copies, waits for them, and re-layouts  13 us
  transfers between devices with their start and end apart: 1, of which 0 were waited for; matrix products, arithmetic and copies ran while one was open for 2% of the time, Pallas kernels for 5%

profile of v3, /device:TPU:0, one launch (start us, length us, event | category | flops | bytes accessed | tf_op | source)
XLA Modules:
  0.0 468.3 jit_solution(6006819893501248866)
XLA Ops:
  0.6 0.5 collective-permute-start
  1.8 1.3 broadcast_in_dim.17.refs_5_
  3.1 1.3 broadcast_in_dim.20.refs_8_.refs_15_
  4.3 1.3 broadcast_in_dim.21.gain_ref.refs_16_
  5.6 1.7 copy.31.refs_3_.refs_12_
  7.3 1.7 copy.32.refs_4_.refs_13_
  9.1 2.2 copy.30.refs_2_.refs_11_
  11.3 1.9 dynamic-slice_bitcast_fusion.refs_9_
  13.1 21.7 %front.1 = (bf16[1024,896]{1,0:T(8,128)(2,1)}, bf16[1024,896]{1,0:T(8,128)(2,1)}, bf16[1024,896]{1,0:T(8,128)(2,1)}, bf16[1024,896]{1,0:T(8,128)(2,1)}, bf16[409...) custom-call(s32[1,1]{1,0:T(1,128)S(6)} %copy.41.length_ref, ...), custom_call_target="tpu_custom_call" | custom-call | tf_op jit(solution)/shard_map/front/pallas_call | solution.py:320
  34.9 0.0 collective-permute-done.wo_o_ref
  34.9 0.0 copy-start.1
  34.9 0.9 copy-done.1
  35.8 83.1 %ffn.1 = (f32[1024,896]{1,0:T(8,128)}, bf16[19,896,384]{2,1,0:T(8,128)(2,1)}, bf16[1024,896]{1,0:T(8,128)(2,1)}, bf16[1024,896]{1,0:T(8,128)(2,1)}) custom-call(bf16[1024,896]{1,0:T(8,128)(2,1)} %get-tuple-element.38.x_ref, bf16[1024,448]{1,0:T(8,128)(2,1)} %get-tuple-element.39.ctx_ref.refs_4_, bf16[1024,448]{1,0:T(8,128)(2,1)} %get-tuple-element.40.ctx_o_ref, ...), custom_call_target="tpu_custom_call" | custom-call | tf_op jit(solution)/shard_map/ffn/pallas_call | solution.py:412
  118.8 320.5 %backward.1 = (bf16[22,896,384]{2,1,0:T(8,128)(2,1)}, bf16[512,896]{1,0:T(8,128)(2,1)}, bf16[512,896]{1,0:T(8,128)(2,1)}) custom-call(bf16[1024,896]{1,0:T(8,128)(2,1)} %get-tuple-element.42.refs_0_, f32[1024,896]{1,0:T(8,128)} %get-tuple-element.43.refs_1_, bf16[1024,896]{1,0:T(8,128)(2,1)} %get-tuple-element.41.cot_ref.refs_2_, bf16[448,896]{1,0:T(8,128)(2,1)} %refs_3_.2, ...), custom_call_target="tpu_custom_call" | custom-call | tf_op jit(solution)/shard_map/backward/pallas_call | solution.py:973
  439.4 20.7 %unpack.1 = (f32[2432,896]{1,0:T(8,128)}, f32[896,2432]{1,0:T(8,128)}, f32[896,2432]{1,0:T(8,128)}, f32[448,896]{1,0:T(8,128)}, f32[896,448]{1,0:T(8,128)S(1)}, ...) custom-call(bf16[22,896,384]{2,1,0:T(8,128)(2,1)} %get-tuple-element.53.chunk_ref.refs_0_.refs_1_.refs_2_, ...), custom_call_target="tpu_custom_call" | custom-call | tf_op jit(solution)/shard_map/unpack/pallas_call | solution.py:1027
  460.1 0.6 slice_bitcast_fusion
  460.7 0.6 slice.16
  461.3 0.6 slice_reduce_fusion
  461.9 1.6 copy.36
  463.5 0.0 copy-start
  463.5 0.9 copy.37
  464.4 0.9 copy.38
  465.2 2.2 copy.42
  467.4 0.0 copy-done
  467.4 0.9 copy.43
Async XLA Ops:
  0.6 34.2 %collective-permute-start = (bf16[448,896]{1,0:T(8,128)(2,1)}, bf16[448,896]{1,0:T(8,128)(2,1)S(1)}, u32[]{:S(2)}, u32[]{:S(2)}) collective-permute-start(bf16[448,896]{1,0:T(8,128)(2,1)} %refs_3_.2), channel_id=1, source_target_pairs={{0,1},{1,0},{2,3},{3,2},{4,5},{5,4},{6,7},{7,6},{8,9},{9,8},{10,11... | collective-permute-start | bytes 2408456 | tf_op jit(solution)/shard_map/ppermute | solution.py:1065
  34.9 0.9 copy-start.1
  463.5 3.9 copy-start

commit v4 on v3

v4 whole, which is shorter than its diff:
```python
import functools
import math

import jax
import jax.numpy as jnp
import numpy as np
from jax import lax
from jax.experimental import pallas as pl
from jax.experimental.pallas import tpu as pltpu
from jax.sharding import PartitionSpec as P

HEAD = 64
SLOT = 128

rope_base = 1000000.0
norm_eps = 1e-06
masked_value = -1e30
bf16 = jnp.bfloat16
f32 = jnp.float32


def dot(left, right, dims, kind=f32):
    return lax.dot_general(left, right, (dims, ((), ())), preferred_element_type=kind)


NN = ((1,), (0,))
NT = ((1,), (1,))
TN = ((0,), (0,))


def bits_of(mesh_axis):
    return [(mesh_axis, bit) for bit in range(int(math.log2(lax.axis_size(mesh_axis))))]


def rotary_table(count):
    half = HEAD // 2
    freq = np.float32(rope_base) ** (-(np.arange(half, dtype=np.float32) * np.float32(2.0)) / np.float32(HEAD))
    phase = np.arange(count, dtype=np.float32)[:, None] * freq[None, :].astype(np.float32)
    phase = phase.astype(np.float64)
    return np.concatenate([np.cos(phase), np.sin(phase)], 1).astype(np.float32)


def spread_table(table):
    n = table.shape[0]
    wide = jnp.concatenate([table, jnp.zeros_like(table)], 1)
    lane = lax.broadcasted_iota(jnp.int32, (n, SLOT), 1)
    cosine = jnp.where(lane < 32, wide, jnp.where(lane < HEAD, pltpu.roll(wide, 32, 1), 1.0))
    sine_a = jnp.where(lane < 32, pltpu.roll(wide, SLOT - 32, 1), 0.0)
    sine_b = jnp.where((lane >= 32) & (lane < HEAD), wide, 0.0)
    return cosine, sine_a, sine_b


def turn(v, table, sign):
    cosine, sine_a, sine_b = table
    return v * cosine + sign * (
        pltpu.roll(v, 32, 1) * sine_b - pltpu.roll(v, SLOT - 32, 1) * sine_a
    )


def meet(peers):
    barrier = pltpu.get_barrier_semaphore()
    for peer in peers:
        pl.semaphore_signal(barrier, 1, device_id=peer, device_id_type=pl.DeviceIdType.MESH)
    pl.semaphore_wait(barrier, len(peers))


def remote(src, dst, send, recv, peer):
    return pltpu.make_async_remote_copy(
        src_ref=src, dst_ref=dst, send_sem=send, recv_sem=recv,
        device_id=peer, device_id_type=pl.DeviceIdType.MESH,
    )


ONES = 72
FRONT_IN = ("own_in", "own_cot", "wq", "wk", "wv", "w_out", "gain1", "bias", "table")
FRONT_OUT = ("cot", "normed", "q", "kv", "ctx", "lse", "resid")


def row_of(ref, count):
    parts = [ref[i : i + 1, :] for i in range(-(-count // 128))]
    return jnp.concatenate(parts, 1)[:, :count]


def weight_copies(hbm, dst, sems, first, blk):
    rows = dst["table"].shape[0]
    nq = hbm["wq"].shape[0]
    nk = hbm["wk"].shape[0]
    parts = [
        (hbm["wq"], dst["w_qkv"].at[0:nq, :]),
        (hbm["wk"], dst["w_qkv"].at[nq : nq + nk, :]),
        (hbm["wv"], dst["w_qkv"].at[nq + nk : nq + 2 * nk, :]),
        (hbm["table"].at[pl.ds(pl.multiple_of(blk * rows, rows), rows), :], dst["table"]),
    ]
    return [
        pltpu.make_async_copy(src, to, sems.at[first + i]) for i, (src, to) in enumerate(parts)
    ]


def front_kernel(heads, length_ref, *refs):
    ni, no = len(FRONT_IN), len(FRONT_OUT)
    hbm = dict(zip(FRONT_IN, refs[:ni]))
    out = dict(zip(FRONT_OUT, refs[ni : ni + no]))
    m = dict(zip(FRONT_OUT, refs[ni + no : ni + 2 * no]))
    (
        x, ctx_o, w_qkv, w_out, w_out_o, gain, bias, gain_rows, bias_rows, table, q1, k1, vt1, m_s, acc_s,
        load_sem, out_sem, pair_send, pair_recv, kv_send, kv_recv,
    ) = refs[ni + 2 * no :]
    rows, width = m["cot"].shape
    half = rows // 2
    blk, nb = lax.axis_index("blk"), lax.axis_size("blk")
    core = lax.axis_index("tensor")
    other = {"tensor": 1 - core}
    ours = pl.multiple_of(core * half, 16)
    theirs = pl.multiple_of((1 - core) * half, 16)
    start = blk * rows
    length = length_ref[0, 0]
    tile, tk = 256, 512

    loads = [
        pltpu.make_async_copy(hbm["own_in"], x.at[pl.ds(ours, half), :], load_sem.at[0]),
        pltpu.make_async_copy(hbm["own_cot"], m["cot"].at[pl.ds(ours, half), :], load_sem.at[1]),
        pltpu.make_async_copy(hbm["w_out"], w_out, load_sem.at[2]),
        pltpu.make_async_copy(hbm["gain1"], gain_rows, load_sem.at[3]),
        pltpu.make_async_copy(hbm["bias"], bias_rows, load_sem.at[4]),
    ] + weight_copies(hbm, dict(w_qkv=w_qkv, table=table), load_sem, 5, blk)
    for copy in loads:
        copy.start()
    meet([other] + [{"blk": lax.rem(blk + d, nb)} for d in range(1, nb)])

    def swap(k, src, dst):
        return remote(src, dst, pair_send.at[k], pair_recv.at[k], other)

    def x_swap():
        return swap(0, hbm["own_in"], x.at[pl.ds(ours, half), :])

    def cot_swap():
        return swap(1, hbm["own_cot"], m["cot"].at[pl.ds(ours, half), :])

    def ctx_swap():
        return swap(2, m["ctx"], ctx_o)

    def out_swap():
        return swap(3, hbm["w_out"], w_out_o)

    def save(name):
        i = FRONT_OUT.index(name)
        return pltpu.make_async_copy(m[name], out[name], out_sem.at[i])

    x_swap().start()
    cot_swap().start()
    out_swap().start()
    loads[0].wait()
    for copy in loads[2:]:
        copy.wait()
    nq = heads * HEAD
    gain[...] = row_of(gain_rows, width)
    bias[...] = row_of(bias_rows, nq + SLOT)
    lane = lax.broadcasted_iota(jnp.int32, (tile, SLOT), 1)

    def rows_in(first):
        def step(r, _):
            at = pl.ds(pl.multiple_of(first + r * tile, tile), tile)
            own = x[at, :].astype(f32)
            rho = lax.rsqrt(jnp.mean(own * own, axis=1, keepdims=True) + norm_eps)
            normed = (own * rho * gain[...]).astype(bf16)
            m["normed"][at, :] = normed
            factors = spread_table(table[at, :])
            proj = dot(normed, w_qkv[...], NT) + bias[...]
            zero = jnp.zeros((tile, HEAD), f32)
            for h in range(heads):
                cols = slice(h * SLOT, (h + 1) * SLOT)
                v = jnp.concatenate([proj[:, h * HEAD : (h + 1) * HEAD], zero], 1)
                v = turn(v, factors, 1.0).astype(bf16).astype(f32) * HEAD**-0.5
                m["q"][at, cols] = v.astype(bf16)
                q1[at, cols] = jnp.where(lane == HEAD, 1.0, v).astype(bf16)
            at_b = pl.ds(pl.multiple_of(start + first + r * tile, tile), tile)
            m["kv"][at_b, :] = turn(proj[:, nq:], factors, 1.0).astype(bf16)
            return 0

        lax.fori_loop(0, half // tile, step, 0)

    rows_in(ours)
    x_swap().wait()
    rows_in(theirs)

    def kv_copy(d):
        at = pl.ds(pl.multiple_of(blk * rows, rows), rows)
        return remote(
            m["kv"].at[at, :], m["kv"].at[at, :], kv_send.at[d - 1], kv_recv.at[d - 1],
            {"blk": lax.rem(blk + d, nb)},
        )

    for d in range(1, nb):
        @pl.when(blk + d < nb)
        def _(d=d):
            kv_copy(d).start()

    save("normed").start()
    save("q").start()
    wide_lane = lax.broadcasted_iota(jnp.int32, (tk, SLOT), 1)
    wide_row = lax.broadcasted_iota(jnp.int32, (tk, SLOT), 0)

    def prepare(first):
        at = pl.ds(pl.multiple_of(first, tk), tk)
        kv = m["kv"][at, :].astype(f32)
        dead = jnp.where(wide_row + first < length, 0.0, masked_value)
        k1[at, :] = jnp.where(
            wide_lane < HEAD, kv, jnp.where(wide_lane == HEAD, dead, 0.0)
        ).astype(bf16)
        vt1[0:HEAD, at] = jnp.transpose(kv)[HEAD:, :].astype(bf16)
        vt1[HEAD:, at] = jnp.ones((ONES - HEAD, tk), bf16)
        return at

    def attend(first, q0, diagonal):
        at = prepare(first)
        kt, vt = k1[at, :], vt1[:, at]
        n = rows - q0
        qs = slice(q0, rows)

        def score(h):
            s = dot(kt, q1[qs, h * SLOT : (h + 1) * SLOT], NT)
            if diagonal:
                ki = lax.broadcasted_iota(jnp.int32, (tk, n), 0)
                qi = lax.broadcasted_iota(jnp.int32, (tk, n), 1)
                s = jnp.where(ki <= qi, s, masked_value)
            return s

        def add(h, p, alpha):
            acc_s[h, :, qs] = acc_s[h, :, qs] * alpha + dot(vt, p, NN)

        ahead, behind = score(0), None
        for h in range(heads):
            s = ahead
            if h + 1 < heads:
                ahead = score(h + 1)
            m_prev = m_s[h : h + 1, qs]
            m_new = jnp.maximum(m_prev, jnp.max(s, axis=0, keepdims=True))
            alpha = jnp.exp(m_prev - m_new)
            p = jnp.exp(s - m_new).astype(bf16)
            m_s[h : h + 1, qs] = m_new
            if behind is not None:
                add(*behind)
            behind = (h, p, alpha)
        add(*behind)

    m_s[...] = jnp.full(m_s.shape, masked_value, f32)
    acc_s[...] = jnp.zeros(acc_s.shape, f32)
    for e in range(rows // tk):
        attend(start + e * tk, e * tk, True)

    def block(d, _):
        src = blk - d
        at = pl.ds(pl.multiple_of(src * rows, rows), rows)
        remote(
            m["kv"].at[at, :], m["kv"].at[at, :], kv_send.at[d - 1], kv_recv.at[d - 1],
            {"blk": src},
        ).wait_recv()

        def key_tile(i, _):
            attend(src * rows + i * tk, 0, False)
            return 0

        lax.fori_loop(0, rows // tk, key_tile, 0)
        return 0

    lax.fori_loop(1, blk + 1, block, 0)
    pos = lax.broadcasted_iota(jnp.int32, (1, rows), 1) + start
    zero = jnp.zeros((HEAD, rows), f32)
    for h in range(heads):
        acc = acc_s[h]
        total = acc[HEAD : HEAD + 1, :]
        ctx = jnp.transpose(jnp.concatenate([acc[:HEAD] / total, zero], 0))
        m["ctx"][:, h * HEAD : (h + 1) * HEAD] = ctx[:, :HEAD].astype(bf16)
        m["lse"][h : h + 1, :] = jnp.where(
            pos < length, m_s[h : h + 1, :] + jnp.log(total), -masked_value
        )
    m["lse"][heads:, :] = jnp.zeros((8 - heads, rows), f32)
    ctx_swap().start()
    save("ctx").start()
    save("lse").start()

    def kv_save(b):
        at = pl.ds(pl.multiple_of(b * rows, rows), rows)
        return pltpu.make_async_copy(
            m["kv"].at[at, :], out["kv"].at[at, :], out_sem.at[FRONT_OUT.index("kv")]
        )

    def keep_kv(b, _):
        kv_save(b).start()
        kv_save(b).wait()
        return 0

    loads[1].wait()
    cot_swap().wait()

    def mask(r, _):
        at = pl.ds(pl.multiple_of(r * tile, tile), tile)
        row = lax.broadcasted_iota(jnp.int32, (tile, width), 0) + start + r * tile
        m["cot"][at, :] = jnp.where(row < length, m["cot"][at, :].astype(f32), 0.0).astype(bf16)
        return 0

    lax.fori_loop(0, rows // tile, mask, 0)
    save("cot").start()
    lax.fori_loop(0, blk + 1, keep_kv, 0)
    for d in range(1, nb):
        @pl.when(blk + d < nb)
        def _(d=d):
            kv_copy(d).wait_send()

    out_swap().wait()
    ctx_swap().wait()

    def out_rows(r, _):
        at = pl.ds(pl.multiple_of(r * tile, tile), tile)
        m["resid"][at, :] = (
            x[at, :].astype(f32)
            + dot(m["ctx"][at, :], w_out[...], NN)
            + dot(ctx_o[at, :], w_out_o[...], NN)
        )
        return 0

    lax.fori_loop(0, rows // tile, out_rows, 0)
    save("resid").start()
    for name in FRONT_OUT:
        if name != "kv":
            save(name).wait()


def front(length, values, heads, nb):
    half, width = values["own_in"].shape
    rows = 2 * half
    keys = rows * nb
    shape = jax.ShapeDtypeStruct
    outs = dict(
        cot=shape((rows, width), bf16),
        normed=shape((rows, width), bf16),
        q=shape((rows, heads * SLOT), bf16),
        kv=shape((keys, SLOT), bf16),
        ctx=shape((rows, heads * HEAD), bf16),
        lse=shape((8, rows), f32),
        resid=shape((rows, width), f32),
    )
    hbm = pl.BlockSpec(memory_space=pl.ANY)
    dma = pltpu.SemaphoreType.DMA
    vm = lambda a: pltpu.VMEM(a.shape, a.dtype)
    results = pl.pallas_call(
        functools.partial(front_kernel, heads),
        out_shape=[outs[name] for name in FRONT_OUT],
        in_specs=[pl.BlockSpec(memory_space=pltpu.SMEM)] + [hbm] * len(FRONT_IN),
        out_specs=[hbm] * len(FRONT_OUT),
        scratch_shapes=[vm(outs[name]) for name in FRONT_OUT]
        + [
            pltpu.VMEM((rows, width), bf16),
            pltpu.VMEM((rows, heads * HEAD), bf16),
            pltpu.VMEM((heads * HEAD + SLOT, width), bf16),
            vm(values["w_out"]),
            vm(values["w_out"]),
            pltpu.VMEM((1, width), f32),
            pltpu.VMEM((1, heads * HEAD + SLOT), f32),
            vm(values["gain1"]),
            vm(values["bias"]),
            pltpu.VMEM((rows, HEAD), f32),
            pltpu.VMEM((rows, heads * SLOT), bf16),
            pltpu.VMEM((keys, SLOT), bf16),
            pltpu.VMEM((ONES, keys), bf16),
            pltpu.VMEM((8, rows), f32),
            pltpu.VMEM((heads, ONES, rows), f32),
            dma((9,)),
            dma((len(FRONT_OUT),)),
            dma((4,)),
            dma((4,)),
            dma((nb - 1,)),
            dma((nb - 1,)),
        ],
        compiler_params=pltpu.CompilerParams(
            collective_id=1, has_side_effects=True, vmem_limit_bytes=58 * 2**20
        ),
        name="front",
    )(length, *[values[name] for name in FRONT_IN])
    return dict(zip(FRONT_OUT, results))


PART = 128
RING = 4
CHUNK = 3 * PART


class Stream:
    def __init__(self, first, count, axes):
        self.first, self.count = first, count
        self.reduce, self.sizes = [], []
        size = count
        for axis, bit in axes:
            if bit == "line":
                kinds = [("up", axis, 0), ("middle", axis, None), ("down", axis, 0)]
            elif size % 32 == 0 and size >= 64:
                kinds = [("half", axis, bit)]
                size //= 2
            else:
                kinds = [("full", axis, bit)]
            self.reduce += kinds
            self.sizes += [size] * len(kinds)
        self.gather = [(axis, bit) for kind, axis, bit in reversed(self.reduce) if kind == "half"]
        self.stages = len(self.reduce) + len(self.gather) + 1

    def scratch(self):
        copies = len(self.reduce) + len(self.gather)
        return [pltpu.VMEM((RING, self.sizes[0], CHUNK), bf16)] + [
            pltpu.VMEM((RING, size, CHUNK), bf16) for size in self.sizes
        ] + [
            pltpu.SemaphoreType.DMA((copies, RING)),
            pltpu.SemaphoreType.DMA((copies, RING)),
            pltpu.SemaphoreType.DMA((2, RING)),
        ]

    def bind(self, refs, sources, out):
        n = len(self.reduce)
        self.keep, self.got = refs[0], refs[1 : n + 1]
        self.send, self.recv, self.local = refs[n + 1 :]
        self.sources, self.out = sources, out
        self.peer, self.mine, offset = [], [], self.first
        self.sends, self.gets = [], []
        self.offsets = []
        for (kind, axis, bit), size in zip(self.reduce, self.sizes):
            at = lax.axis_index(axis)
            if kind == "middle":
                self.peer.append({axis: 3 - at})
            else:
                one = lax.rem(at // (1 << bit), 2)
                self.peer.append({axis: at + (1 - 2 * one) * (1 << bit)})
            middle = (at + 1) // 2 == 1
            self.middle = middle
            sends = {"up": jnp.logical_not(middle), "middle": middle, "down": middle}
            gets = {"up": middle, "middle": middle, "down": jnp.logical_not(middle)}
            self.sends.append(sends.get(kind))
            self.gets.append(gets.get(kind))
            self.mine.append(one if kind == "half" else 0)
            offset = offset + one * size if kind == "half" else offset
            self.offsets.append(offset)
        self.whole = []
        offset, size = self.offsets[-1], self.sizes[-1]
        self.gather_peer = []
        for k in reversed(range(n)):
            if self.reduce[k][0] == "half":
                self.whole.append((offset, size))
                self.gather_peer.append(self.peer[k])
                offset, size = offset - self.mine[k] * size, 2 * size

    def copy(self, k, ring, src, dst, peer):
        return pltpu.make_async_remote_copy(
            src_ref=src,
            dst_ref=dst,
            send_sem=self.send.at[k, ring],
            recv_sem=self.recv.at[k, ring],
            device_id=peer,
            device_id_type=pl.DeviceIdType.MESH,
        )

    def start_first(self, ring, source):
        size, one = self.sizes[0], self.mine[0]
        theirs = pl.multiple_of(self.first + (1 - one) * size, 16)
        own = pl.multiple_of(self.first + one * size, 16)
        self.copy(
            0, ring, source.at[pl.ds(theirs, size), :], self.got[0].at[ring], self.peer[0]
        ).start()
        pltpu.make_async_copy(
            source.at[pl.ds(own, size), :], self.keep.at[ring], self.local.at[0, ring]
        ).start()

    def reduce_copy(self, k, ring):
        if k == 0:
            src = self.keep.at[ring]
        elif self.reduce[k][0] == "half":
            size = self.sizes[k]
            theirs = pl.multiple_of((1 - self.mine[k]) * size, 16)
            src = self.got[k - 1].at[ring, pl.ds(theirs, size), :]
        else:
            src = self.got[k - 1].at[ring]
        return self.copy(k, ring, src, self.got[k].at[ring], self.peer[k])

    def gather_copy(self, t, ring, chunk):
        offset, size = self.whole[t]
        rows = pl.ds(pl.multiple_of(offset, 16), size)
        place = self.out.at[chunk, rows, :]
        src = self.got[-1].at[ring] if t == 0 else place
        return self.copy(len(self.reduce) + t, ring, src, place, self.gather_peer[t])

    def own_copy(self, ring, chunk):
        offset, size = self.whole[0]
        rows = pl.ds(pl.multiple_of(offset, 16), size)
        return pltpu.make_async_copy(
            self.got[-1].at[ring], self.out.at[chunk, rows, :], self.local.at[1, ring]
        )

    def stage(self, s, turn, chunk):
        ring = lax.rem(turn, RING)
        n = len(self.reduce)
        if s == 0:
            base = 0
            for count, place in self.sources:
                @pl.when((chunk >= base) & (chunk < base + count))
                def _(base=base, place=place):
                    self.start_first(ring, place(chunk - base))

                base += count
            return
        if s <= n:
            k = s - 1
            if k == 0:
                pltpu.make_async_copy(
                    self.got[0].at[ring], self.keep.at[ring], self.local.at[0, ring]
                ).wait()
            kind, size = self.reduce[k][0], self.sizes[k]
            copy = self.reduce_copy(k, ring)
            if kind in ("half", "full"):
                copy.wait()
                if k == 0:
                    own = self.keep[ring]
                elif kind == "half":
                    rows = pl.ds(pl.multiple_of(self.mine[k] * size, 16), size)
                    own = self.got[k - 1][ring, rows, :]
                else:
                    own = self.got[k - 1][ring]
                total = own.astype(f32) + self.got[k][ring].astype(f32)
                self.got[k][ring] = total.astype(bf16)
            else:
                pl.when(self.sends[k])(copy.wait_send)
                pl.when(self.gets[k])(copy.wait_recv)

                @pl.when(self.middle)
                def _():
                    if kind == "down":
                        self.got[k][ring] = self.got[k - 1][ring]
                    else:
                        total = self.got[k - 1][ring].astype(f32) + self.got[k][ring].astype(f32)
                        self.got[k][ring] = total.astype(bf16)

            if s < n:
                follow = self.reduce_copy(s, ring)
                if self.sends[s] is None:
                    follow.start()
                else:
                    pl.when(self.sends[s])(follow.start)
            else:
                self.own_copy(ring, chunk).start()
                self.gather_copy(0, ring, chunk).start()
            return
        t = s - n - 1
        self.gather_copy(t, ring, chunk).wait()
        if t == 0:
            self.own_copy(ring, chunk).wait()
        if t + 1 < len(self.gather):
            self.gather_copy(t + 1, ring, chunk).start()


def make_streams(width, plane, line):
    unit = width // 14
    short = [(line[0][0], "line")] if len(line) == 2 else line
    return [
        Stream(0, 5 * unit, plane + short),
        Stream(5 * unit, 5 * unit, plane[::-1] + short),
        Stream(10 * unit, 4 * unit, line + plane),
    ]


LOADS = ("resid", "cot", "gain1", "gain2", "w_out", "ctx", "q", "kv", "lse", "normed", "own_in")
FIRST = ("resid", "cot", "gain1", "gain2")
STREAMED = ("wq", "wk", "wv", "table", "w_gate", "w_up", "w_down")


def backward_kernel(heads, streams, n_ffn, n_small, *refs):
    nl, ns = len(LOADS), len(STREAMED)
    hbm = dict(zip(LOADS + STREAMED, refs[: nl + ns]))
    sums_ref, layer_out_ref, input_grad_ref, grads_ref = refs[nl + ns : nl + ns + 4]
    refs = list(refs[nl + ns + 4 :])
    m = dict(zip(LOADS, refs[:nl]))
    refs = refs[nl:]
    (
        load_sem, w_qkv, table_s, up_t, cot_t, wide, trio, acc, out_s, wg, wu, wd, made,
        w_sem, made_sem, dmid_o, part_o, dlow, delta, dkv, dkv_o, k0, small,
        din_o, rowsum, pair_send, pair_recv, kv_send, kv_recv, out_sem,
        gain_own, gain_o, dq_t, k_t, gain1, gain2,
    ) = refs[:36]
    refs = refs[36:]
    mlp = do = wide
    dmid_s = acc
    dproj = trio
    vec = acc.at[0:SLOT, :]
    din_own = dmid_o.at[0 : dmid_o.shape[0] // 2, :]
    to_send = wd
    rows, width = m["cot"].shape
    half = rows // 2
    blk, nb = lax.axis_index("blk"), lax.axis_size("blk")
    core = lax.axis_index("tensor")
    nz = lax.axis_size("batch")
    other = {"tensor": 1 - core}
    tile = 256
    nq = heads * HEAD
    qkv = nq + SLOT

    pos = 0
    for st in streams:
        cnt = len(st.scratch())
        st.bind(
            refs[pos : pos + cnt],
            [(n_ffn, lambda c: grads_ref.at[c]), (n_small, lambda c: small.at[c])],
            sums_ref,
        )
        pos += cnt

    loads = {
        name: pltpu.make_async_copy(hbm[name], m[name], load_sem.at[i])
        for i, name in enumerate(LOADS)
    }
    late = weight_copies(hbm, dict(w_qkv=w_qkv, table=table_s), load_sem, nl, blk)

    n_pairs = -(-n_ffn // 2)
    odd = n_ffn % 2 == 1
    wide2 = 2 * PART

    def weights(p, count):
        slot = lax.rem(p, 2)
        cols = pl.ds(pl.multiple_of(p * wide2, wide2), count)
        return [
            pltpu.make_async_copy(
                hbm["w_gate"].at[:, cols], wg.at[slot, :, 0:count], w_sem.at[0, slot]
            ),
            pltpu.make_async_copy(
                hbm["w_up"].at[:, cols], wu.at[slot, :, 0:count], w_sem.at[1, slot]
            ),
            pltpu.make_async_copy(
                hbm["w_down"].at[cols, :],
                wd.at[pl.ds(pl.multiple_of(slot * wide2, wide2), count), :],
                w_sem.at[2, slot],
            ),
        ]

    def for_weights(p, act):
        last = n_pairs - 1 if odd else n_pairs

        @pl.when(p < last)
        def _():
            for copy in weights(p, wide2):
                act(copy)

        if odd:
            @pl.when(p == last)
            def _():
                for copy in weights(p, PART):
                    act(copy)

    for name in FIRST:
        loads[name].start()
    for_weights(0, lambda copy: copy.start())
    for_weights(1, lambda copy: copy.start())
    for name in LOADS:
        if name not in FIRST:
            loads[name].start()
    for copy in late:
        copy.start()

    batch = lax.axis_index("batch")
    meet(
        [other]
        + [{"blk": lax.rem(blk + d, nb)} for d in range(1, nb)]
        + [
            {"batch": batch + (1 - 2 * lax.rem(batch // (1 << b), 2)) * (1 << b)}
            for b in range(int(math.log2(nz)))
        ]
        + ([{"batch": 3 - batch}] if nz == 4 else [])
    )

    def swap(k, src, dst):
        return remote(src, dst, pair_send.at[k], pair_recv.at[k], other)

    def dmid_swap():
        return swap(0, dlow, dmid_o)

    theirs = pl.multiple_of((1 - core) * half, 16)
    ours = pl.multiple_of(core * half, 16)

    def part_swap():
        return swap(1, to_send, part_o)

    def din_swap():
        return swap(2, to_send, din_o)

    def gain_swap():
        return swap(3, gain_own, gain_o)

    def put(first, at, value):
        done, n = 0, value.shape[1]
        while done < n:
            c, lane = divmod(first + done, CHUNK)
            take = min(n - done, CHUNK - lane)
            small[c, at, lane : lane + take] = value[:, done : done + take].astype(bf16)
            done += take

    tq, tk = 256, 512

    def begin():
        for name in FIRST:
            loads[name].wait()
        gain1[...] = row_of(m["gain1"], width)
        gain2[...] = row_of(m["gain2"], width)

        def step(r, _):
            at = pl.ds(pl.multiple_of(r * tile, tile), tile)
            resid = m["resid"][at, :]
            rho = lax.rsqrt(jnp.mean(resid * resid, axis=1, keepdims=True) + norm_eps)
            normed = resid * rho * gain2[...]
            mlp[at, :] = normed.astype(bf16)
            up_t[:, at] = jnp.transpose(normed).astype(bf16)
            cot_t[:, at] = jnp.transpose(m["cot"][at, :].astype(f32)).astype(bf16)
            return 0

        lax.fori_loop(0, rows // tile, step, 0)
        dmid_s[...] = jnp.zeros(dmid_s.shape, f32)
        out_s[...] = jnp.zeros(out_s.shape, f32)

    def made_copy(p):
        slot = lax.rem(p, 2)
        return pltpu.make_async_copy(
            made.at[slot], grads_ref.at[pl.ds(p * 2, 2)], made_sem.at[slot]
        )

    def feed_forward(p):
        slot = lax.rem(p, 2)

        @pl.when(p >= 2)
        def _():
            made_copy(p - 1).wait()

        for_weights(p, lambda copy: copy.wait())
        if odd:
            @pl.when(p == n_pairs - 1)
            def _():
                wg[slot, :, PART:] = jnp.zeros((width, PART), bf16)
                wu[slot, :, PART:] = jnp.zeros((width, PART), bf16)
                rest = pl.ds(pl.multiple_of(slot * wide2 + PART, PART), PART)
                wd[rest, :] = jnp.zeros((PART, width), bf16)

        w_g, w_u = wg[slot], wu[slot]
        w_d = wd[pl.ds(pl.multiple_of(slot * wide2, wide2), wide2), :]
        for r in range(rows // tile):
            at = slice(r * tile, (r + 1) * tile)
            gate = dot(mlp[at, :], w_g, NN)
            upper = dot(mlp[at, :], w_u, NN)
            d_hidden = dot(m["cot"][at, :], w_d, NT)
            sigma = 1.0 / (1.0 + jnp.exp(-gate))
            activ = gate * sigma
            hidden = (activ * upper).astype(bf16)
            d_gate = (d_hidden * upper * sigma * (1.0 + gate * (1.0 - sigma))).astype(bf16)
            d_up = (d_hidden * activ).astype(bf16)
            for c in range(2):
                cols = slice(c * PART, (c + 1) * PART)
                trio[at, c * CHUNK : c * CHUNK + PART] = hidden[:, cols]
                trio[at, c * CHUNK + PART : c * CHUNK + 2 * PART] = d_gate[:, cols]
                trio[at, c * CHUNK + 2 * PART : (c + 1) * CHUNK] = d_up[:, cols]
            out_s[at, :] += dot(hidden, w_d, NN)
            dmid_s[at, :] += dot(d_gate, w_g, NT) + dot(d_up, w_u, NT)
        for c in range(2):
            first = c * CHUNK
            made[slot, c, :, :PART] = dot(
                cot_t[...], trio[:, first : first + PART], NN
            ).astype(bf16)
            made[slot, c, :, PART:] = dot(
                up_t[...], trio[:, first + PART : first + CHUNK], NN
            ).astype(bf16)
        made_copy(p).start()
        for_weights(p + 2, lambda copy: copy.start())

        @pl.when(p == 0)
        def _():
            made_copy(p).wait()

    def hand_over():
        made_copy(n_pairs - 1).wait()

        def step(r, _):
            at = pl.ds(pl.multiple_of(r * tile, tile), tile)
            dlow[at, :] = dmid_s[at, :].astype(bf16)
            return 0

        lax.fori_loop(0, rows // tile, step, 0)
        dmid_swap().start()

        def step_part(r, _):
            at = pl.ds(pl.multiple_of(r * tile, tile), tile)
            src = pl.ds(pl.multiple_of(theirs + r * tile, tile), tile)
            to_send[at, :] = out_s[src, :].astype(bf16)
            return 0

        lax.fori_loop(0, half // tile, step_part, 0)
        part_swap().start()

    def before():
        for name in LOADS:
            if name not in FIRST:
                loads[name].wait()
        for copy in late:
            copy.wait()
        dmid_swap().wait()
        part_swap().wait()
        vec[...] = jnp.zeros(vec.shape, f32)

        def out_rows(r, _):
            at = pl.ds(pl.multiple_of(r * tile, tile), tile)
            mine = pl.ds(pl.multiple_of(ours + r * tile, tile), tile)
            part_o[at, :] = (
                m["resid"][mine, :] + out_s[mine, :] + part_o[at, :].astype(f32)
            ).astype(bf16)
            return 0

        lax.fori_loop(0, half // tile, out_rows, 0)
        pltpu.make_async_copy(part_o, layer_out_ref, out_sem.at[0]).start()

        head = lax.broadcasted_iota(jnp.int32, (8, nq), 0)
        column = lax.broadcasted_iota(jnp.int32, (8, nq), 1)
        inside = (column >= head * HEAD) & (column < (head + 1) * HEAD)
        of_head = jnp.where(inside, 1.0, 0.0).astype(bf16)

        def norm(r, _):
            at = pl.ds(pl.multiple_of(r * tile, tile), tile)
            dmid = dlow[at, :].astype(f32) + dmid_o[at, :].astype(f32)
            resid = m["resid"][at, :]
            rho = lax.rsqrt(jnp.mean(resid * resid, axis=1, keepdims=True) + norm_eps)
            n2 = resid * rho
            vec[1:2, :] += jnp.sum(dmid * n2, axis=0, keepdims=True)
            weighted = dmid * gain2[...]
            d_resid = m["cot"][at, :].astype(f32) + rho * (
                weighted - n2 * jnp.mean(weighted * n2, axis=1, keepdims=True)
            )
            m["resid"][at, :] = d_resid
            low = d_resid.astype(bf16)
            dlow[at, :] = low
            d_ctx = dot(low, m["w_out"][...], NT).astype(bf16).astype(f32)
            zero = jnp.zeros((tile, HEAD), f32)
            for h in range(heads):
                own = d_ctx[:, h * HEAD : (h + 1) * HEAD]
                do[at, h * SLOT : (h + 1) * SLOT] = jnp.concatenate([zero, own], 1).astype(bf16)
            rest = d_ctx * m["ctx"][at, :].astype(f32)
            total = jnp.zeros((8, tile), f32)
            for _ in range(3):
                term = rest.astype(bf16)
                total = total + dot(of_head, term, NT)
                rest = rest - term.astype(f32)
            delta[:, at] = total
            return 0

        lax.fori_loop(0, rows // tile, norm, 0)
        lane = lax.broadcasted_iota(jnp.int32, (tk, SLOT), 1)

        def keys(i, _):
            at = pl.ds(pl.multiple_of(i * tk, tk), tk)
            kv = m["kv"][at, :].astype(f32)
            k0[at, :] = jnp.where(lane < HEAD, kv, 0.0).astype(bf16)
            k_t[:, at] = jnp.transpose(kv)[:HEAD, :].astype(bf16)
            return 0

        lax.fori_loop(0, (blk + 1) * (rows // tk), keys, 0)
        dq_t[...] = jnp.zeros(dq_t.shape, f32)

    def grad_out():
        def step(k, _):
            at = pl.ds(pl.multiple_of(k * 128, 128), 128)
            put(0, at, dot(dlow[:, at], m["ctx"][...], TN))
            return 0

        lax.fori_loop(0, width // 128, step, 0)

    def pair(kt, kvt, kt_t, qt, masked):
        at = pl.ds(pl.multiple_of(qt * tq, tq), tq)

        def score(h):
            cols = slice(h * SLOT, (h + 1) * SLOT)
            return dot(kt, m["q"][at, cols], NT), dot(kvt, do[at, cols], NT)

        def add(h, p, ds):
            cols = slice(h * SLOT, (h + 1) * SLOT)
            dq_t[h, :, at] += dot(kt_t, ds, NN)
            return dot(ds, m["q"][at, cols], NN) + dot(p, do[at, cols], NN)

        grad, ahead, behind = None, score(0), None
        for h in range(heads):
            s, dp = ahead
            if h + 1 < heads:
                ahead = score(h + 1)
            p = jnp.exp(s - m["lse"][h : h + 1, at])
            if masked is not None:
                p = jnp.where(masked, p, 0.0)
            ds = (p * (dp - delta[h : h + 1, at])).astype(bf16)
            if behind is not None:
                part = add(*behind)
                grad = part if grad is None else grad + part
            behind = (h, p.astype(bf16), ds)
        return grad + add(*behind)

    def own_tile(e):
        ki = lax.broadcasted_iota(jnp.int32, (tk, tq), 0)
        qi = lax.broadcasted_iota(jnp.int32, (tk, tq), 1)
        at_k = pl.ds(pl.multiple_of(blk * rows + e * tk, tk), tk)
        kt, kvt, kt_t = k0[at_k, :], m["kv"][at_k, :], k_t[:, at_k]
        first = e * (tk // tq)

        def near(j, grad):
            return grad + pair(kt, kvt, kt_t, first + j, ki <= qi + j * tq)

        def far(qt, grad):
            return grad + pair(kt, kvt, kt_t, qt, None)

        grad = lax.fori_loop(0, tk // tq, near, jnp.zeros((tk, SLOT), f32))
        grad = lax.fori_loop(first + tk // tq, rows // tq, far, grad)
        dkv[at_k, :] = grad.astype(bf16)

    def earlier(i):
        at_k = pl.ds(pl.multiple_of(i * tk, tk), tk)
        kt, kvt, kt_t = k0[at_k, :], m["kv"][at_k, :], k_t[:, at_k]

        def step(qt, grad):
            return grad + pair(kt, kvt, kt_t, qt, None)

        grad = lax.fori_loop(0, rows // tq, step, jnp.zeros((tk, SLOT), f32))
        dkv[at_k, :] = grad.astype(bf16)

    def kv_copy(d):
        to = lax.rem(blk + d, nb)
        at = pl.ds(pl.multiple_of(to * rows, rows), rows)
        return remote(
            dkv.at[at, :], dkv_o.at[d - 1], kv_send.at[d - 1], kv_recv.at[d - 1], {"blk": to}
        )

    def kv_start():
        for d in range(1, nb):
            @pl.when(lax.rem(blk + d, nb) < blk)
            def _(d=d):
                kv_copy(d).start()

    def project_queries():
        def step(r, _):
            at = pl.ds(pl.multiple_of(r * tile, tile), tile)
            table = spread_table(table_s[at, :])
            zero = jnp.zeros((HEAD, tile), f32)
            for h in range(heads):
                v = jnp.transpose(jnp.concatenate([dq_t[h, :, at], zero], 0))
                v = turn(v * HEAD**-0.5, table, -1.0)
                dproj[at, h * HEAD : (h + 1) * HEAD] = v[:, :HEAD].astype(bf16)
            return 0

        lax.fori_loop(0, rows // tile, step, 0)

    def project():
        for d in range(1, nb):
            @pl.when(lax.rem(blk + d, nb) < blk)
            def _(d=d):
                kv_copy(d).wait_send()

            @pl.when(lax.rem(blk + nb - d, nb) > blk)
            def _(d=d):
                kv_copy(d).wait_recv()
                for r in range(rows // tile):
                    at = pl.ds(pl.multiple_of(blk * rows + r * tile, tile), tile)
                    total = dkv[at, :].astype(f32) + dkv_o[d - 1, r * tile : (r + 1) * tile].astype(f32)
                    dkv[at, :] = total.astype(bf16)

        rowsum[...] = jnp.zeros(rowsum.shape, f32)

        def unrotate(r, _):
            at = pl.ds(pl.multiple_of(r * tile, tile), tile)
            at_b = pl.ds(pl.multiple_of(blk * rows + r * tile, tile), tile)
            table = spread_table(table_s[at, :])
            dproj[at, nq:qkv] = turn(dkv[at_b, :].astype(f32), table, -1.0).astype(bf16)
            rowsum[0:1, :] += jnp.sum(dproj[at, :qkv].astype(f32), axis=0, keepdims=True)
            return 0

        lax.fori_loop(0, rows // tile, unrotate, 0)

        def d_in(to, first):
            def step(r, _):
                src = pl.ds(pl.multiple_of(first + r * tile, tile), tile)
                at = pl.ds(pl.multiple_of(r * tile, tile), tile)
                to[at, :] = dot(dproj[src, :qkv], w_qkv[...], NN).astype(bf16)
                return 0

            lax.fori_loop(0, half // tile, step, 0)

        d_in(to_send, theirs)
        din_swap().start()
        d_in(din_own, ours)

        def grads(k, _):
            at = pl.ds(pl.multiple_of(k * 128, 128), 128)
            put(nq, at, dot(m["normed"][:, at], dproj[:, :qkv], TN))
            return 0

        lax.fori_loop(0, width // 128, grads, 0)

    def finish():
        din_swap().wait()

        def step(r, _):
            at = pl.ds(pl.multiple_of(r * tile, tile), tile)
            mine = pl.ds(pl.multiple_of(ours + r * tile, tile), tile)
            d_in = din_own[at, :].astype(f32) + din_o[at, :].astype(f32)
            x = m["own_in"][at, :].astype(f32)
            rho = lax.rsqrt(jnp.mean(x * x, axis=1, keepdims=True) + norm_eps)
            n1 = x * rho
            vec[0:1, :] += jnp.sum(d_in * n1, axis=0, keepdims=True)
            weighted = d_in * gain1[...]
            grad = m["resid"][mine, :] + rho * (
                weighted - n1 * jnp.mean(weighted * n1, axis=1, keepdims=True)
            )
            din_own[at, :] = grad.astype(bf16)
            return 0

        lax.fori_loop(0, half // tile, step, 0)
        pltpu.make_async_copy(din_own, input_grad_ref, out_sem.at[1]).start()
        gain_own[...] = vec[0:8, :]
        gain_swap().start()
        vec[2:3, : nq + SLOT] = rowsum[0:1, :]
        gain_swap().wait()
        vec[0:1, :] = gain_own[0:1, :] + gain_o[0:1, :]
        put(2 * nq + SLOT, slice(None), jnp.transpose(vec[...]))

    plan = slots_of(n_ffn, rows // tk, nb)

    def compute(i):
        pl.when(i == 0)(begin)
        few = plan["singles"]
        count = jnp.where(i < few, 1, jnp.where(i < plan["before"], 2, 0))
        first = jnp.where(i < few, i, 2 * i - few)
        count = jnp.minimum(count, jnp.maximum(n_pairs - first, 0))

        def step(c, _):
            feed_forward(first + c)
            return 0

        lax.fori_loop(0, count, step, 0)
        pl.when(i == plan["before"] - 1)(hand_over)
        pl.when(i == plan["before"])(before)

        @pl.when((i >= plan["own"]) & (i < plan["own"] + rows // tk))
        def _():
            own_tile(i - plan["own"])

        pl.when(i == plan["early"] - 1)(grad_out)

        @pl.when((i >= plan["early"]) & (i - plan["early"] < blk * (rows // tk)))
        def _():
            earlier(i - plan["early"])

        pl.when(i == plan["queries"] - 1)(kv_start)
        pl.when(i == plan["queries"])(project_queries)
        pl.when(i == plan["queries"] + 1)(project)
        pl.when(i == plan["queries"] + 2)(finish)

    early_turn = min(plan["early"] - 1, n_ffn)
    gap = max(0, plan["queries"] + 2 - n_ffn - n_small + 1)
    n = n_ffn + n_small + gap
    depth = max(st.stages for st in streams)

    def chunk_of(t):
        late = jnp.where(t <= n_ffn, t - 1, t - gap)
        return jnp.where(t < early_turn, t, jnp.where(t == early_turn, n_ffn, late))

    def slot(i, _):
        compute(i)
        for st in streams:
            for s in reversed(range(st.stages)):
                t = i - s
                real = (t >= 0) & (t < n)
                if gap:
                    real = real & ((t <= n_ffn) | (t > n_ffn + gap))

                @pl.when(real)
                def _(st=st, s=s, t=t):
                    st.stage(s, t, chunk_of(t))

        return 0

    lax.fori_loop(0, n + depth - 1, slot, 0)
    pltpu.make_async_copy(part_o, layer_out_ref, out_sem.at[0]).wait()
    pltpu.make_async_copy(din_own, input_grad_ref, out_sem.at[1]).wait()


def slots_of(n_ffn, tiles, nb):
    pairs = -(-n_ffn // 2)
    singles = pairs
    before = singles + -(-(pairs - singles) // 2)
    own = before + 1
    early = own + tiles
    return dict(
        singles=singles, before=before, own=own, early=early, queries=early + (nb - 1) * tiles
    )


def backward(values, heads, plane, line, nb):
    rows, width = values["cot"].shape
    half = rows // 2
    keys = values["kv"].shape[0]
    n_ffn = values["w_gate"].shape[1] // PART
    n_small = -(-(2 * heads * HEAD + 2 * SLOT) // CHUNK)
    streams = make_streams(width, plane, line)
    hbm = pl.BlockSpec(memory_space=pl.ANY)
    dma = pltpu.SemaphoreType.DMA
    vm = pltpu.VMEM
    assert half == 4 * PART and heads * SLOT == width
    scratch = [vm(values[name].shape, values[name].dtype) for name in LOADS]
    scratch += [
        dma((len(LOADS) + 4,)),
        vm((heads * HEAD + SLOT, width), bf16),
        vm((rows, HEAD), f32),
        vm((width, rows), bf16),
        vm((width, rows), bf16),
        vm((rows, width), bf16),
        vm((rows, 2 * CHUNK), bf16),
        vm((rows, width), f32),
        vm((rows, width), f32),
        vm((2, width, 2 * PART), bf16),
        vm((2, width, 2 * PART), bf16),
        vm((4 * PART, width), bf16),
        vm((2, 2, width, CHUNK), bf16),
        dma((3, 2)),
        dma((2,)),
        vm((rows, width), bf16),
        vm((half, width), bf16),
        vm((rows, width), bf16),
        vm((8, rows), f32),
        vm((keys, SLOT), bf16),
        vm((nb - 1, rows, SLOT), bf16),
        vm((keys, SLOT), bf16),
        vm((n_small, width, CHUNK), bf16),
        vm((half, width), bf16),
        vm((8, heads * HEAD + SLOT), f32),
        dma((4,)),
        dma((4,)),
        dma((nb - 1,)),
        dma((nb - 1,)),
        dma((2,)),
        vm((8, width), f32),
        vm((8, width), f32),
        vm((heads, HEAD, rows), f32),
        vm((HEAD, keys), bf16),
        vm((1, width), f32),
        vm((1, width), f32),
    ]
    for st in streams:
        scratch += st.scratch()
    return pl.pallas_call(
        functools.partial(backward_kernel, heads, streams, n_ffn, n_small),
        out_shape=(
            jax.ShapeDtypeStruct((n_ffn + n_small, width, CHUNK), bf16),
            jax.ShapeDtypeStruct((half, width), bf16),
            jax.ShapeDtypeStruct((half, width), bf16),
            jax.ShapeDtypeStruct((n_ffn + n_ffn % 2, width, CHUNK), bf16),
        ),
        in_specs=[hbm] * (len(LOADS) + len(STREAMED)),
        out_specs=(hbm, hbm, hbm, hbm),
        scratch_shapes=scratch,
        compiler_params=pltpu.CompilerParams(
            collective_id=0, has_side_effects=True, vmem_limit_bytes=60 * 2**20
        ),
        name="backward",
    )(*[values[name] for name in LOADS + STREAMED])


def unpack_kernel(heads, n_small, chunk_ref, *refs):
    small = refs[:n_small]
    down, gate, up, g_out, g_q, g_k, g_v, gain1, gain2, bias = refs[n_small:]
    step = pl.program_id(0)
    for c in range(2):
        value, at = chunk_ref[c], slice(c * PART, (c + 1) * PART)
        down[at, :] = jnp.transpose(value[:, :PART].astype(f32))
        gate[:, at] = value[:, PART : 2 * PART].astype(f32)
        up[:, at] = value[:, 2 * PART :].astype(f32)

    def take(first, count):
        done = 0
        while done < count:
            c, lane = divmod(first + done, CHUNK)
            n = min(count - done, SLOT - lane % SLOT)
            yield done, n, small[c][0, :, lane : lane + n].astype(f32)
            done += n

    @pl.when(step == 0)
    def _():
        nq = heads * HEAD
        for done, n, piece in take(0, nq):
            g_out[done : done + n, :] = jnp.transpose(piece)
        for done, n, piece in take(nq, nq):
            g_q[done : done + n, :] = jnp.transpose(piece)
        for done, n, piece in take(2 * nq, HEAD):
            g_k[...] = jnp.transpose(piece)
        for done, n, piece in take(2 * nq + HEAD, HEAD):
            g_v[...] = jnp.transpose(piece)
        for done, n, piece in take(2 * nq + 2 * HEAD, SLOT):
            vec = jnp.transpose(piece)
            for row, to in ((0, gain1), (1, gain2), (2, bias)):
                for i in range(to.shape[0]):
                    to[i : i + 1, :] = vec[row : row + 1, i * 128 : (i + 1) * 128]


def unpack(sums, n_ffn, heads):
    n, width, _ = sums.shape
    n_small = n - n_ffn
    shape = lambda *dims: jax.ShapeDtypeStruct(dims, f32)
    nq = heads * HEAD
    lanes = [(width // 128, 128), (width // 128, 128), (-(-(nq + SLOT) // 128), 128)]
    whole = [(nq, width), (nq, width), (HEAD, width), (HEAD, width)] + lanes
    return pl.pallas_call(
        functools.partial(unpack_kernel, heads, n_small),
        grid=(-(-n_ffn // 2),),
        out_shape=[
            shape(n_ffn * PART, width), shape(width, n_ffn * PART), shape(width, n_ffn * PART)
        ] + [shape(*dims) for dims in whole],
        in_specs=[pl.BlockSpec((2, width, CHUNK), lambda j: (j, 0, 0))]
        + [
            pl.BlockSpec((1, width, CHUNK), lambda j, c=c: (n_ffn + c, 0, 0))
            for c in range(n_small)
        ],
        out_specs=[
            pl.BlockSpec((2 * PART, width), lambda j: (j, 0)),
            pl.BlockSpec((width, 2 * PART), lambda j: (0, j)),
            pl.BlockSpec((width, 2 * PART), lambda j: (0, j)),
        ] + [pl.BlockSpec(dims, lambda j: (0, 0)) for dims in whole],
        compiler_params=pltpu.CompilerParams(
            vmem_limit_bytes=48 * 2**20, dimension_semantics=("arbitrary",)
        ),
        name="unpack",
    )(*[sums] * (1 + n_small))


def shards(
    layer_in, cotangent, lengths, attn_gain, w_query, query_bias, w_key, key_bias, w_value,
    value_bias, w_out, mlp_gain, w_gate, w_up, w_down,
):
    half, width = layer_in.shape
    rows = half * lax.axis_size("tensor")
    nb = lax.axis_size("blk")
    heads = w_query.shape[1] // HEAD
    biases = jnp.concatenate([query_bias, key_bias, value_bias]).astype(f32)
    biases = jnp.pad(biases, (0, -biases.shape[0] % 128)).reshape(-1, 128)
    values = dict(
        own_in=layer_in, own_cot=cotangent, wq=w_query.T, wk=w_key.T, wv=w_value.T, w_out=w_out,
        gain1=attn_gain.reshape(-1, 128), gain2=mlp_gain.reshape(-1, 128), bias=biases,
        table=jnp.asarray(rotary_table(rows * nb)), w_gate=w_gate, w_up=w_up, w_down=w_down,
    )
    values |= front(lengths, values, heads, nb)
    sums, layer_out, input_grad, _ = backward(
        values, heads, bits_of("blk"), bits_of("batch"), nb
    )
    g_down, g_gate, g_up, g_out, g_query, g_key, g_value, g_gain1, g_gain2, g_bias = unpack(
        sums, w_gate.shape[1] // PART, heads
    )
    nq = heads * HEAD
    g_bias = g_bias.reshape(-1)
    return (
        layer_out, input_grad, g_gain1.reshape(-1), g_query.T, g_bias[:nq], g_key.T,
        g_bias[nq : nq + HEAD], g_value.T, g_bias[nq + HEAD : nq + 2 * HEAD], g_out,
        g_gain2.reshape(-1), g_gate, g_up, g_down,
    )


def solution(mesh):
    rows = P(("batch", "blk", "tensor"), None)
    cols, part, split = P(None, "tensor"), P("tensor"), P("tensor", None)
    return jax.shard_map(
        shards,
        mesh=mesh,
        in_specs=(
            rows, rows, P("batch", None), P(), cols, part, cols, part, cols, part, split, P(),
            cols, cols, split,
        ),
        out_specs=(
            rows, rows, P(), cols, part, cols, part, cols, part, split, P(), cols, cols, split,
        ),
        check_vma=False,
    )
```

time: 469 us -> 340 us (0.72)
  Pallas kernels: 446 us -> 334 us
  local copies, waits for them, and re-layouts: 20.4 us -> 3.02 us
    pallas_call x2 -> x1, Pallas kernels: 104 us -> 18 us  [unpack(): pl.pallas_call(functools.partial(unpack_kernel, heads, n_small), grid=(-(...]
    pallas_call x1, Pallas kernels: 321 us -> 290 us  [backward(): pl.pallas_call(functools.partial(backward_kernel, heads, streams, n_ffn,...]
    unnamed x12 -> x6, local copies, waits for them, and re-layouts: 13 us -> 1.85 us
  transfers between devices with their start and end apart: 1 -> 0, of which waited for: 0 -> 0; matrix products, arithmetic and copies ran while one was open for 2% -> 0% of each run, Pallas kernels for 5% -> 0%
where the time goes in v4:
time: 340 us
  Pallas kernels  334 us (98%)
    pallas_call x1, Pallas kernels, backward(): pl.pallas_call(functools.partial(backward_kernel, heads, streams, n_ffn,...  290 us
    pallas_call x1, Pallas kernels, front(): pl.pallas_call(functools.partial(front_kernel, heads), out_shape=[outs[na...  25.9 us
    pallas_call x1, Pallas kernels, unpack(): pl.pallas_call(functools.partial(unpack_kernel, heads, n_small), grid=(-(...  18 us

profile of v4, /device:TPU:0, one launch (start us, length us, event | category | flops | bytes accessed | tf_op | source)
XLA Modules:
  0.0 339.9 jit_solution(6079069161694088677)
XLA Ops:
  1.3 1.4 fusion.6.refs_7_
  2.7 25.9 %front.1 = (bf16[1024,896]{1,0:T(8,128)(2,1)}, bf16[1024,896]{1,0:T(8,128)(2,1)}, bf16[1024,896]{1,0:T(8,128)(2,1)}, bf16[4096,128]{1,0:T(8,128)(2,1)}, bf16[102...) custom-call(s32[1,1]{1,0:T(1,128)S(6)} %copy.32.length_ref, bf16[512,896]{1,0:T(8,128)(2,1)} %refs_10_.1, ...), custom_call_target="tpu_custom_call" | custom-call | tf_op jit(solution)/shard_map/front/pallas_call | solution.py:346
  28.6 290.3 %backward.1 = (bf16[22,896,384]{2,1,0:T(8,128)(2,1)}, bf16[512,896]{1,0:T(8,128)(2,1)}, bf16[512,896]{1,0:T(8,128)(2,1)}, bf16[20,896,384]{2,1,0:T(8,128)(2,1)}) custom-call(f32[1024,896]{1,0:T(8,128)} %get-tuple-element.34.refs_0_, bf16[1024,896]{1,0:T(8,128)(2,1)} %get-tuple-element.35.refs_1_, f32[7,128]{1,0:T(8,128)} %bitcast.25, f32[7,128]{1,0:T(8,128)} %bitcast.26, ...), custom_call_target="tpu_custom_call" | custom-call | tf_op jit(solution)/shard_map/backward/pallas_call | solution.py:1149
  318.9 0.0 copy-start.1
  318.9 0.0 copy-start
  318.9 18.0 %unpack.1 = (f32[2432,896]{1,0:T(8,128)}, f32[896,2432]{1,0:T(8,128)}, f32[896,2432]{1,0:T(8,128)}, f32[448,896]{1,0:T(8,128)}, f32[448,896]{1,0:T(8,128)}, /*in...) custom-call(bf16[22,896,384]{2,1,0:T(8,128)(2,1)} %get-tuple-element.43.ch, ...), custom_call_target="tpu_custom_call" | custom-call | tf_op jit(solution)/shard_map/unpack/pallas_call | solution.py:1210
  336.9 0.6 fusion.7
  337.5 0.6 slice.9
  338.1 0.0 copy-done.1
  338.1 0.9 copy.33
  339.0 0.0 copy-done
  339.0 0.9 copy.34
Async XLA Ops:
  318.9 19.2 %copy-start.1 = (bf16[512,896]{1,0:T(8,128)(2,1)S(1)}, bf16[512,896]{1,0:T(8,128)(2,1)}, u32[]{:S(2)}) copy-start(bf16[512,896]{1,0:T(8,128)(2,1)} %get-tuple-element.70) | copy-start | bytes 2752516
  318.9 20.1 %copy-start = (bf16[512,896]{1,0:T(8,128)(2,1)S(1)}, bf16[512,896]{1,0:T(8,128)(2,1)}, u32[]{:S(2)}) copy-start(bf16[512,896]{1,0:T(8,128)(2,1)} %get-tuple-element.71) | copy-start | bytes 2752516

commit v5 on v4

--- a/solution.py
+++ b/solution.py
@@ -317,10 +317,12 @@
             + dot(m["ctx"][at, :], w_out[...], NN)
             + dot(ctx_o[at, :], w_out_o[...], NN)
         )
+        pltpu.make_async_copy(
+            m["resid"].at[at, :], out["resid"].at[at, :], out_sem.at[FRONT_OUT.index("resid")]
+        ).start()
         return 0
 
     lax.fori_loop(0, rows // tile, out_rows, 0)
-    save("resid").start()
     for name in FRONT_OUT:
         if name != "kv":
             save(name).wait()
@@ -576,12 +578,12 @@
     m = dict(zip(LOADS, refs[:nl]))
     refs = refs[nl:]
     (
-        load_sem, w_qkv, table_s, up_t, cot_t, wide, trio, acc, out_s, wg, wu, wd, made,
+        load_sem, w_qkv, table_s, up_t, cot_t, wide, trio, acc, out_s, wgu, wd, made,
         w_sem, made_sem, dmid_o, part_o, dlow, delta, dkv, dkv_o, k0, small,
         din_o, rowsum, pair_send, pair_recv, kv_send, kv_recv, out_sem,
         gain_own, gain_o, dq_t, k_t, gain1, gain2,
-    ) = refs[:36]
-    refs = refs[36:]
+    ) = refs[:35]
+    refs = refs[35:]
     mlp = do = wide
     dmid_s = acc
     dproj = trio
@@ -623,10 +625,10 @@
         cols = pl.ds(pl.multiple_of(p * wide2, wide2), count)
         return [
             pltpu.make_async_copy(
-                hbm["w_gate"].at[:, cols], wg.at[slot, :, 0:count], w_sem.at[0, slot]
+                hbm["w_gate"].at[:, cols], wgu.at[slot, :, 0:count], w_sem.at[0, slot]
             ),
             pltpu.make_async_copy(
-                hbm["w_up"].at[:, cols], wu.at[slot, :, 0:count], w_sem.at[1, slot]
+                hbm["w_up"].at[:, cols], wgu.at[slot, :, wide2 : wide2 + count], w_sem.at[1, slot]
             ),
             pltpu.make_async_copy(
                 hbm["w_down"].at[cols, :],
@@ -735,38 +737,37 @@
         if odd:
             @pl.when(p == n_pairs - 1)
             def _():
-                wg[slot, :, PART:] = jnp.zeros((width, PART), bf16)
-                wu[slot, :, PART:] = jnp.zeros((width, PART), bf16)
+                wgu[slot, :, PART:wide2] = jnp.zeros((width, PART), bf16)
+                wgu[slot, :, wide2 + PART :] = jnp.zeros((width, PART), bf16)
                 rest = pl.ds(pl.multiple_of(slot * wide2 + PART, PART), PART)
                 wd[rest, :] = jnp.zeros((PART, width), bf16)
 
-        w_g, w_u = wg[slot], wu[slot]
+        w_gu = wgu[slot]
         w_d = wd[pl.ds(pl.multiple_of(slot * wide2, wide2), wide2), :]
         for r in range(rows // tile):
             at = slice(r * tile, (r + 1) * tile)
-            gate = dot(mlp[at, :], w_g, NN)
-            upper = dot(mlp[at, :], w_u, NN)
+            both = dot(mlp[at, :], w_gu, NN)
+            gate, upper = both[:, :wide2], both[:, wide2:]
             d_hidden = dot(m["cot"][at, :], w_d, NT)
             sigma = 1.0 / (1.0 + jnp.exp(-gate))
             activ = gate * sigma
             hidden = (activ * upper).astype(bf16)
             d_gate = (d_hidden * upper * sigma * (1.0 + gate * (1.0 - sigma))).astype(bf16)
             d_up = (d_hidden * activ).astype(bf16)
+            d_pair = jnp.concatenate([d_gate, d_up], 1)
+            trio[at, :wide2] = hidden
+            trio[at, wide2:] = d_pair
+            out_s[at, :] += dot(hidden, w_d, NN)
+            dmid_s[at, :] += dot(d_pair, w_gu, NT)
+        for r in range(2):
+            at = slice(r * width // 2, (r + 1) * width // 2)
+            down = dot(cot_t[at, :], trio[:, :wide2], NN).astype(bf16)
+            pairs = dot(up_t[at, :], trio[:, wide2:], NN).astype(bf16)
             for c in range(2):
                 cols = slice(c * PART, (c + 1) * PART)
-                trio[at, c * CHUNK : c * CHUNK + PART] = hidden[:, cols]
-                trio[at, c * CHUNK + PART : c * CHUNK + 2 * PART] = d_gate[:, cols]
-                trio[at, c * CHUNK + 2 * PART : (c + 1) * CHUNK] = d_up[:, cols]
-            out_s[at, :] += dot(hidden, w_d, NN)
-            dmid_s[at, :] += dot(d_gate, w_g, NT) + dot(d_up, w_u, NT)
-        for c in range(2):
-            first = c * CHUNK
-            made[slot, c, :, :PART] = dot(
-                cot_t[...], trio[:, first : first + PART], NN
-            ).astype(bf16)
-            made[slot, c, :, PART:] = dot(
-                up_t[...], trio[:, first + PART : first + CHUNK], NN
-            ).astype(bf16)
+                made[slot, c, at, :PART] = down[:, cols]
+                made[slot, c, at, PART : 2 * PART] = pairs[:, cols]
+                made[slot, c, at, 2 * PART :] = pairs[:, wide2 + c * PART : wide2 + (c + 1) * PART]
         made_copy(p).start()
         for_weights(p + 2, lambda copy: copy.start())
 
@@ -796,7 +797,7 @@
 
     def before():
         for name in LOADS:
-            if name not in FIRST:
+            if name not in FIRST + ("kv",):
                 loads[name].wait()
         for copy in late:
             copy.wait()
@@ -849,6 +850,9 @@
             return 0
 
         lax.fori_loop(0, rows // tile, norm, 0)
+
+    def keys_first():
+        loads["kv"].wait()
         lane = lax.broadcasted_iota(jnp.int32, (tk, SLOT), 1)
 
         def keys(i, _):
@@ -1036,6 +1040,7 @@
             return 0
 
         lax.fori_loop(0, count, step, 0)
+        pl.when(i == max(plan["before"] - 3, 0))(keys_first)
         pl.when(i == plan["before"] - 1)(hand_over)
         pl.when(i == plan["before"])(before)
 
@@ -1116,8 +1121,7 @@
         vm((rows, 2 * CHUNK), bf16),
         vm((rows, width), f32),
         vm((rows, width), f32),
-        vm((2, width, 2 * PART), bf16),
-        vm((2, width, 2 * PART), bf16),
+        vm((2, width, 4 * PART), bf16),
         vm((4 * PART, width), bf16),
         vm((2, 2, width, CHUNK), bf16),
         dma((3, 2)),

time: 340 us -> 335 us (0.985)
  Pallas kernels: 334 us -> 329 us
    pallas_call x1, Pallas kernels: 290 us -> 286 us  [backward(): pl.pallas_call(functools.partial(backward_kernel, heads, streams, n_ffn,...]
where the time goes in v5:
time: 335 us
  Pallas kernels  329 us (98%)
    pallas_call x1, Pallas kernels, backward(): pl.pallas_call(functools.partial(backward_kernel, heads, streams, n_ffn,...  286 us
    pallas_call x1, Pallas kernels, front(): pl.pallas_call(functools.partial(front_kernel, heads), out_shape=[outs[na...  25.1 us
    pallas_call x1, Pallas kernels, unpack(): pl.pallas_call(functools.partial(unpack_kernel, heads, n_small), grid=(-(...  18 us

profile of v5, /device:TPU:0, one launch (start us, length us, event | category | flops | bytes accessed | tf_op | source)
XLA Modules:
  0.0 335.0 jit_solution(2196733145880083373)
XLA Ops:
  1.3 1.4 fusion.6.refs_7_
  2.7 25.1 %front.1 = (bf16[1024,896]{1,0:T(8,128)(2,1)}, bf16[1024,896]{1,0:T(8,128)(2,1)}, bf16[1024,896]{1,0:T(8,128)(2,1)}, bf16[4096,128]{1,0:T(8,128)(2,1)}, bf16[102...) custom-call(s32[1,1]{1,0:T(1,128)S(6)} %copy.32.length_ref, bf16[512,896]{1,0:T(8,128)(2,1)} %refs_10_.1, ...), custom_call_target="tpu_custom_call" | custom-call | tf_op jit(solution)/shard_map/front/pallas_call | solution.py:348
  27.7 286.2 %backward.1 = (bf16[22,896,384]{2,1,0:T(8,128)(2,1)}, bf16[512,896]{1,0:T(8,128)(2,1)}, bf16[512,896]{1,0:T(8,128)(2,1)}, bf16[20,896,384]{2,1,0:T(8,128)(2,1)}) custom-call(f32[1024,896]{1,0:T(8,128)} %get-tuple-element.34.refs_0_, bf16[1024,896]{1,0:T(8,128)(2,1)} %get-tuple-element.35.refs_1_, f32[7,128]{1,0:T(8,128)} %bitcast.25, f32[7,128]{1,0:T(8,128)} %bitcast.26, ...), custom_call_target="tpu_custom_call" | custom-call | tf_op jit(solution)/shard_map/backward/pallas_call | solution.py:1153
  314.0 0.0 copy-start.1
  314.0 0.0 copy-start
  314.0 18.0 %unpack.1 = (f32[2432,896]{1,0:T(8,128)}, f32[896,2432]{1,0:T(8,128)}, f32[896,2432]{1,0:T(8,128)}, f32[448,896]{1,0:T(8,128)}, f32[448,896]{1,0:T(8,128)}, /*in...) custom-call(bf16[22,896,384]{2,1,0:T(8,128)(2,1)} %get-tuple-element.43.ch, ...), custom_call_target="tpu_custom_call" | custom-call | tf_op jit(solution)/shard_map/unpack/pallas_call | solution.py:1214
  332.0 0.6 fusion.7
  332.6 0.6 slice.9
  333.1 0.0 copy-done.1
  333.1 0.9 copy.33
  334.1 0.0 copy-done
  334.1 0.9 copy.34
Async XLA Ops:
  314.0 19.2 %copy-start.1 = (bf16[512,896]{1,0:T(8,128)(2,1)S(1)}, bf16[512,896]{1,0:T(8,128)(2,1)}, u32[]{:S(2)}) copy-start(bf16[512,896]{1,0:T(8,128)(2,1)} %get-tuple-element.70) | copy-start | bytes 2752516
  314.0 20.1 %copy-start = (bf16[512,896]{1,0:T(8,128)(2,1)S(1)}, bf16[512,896]{1,0:T(8,128)(2,1)}, u32[]{:S(2)}) copy-start(bf16[512,896]{1,0:T(8,128)(2,1)} %get-tuple-element.71) | copy-start | bytes 2752516

commit v6 on v5

--- a/solution.py
+++ b/solution.py
@@ -883,7 +883,11 @@
         def add(h, p, ds):
             cols = slice(h * SLOT, (h + 1) * SLOT)
             dq_t[h, :, at] += dot(kt_t, ds, NN)
-            return dot(ds, m["q"][at, cols], NN) + dot(p, do[at, cols], NN)
+            return dot(
+                jnp.concatenate([ds, p], 1),
+                jnp.concatenate([m["q"][at, cols], do[at, cols]], 0),
+                NN,
+            )
 
         grad, ahead, behind = None, score(0), None
         for h in range(heads):
@@ -1070,7 +1074,7 @@
 
     def slot(i, _):
         compute(i)
-        for st in streams:
+        for st in streams[::-1]:
             for s in reversed(range(st.stages)):
                 t = i - s
                 real = (t >= 0) & (t < n)
@@ -1170,7 +1174,11 @@
 
 def unpack_kernel(heads, n_small, chunk_ref, *refs):
     small = refs[:n_small]
-    down, gate, up, g_out, g_q, g_k, g_v, gain1, gain2, bias = refs[n_small:]
+    rows_in, refs = refs[n_small : n_small + 2], refs[n_small + 2 :]
+    rows_out, refs = refs[-2:], refs[:-2]
+    for src, dst in zip(rows_in, rows_out):
+        dst[...] = src[...]
+    down, gate, up, g_out, g_q, g_k, g_v, gain1, gain2, bias = refs
     step = pl.program_id(0)
     for c in range(2):
         value, at = chunk_ref[c], slice(c * PART, (c + 1) * PART)
@@ -1204,34 +1212,40 @@
                     to[i : i + 1, :] = vec[row : row + 1, i * 128 : (i + 1) * 128]
 
 
-def unpack(sums, n_ffn, heads):
+def unpack(sums, layer_out, input_grad, n_ffn, heads):
     n, width, _ = sums.shape
     n_small = n - n_ffn
     shape = lambda *dims: jax.ShapeDtypeStruct(dims, f32)
     nq = heads * HEAD
     lanes = [(width // 128, 128), (width // 128, 128), (-(-(nq + SLOT) // 128), 128)]
     whole = [(nq, width), (nq, width), (HEAD, width), (HEAD, width)] + lanes
+    half = layer_out.shape[0]
+    steps = -(-n_ffn // 2)
+    cut = max(c for c in (1, 2, 4, 8) if c <= steps)
+    rows = pl.BlockSpec((half // cut, width), lambda j: (jnp.minimum(j, cut - 1), 0))
     return pl.pallas_call(
         functools.partial(unpack_kernel, heads, n_small),
         grid=(-(-n_ffn // 2),),
         out_shape=[
             shape(n_ffn * PART, width), shape(width, n_ffn * PART), shape(width, n_ffn * PART)
-        ] + [shape(*dims) for dims in whole],
+        ] + [shape(*dims) for dims in whole] + [
+            jax.ShapeDtypeStruct((half, width), bf16)
+        ] * 2,
         in_specs=[pl.BlockSpec((2, width, CHUNK), lambda j: (j, 0, 0))]
         + [
             pl.BlockSpec((1, width, CHUNK), lambda j, c=c: (n_ffn + c, 0, 0))
             for c in range(n_small)
-        ],
+        ] + [rows, rows],
         out_specs=[
             pl.BlockSpec((2 * PART, width), lambda j: (j, 0)),
             pl.BlockSpec((width, 2 * PART), lambda j: (0, j)),
             pl.BlockSpec((width, 2 * PART), lambda j: (0, j)),
-        ] + [pl.BlockSpec(dims, lambda j: (0, 0)) for dims in whole],
+        ] + [pl.BlockSpec(dims, lambda j: (0, 0)) for dims in whole] + [rows, rows],
         compiler_params=pltpu.CompilerParams(
             vmem_limit_bytes=48 * 2**20, dimension_semantics=("arbitrary",)
         ),
         name="unpack",
-    )(*[sums] * (1 + n_small))
+    )(*[sums] * (1 + n_small), layer_out, input_grad)
 
 
 def shards(
@@ -1253,9 +1267,10 @@
     sums, layer_out, input_grad, _ = backward(
         values, heads, bits_of("blk"), bits_of("batch"), nb
     )
-    g_down, g_gate, g_up, g_out, g_query, g_key, g_value, g_gain1, g_gain2, g_bias = unpack(
-        sums, w_gate.shape[1] // PART, heads
-    )
+    (
+        g_down, g_gate, g_up, g_out, g_query, g_key, g_value, g_gain1, g_gain2, g_bias,
+        layer_out, input_grad,
+    ) = unpack(sums, layer_out, input_grad, w_gate.shape[1] // PART, heads)
     nq = heads * HEAD
     g_bias = g_bias.reshape(-1)
     return (

time: 335 us -> 334 us (level)
  no operation moved by 1% of the time
where the time goes in v6:
time: 334 us; the launch traced here: 333 us
  Pallas kernels  327 us (98%)
  local copies, waits for them, and re-layouts  3.51 us (1%)
    pallas_call x1, Pallas kernels, backward(): pl.pallas_call(functools.partial(backward_kernel, heads, streams, n_ffn,...  284 us
    pallas_call x1, Pallas kernels, front(): pl.pallas_call(functools.partial(front_kernel, heads), out_shape=[outs[na...  25 us
    pallas_call x1, Pallas kernels, unpack(): pl.pallas_call(functools.partial(unpack_kernel, heads, n_small), grid=(-(...  18.2 us

profile of v6, /device:TPU:0, one launch (start us, length us, event | category | flops | bytes accessed | tf_op | source)
XLA Modules:
  0.0 333.4 jit_solution(14215811633652554705)
XLA Ops:
  1.3 1.4 fusion.6.refs_7_
  2.7 25.0 %front.1 = (bf16[1024,896]{1,0:T(8,128)(2,1)}, bf16[1024,896]{1,0:T(8,128)(2,1)}, bf16[1024,896]{1,0:T(8,128)(2,1)}, bf16[4096,128]{1,0:T(8,128)(2,1)}, bf16[102...) custom-call(s32[1,1]{1,0:T(1,128)S(6)} %copy.30.length_ref, bf16[512,896]{1,0:T(8,128)(2,1)} %refs_10_.1, ...), custom_call_target="tpu_custom_call" | custom-call | tf_op jit(solution)/shard_map/front/pallas_call | solution.py:348
  27.7 284.0 %backward.1 = (bf16[22,896,384]{2,1,0:T(8,128)(2,1)}, bf16[512,896]{1,0:T(8,128)(2,1)}, bf16[512,896]{1,0:T(8,128)(2,1)}, bf16[20,896,384]{2,1,0:T(8,128)(2,1)}) custom-call(f32[1024,896]{1,0:T(8,128)} %get-tuple-element.36.refs_0_, bf16[1024,896]{1,0:T(8,128)(2,1)} %get-tuple-element.37.refs_1_, f32[7,128]{1,0:T(8,128)} %bitcast.25, f32[7,128]{1,0:T(8,128)} %bitcast.26, ...), custom_call_target="tpu_custom_call" | custom-call | tf_op jit(solution)/shard_map/backward/pallas_call | solution.py:1157
  311.7 0.0 copy-start
  311.7 1.2 copy-done
  312.9 0.0 copy-start.1
  312.9 1.2 copy-done.1
  314.1 18.2 %unpack.1 = (f32[2432,896]{1,0:T(8,128)}, f32[896,2432]{1,0:T(8,128)}, f32[896,2432]{1,0:T(8,128)}, f32[448,896]{1,0:T(8,128)}, f32[448,896]{1,0:T(8,128)}, /*in...) custom-call(bf16[22,896,384]{2,1,0:T(8,128)(2,1)} %get-tuple-element, ...), custom_call_target="tpu_custom_call" | custom-call | tf_op jit(solution)/shard_map/unpack/pallas_call | solution.py:1226
  332.3 0.6 fusion.7
  332.8 0.6 slice.9
Async XLA Ops:
  311.7 1.2 copy-start
  312.9 1.2 copy-start.1

commit v7 on v6

--- a/solution.py
+++ b/solution.py
@@ -605,7 +605,11 @@
         cnt = len(st.scratch())
         st.bind(
             refs[pos : pos + cnt],
-            [(n_ffn, lambda c: grads_ref.at[c]), (n_small, lambda c: small.at[c])],
+            [
+                (1, lambda c: made.at[0, 0]),
+                (n_ffn - 1, lambda c: grads_ref.at[1 + c]),
+                (n_small, lambda c: small.at[c]),
+            ],
             sums_ref,
         )
         pos += cnt
@@ -729,7 +733,7 @@
     def feed_forward(p):
         slot = lax.rem(p, 2)
 
-        @pl.when(p >= 2)
+        @pl.when(p >= 1)
         def _():
             made_copy(p - 1).wait()
 
@@ -770,10 +774,6 @@
                 made[slot, c, at, 2 * PART :] = pairs[:, wide2 + c * PART : wide2 + (c + 1) * PART]
         made_copy(p).start()
         for_weights(p + 2, lambda copy: copy.start())
-
-        @pl.when(p == 0)
-        def _():
-            made_copy(p).wait()
 
     def hand_over():
         made_copy(n_pairs - 1).wait()

time: 334 us -> 336 us (level)
  no operation moved by 1% of the time
where the time goes in v7:
time: 336 us
  Pallas kernels  330 us (98%)
  local copies, waits for them, and re-layouts  3.51 us (1%)
    pallas_call x1, Pallas kernels, backward(): pl.pallas_call(functools.partial(backward_kernel, heads, streams, n_ffn,...  286 us
    pallas_call x1, Pallas kernels, front(): pl.pallas_call(functools.partial(front_kernel, heads), out_shape=[outs[na...  25 us
    pallas_call x1, Pallas kernels, unpack(): pl.pallas_call(functools.partial(unpack_kernel, heads, n_small), grid=(-(...  18.2 us

profile of v7, /device:TPU:0, one launch (start us, length us, event | category | flops | bytes accessed | tf_op | source)
XLA Modules:
  0.0 335.8 jit_solution(2008962282830957829)
XLA Ops:
  1.3 1.4 fusion.6.refs_7_
  2.7 25.0 %front.1 = (bf16[1024,896]{1,0:T(8,128)(2,1)}, bf16[1024,896]{1,0:T(8,128)(2,1)}, bf16[1024,896]{1,0:T(8,128)(2,1)}, bf16[4096,128]{1,0:T(8,128)(2,1)}, bf16[102...) custom-call(s32[1,1]{1,0:T(1,128)S(6)} %copy.30.length_ref, bf16[512,896]{1,0:T(8,128)(2,1)} %refs_10_.1, ...), custom_call_target="tpu_custom_call" | custom-call | tf_op jit(solution)/shard_map/front/pallas_call | solution.py:348
  27.7 286.4 %backward.1 = (bf16[22,896,384]{2,1,0:T(8,128)(2,1)}, bf16[512,896]{1,0:T(8,128)(2,1)}, bf16[512,896]{1,0:T(8,128)(2,1)}, bf16[20,896,384]{2,1,0:T(8,128)(2,1)}) custom-call(f32[1024,896]{1,0:T(8,128)} %get-tuple-element.36.refs_0_, bf16[1024,896]{1,0:T(8,128)(2,1)} %get-tuple-element.37.refs_1_, f32[7,128]{1,0:T(8,128)} %bitcast.25, f32[7,128]{1,0:T(8,128)} %bitcast.26, ...), custom_call_target="tpu_custom_call" | custom-call | tf_op jit(solution)/shard_map/backward/pallas_call | solution.py:1157
  314.2 0.0 copy-start
  314.2 1.2 copy-done
  315.3 0.0 copy-start.1
  315.3 1.2 copy-done.1
  316.5 18.2 %unpack.1 = (f32[2432,896]{1,0:T(8,128)}, f32[896,2432]{1,0:T(8,128)}, f32[896,2432]{1,0:T(8,128)}, f32[448,896]{1,0:T(8,128)}, f32[448,896]{1,0:T(8,128)}, /*in...) custom-call(bf16[22,896,384]{2,1,0:T(8,128)(2,1)} %get-tuple-element, ...), custom_call_target="tpu_custom_call" | custom-call | tf_op jit(solution)/shard_map/unpack/pallas_call | solution.py:1226
  334.7 0.6 fusion.7
  335.3 0.6 slice.9
Async XLA Ops:
  314.2 1.2 copy-start
  315.3 1.2 copy-start.1
